TPU v7x, 128 devices: a whole 4x4x4 slice. The times are simulated.
128 devices in a mesh: owner: 16 (over x_lo, z, core), col: 8 (over x_hi, y).
Axes of the slice: x: 4 (x_hi: 2, x_lo: 2; x = x_hi * 2 + x_lo), y: 4, z: 4, core: 2. Of those that a mesh axis runs over, the one named last changes fastest.
Arguments:
- token_ids: int32 [12288, 16], P('owner'), may hold values from 0 to 30719, as said below
- doc_lengths: int32 [12288], P(('owner', 'col')), may hold values from 1 to 16
- clusters: int32 [12288, 1], P(('owner', 'col')), may hold values from 0 to 63; in each aligned block of 96 rows (0 to 95, 96 to 191, ...) at most 3 rows name the same one
- embed_table: bfloat16 [30720, 1024], P('col'), may hold values from -6 to 6
- positions: bfloat16 [16, 1024], replicated, may hold values from -3 to 3
- w_in: bfloat16 [4096, 1024], P(('owner', 'col')), may hold values from -0.1875 to 0.1875
- w_out: bfloat16 [4096, 1024], P(('owner', 'col')), may hold values from -0.09375 to 0.09375
Outputs:
- best_match: float32 [12288], P(('owner', 'col'))
Inputs may be any that keep to these rules, and one draw needn't show every extreme that they name: `token_ids`: the table is cut into 8 shards of 30720 / 8 consecutive rows; within the tokens of one device (aligned blocks of 96 documents) at most 384 ids lie in one shard, and exactly 384 in some shard of every block. `clusters`: within the rows of one device (aligned blocks of 96 rows) no cluster is named by more than 3 rows, a bound that some block reaches.
All inputs are finite; a program needn't handle non-finite values.
Results may differ from a plain program's by a relative error of at most 0.00035.
Values may be sent and summed in bfloat16 or wider, within the bound.
No kernel may reach another device: no remote copies, remote signals or barrier semaphores. Data moves between devices by JAX's collectives and lax.ppermute only.
A program may use at most 128 MiB of HBM per device.

v0:
```python
import jax
import jax.numpy as jnp
from jax import lax
from jax.sharding import PartitionSpec as P

CL_OWN = 4


def shifted(value, axis, steps):
    count = lax.axis_size(axis)
    pairs = [(source, (source + steps) % count) for source in range(count)]
    return lax.ppermute(value, axis, pairs)


def layer_norm(values):
    mean = jnp.mean(values, axis=-1, keepdims=True)
    centred = values - mean
    var = jnp.mean(centred * centred, axis=-1, keepdims=True)
    return centred * lax.rsqrt(var + 1e-05)


def local(token_ids, doc_lengths, clusters, embed_table, positions, w_in, w_out):
    doc_dev = doc_lengths.shape[0]
    seq = token_ids.shape[1]
    width = embed_table.shape[1]
    tok_dev = doc_dev * seq
    n_own = lax.axis_size("owner")
    n_col = lax.axis_size("col")
    cap = 2 * doc_dev // (CL_OWN * n_own)
    vocab_rows = embed_table.shape[0]
    group_ids = token_ids.reshape(-1)
    first_row = lax.axis_index("col") * vocab_rows
    local_ids = group_ids - first_row
    inside = (local_ids >= 0) & (local_ids < vocab_rows)
    picked = jnp.take(embed_table, jnp.clip(local_ids, 0, vocab_rows - 1), axis=0)
    looked = lax.psum_scatter(
        jnp.where(inside[:, None], picked.astype(jnp.float32), 0.0).astype(jnp.bfloat16),
        "col",
        scatter_dimension=0,
        tiled=True,
    ).astype(jnp.float32)
    embedded = looked.reshape(doc_dev, seq, width) + positions.astype(jnp.float32)[None]
    normed = layer_norm(embedded).reshape(tok_dev, width)
    normed_half = normed.astype(jnp.bfloat16)
    pre = lax.dot_general(
        normed_half,
        lax.all_gather(w_in, ("owner", "col"), axis=0, tiled=True),
        (((1,), (1,)), ((), ())),
        preferred_element_type=jnp.float32,
    )
    hidden = jax.nn.gelu(pre, approximate=False).astype(jnp.bfloat16)
    branch = jnp.dot(
        hidden,
        lax.all_gather(w_out, ("owner", "col"), axis=0, tiled=True),
        preferred_element_type=jnp.float32,
    )
    states = (normed + branch).reshape(doc_dev, seq, width)
    valid = (jnp.arange(seq, dtype=jnp.int32)[None, :] < doc_lengths[:, None]).astype(jnp.float32)
    pooled = jnp.sum(states * valid[:, :, None], axis=1) / doc_lengths.astype(jnp.float32)[:, None]
    scale = lax.rsqrt(jnp.sum(pooled * pooled, axis=-1, keepdims=True) + 1e-06)
    embedding = (pooled * scale).astype(jnp.bfloat16)
    labels = clusters[:, 0]
    same = labels[:, None] == labels[None, :]
    order = jnp.arange(doc_dev, dtype=jnp.int32)
    earlier = order[:, None] > order[None, :]
    slot_rank = jnp.sum((same & earlier).astype(jnp.int32), axis=1)
    owner_of = labels // CL_OWN
    within = labels % CL_OWN
    position = within * (n_own * cap) + owner_of * cap + slot_rank
    outgoing = jnp.zeros((CL_OWN * n_own * cap, width), jnp.bfloat16).at[position].set(embedding)
    outgoing = outgoing.reshape(CL_OWN, n_own * cap, width)
    members = lax.all_to_all(outgoing, "owner", split_axis=1, concat_axis=1, tiled=True)
    member_count = n_own * cap
    diagonal = jnp.eye(member_count, dtype=jnp.bool_)[None]

    def compare(best, block, own):
        scores = jnp.einsum("kmd,knd->kmn", members, block, preferred_element_type=jnp.float32)
        filled = jnp.sum(jnp.square(block.astype(jnp.float32)), axis=-1) > 0.5
        keep = filled[:, None, :]
        if own:
            keep = keep & jnp.logical_not(diagonal)
        return jnp.maximum(best, jnp.max(jnp.where(keep, scores, -1.0), axis=-1))

    best = compare(jnp.full((CL_OWN, member_count), -1.0, jnp.float32), members, True)

    def advance(step, carry):
        block, running = carry
        block = shifted(block, "col", 1)
        return (block, compare(running, block, False))

    moving, best = lax.fori_loop(0, n_col - 1, advance, (members, best))
    returned = lax.all_to_all(best, "owner", split_axis=1, concat_axis=1, tiled=True)
    return jnp.take(returned.reshape(-1), position, axis=0)


def solution(mesh):
    return jax.shard_map(
        local,
        mesh=mesh,
        in_specs=(
            P("owner", None),
            P(("owner", "col")),
            P(("owner", "col"), None),
            P("col", None),
            P(),
            P(("owner", "col"), None),
            P(("owner", "col"), None),
        ),
        out_specs=P(("owner", "col")),
        check_vma=False,
    )
```

profile of v0, /device:TPU:0, one launch (start us, length us, event | category | flops | bytes accessed | tf_op | source)
XLA Modules:
  0.0 1050.2 jit_solution(16844908667546689978)
XLA Ops:
  7.4 0.8 subtract_clamp_fusion
  8.7 0.8 compare_and_fusion.1
  10.1 64.7 %gather_fusion = bf16[12288,1024]{1,0:T(8,128)(2,1)} fusion(bf16[3840,1024]{1,0:T(8,128)(2,1)} %param.12, s32[12288]{0:T(1024)S(1)} %broadcast_clamp_fusion), kind=kCustom, calls=%fused_computation | custom fusion | bytes 50380800 | tf_op jit(solution)/shard_map/jit(_take)/gather | solution.py:35
  74.8 22.7 %select_convert_fusion = bf16[12288,1024]{1,0:T(8,128)(2,1)} fusion(bf16[12288,1024]{1,0:T(8,128)(2,1)} %gather_fusion, pred[12288]{0:T(1024)(128)(4,1)S(1)} %compare_and_fusion, pred[12288]{0:T(1024)(128)(4,1)S(1)} %and.61), kind=kLoop, calls=%fused_computation.6 | loop fusion | flops 50331648 | bytes 50356224 | tf_op jit(solution)/shard_map/convert_element_type | solution.py:37
  98.6 0.6 convert_element_type.48
  100.0 0.7 fusion.44
  100.7 271.3 %reduce-scatter.2.cloned.1.call-done = bf16[1536,1024]{1,0:T(8,128)(2,1)} async-done(((bf16[12288,1024]{1,0:T(8,128)(2,1)}), bf16[1536,1024]{1,0:T(8,128)(2,1)}) %reduce-scatter.2.cloned.1.call-update) | async-done | bytes 3145744 | tf_op jit(solution)/shard_map/reduce_scatter | solution.py:36
  372.0 2.6 fusion.35
  374.6 3.0 multiply_reduce_fusion.2
  378.2 4.5 fusion.38
  382.7 199.5 %all-gather.3.cloned.1.call-done = bf16[4096,1024]{1,0:T(8,128)(2,1)} async-done(((bf16[32,1024]{1,0:T(8,128)(2,1)}), bf16[4096,1024]{1,0:T(8,128)(2,1)}) %all-gather.3.cloned.1.call-update) | async-done | bytes 8388624 | tf_op jit(solution)/shard_map/all_gather | solution.py:47
  582.2 68.9 %fusion.2.clone.6 = bf16[1536,4096]{1,0:T(8,128)(2,1)} fusion(bf16[1536,1024]{1,0:T(8,128)(2,1)} %fusion.38, bf16[4096,1024]{1,0:T(8,128)(2,1)} %all-gather.3.cloned.1.call-done), kind=kOutput, calls=%fused_computation.10.clone.clone.clone.clone.clone.1 | convolution fusion | flops 13293846528 | bytes 24117248 | tf_op jit(solution)/shard_map/dot_general | solution.py:45
  651.1 247.9 %all-gather.5.cloned.1.call-done = bf16[4096,1024]{1,0:T(8,128)(2,1)} async-done(((bf16[32,1024]{1,0:T(8,128)(2,1)}), bf16[4096,1024]{1,0:T(8,128)(2,1)}) %all-gather.5.cloned.1.call-update) | async-done | bytes 8388624 | tf_op jit(solution)/shard_map/all_gather | solution.py:54
  899.0 18.7 %fusion.37 = f32[1536,1024]{1,0:T(8,128)S(1)} fusion(bf16[1536,1024]{1,0:T(8,128)(2,1)S(1)} %copy-done, bf16[4096,1024]{1,0:T(8,128)(2,1)} %all-gather.5.cloned.1.call-done, f32[1536]{0:T(1024)S(1)} %copy-done.7, f32[1536]{0:T(1024)S(1)} %copy-done.5, f32[16,1024]{1,0:T(8,128)S(1)} %copy-done.2, bf16[1536,4096]{1,0:T(8,128)(2,1)} %fusion.2.clone.6), kind=kOutput, calls=%fused_computation.56 | convolution fusion | flops 12892766208 | bytes 30486528 | tf_op jit(solution)/shard_map/dot_general | solution.py:52
  917.8 1.3 multiply_reduce_fusion.1
  919.4 1.2 scatter_custom_fusion
  920.6 1.0 copy.55
  921.6 5.9 all-to-all-start
  927.5 9.4 all-to-all-done
  937.8 88.7 %while.12 = (s32[]{:T(128)}, bf16[4,48,1024]{2,1,0:T(8,128)(2,1)S(1)}, f32[4,48]{1,0:T(4,128)S(1)}, bf16[4,48,1024]{2,1,0:T(8,128)(2,1)S(1)}, s32[]{:T(128)}) while((s32[]{:T(128)}, bf16[4,48,1024]{2,1,0:T(8,128)(2,1)S(1)}, f32[4,48]{1,0:T(4,128)S(1)}, bf16[4,48,1024]{2,1,0:T(8,128)(2,1)S(1)}, s32[]{:T(128)}) %tuple.23), condition=%wide.region_12.13_spmd, body=%wide.region_9.12_spmd.sunk | while | flops 19482624 | bytes 3544037 | solution.py:91
  937.8 2.1 collective-permute-start
  939.9 12.0 %collective-permute-done = bf16[4,48,1024]{2,1,0:T(8,128)(2,1)S(1)} collective-permute-done((bf16[4,48,1024]{2,1,0:T(8,128)(2,1)S(1)}, bf16[4,48,1024]{2,1,0:T(8,128)(2,1)S(1)}, u32[]{:S(2)}, u32[]{:S(2)}) %collective-permute-start) | collective-permute-done | bytes 393248 | tf_op jit(solution)/shard_map/while/body/eval_jaxpr/ppermute | solution.py:12
  952.4 13.0 %collective-permute-done = bf16[4,48,1024]{2,1,0:T(8,128)(2,1)S(1)} collective-permute-done((bf16[4,48,1024]{2,1,0:T(8,128)(2,1)S(1)}, bf16[4,48,1024]{2,1,0:T(8,128)(2,1)S(1)}, u32[]{:S(2)}, u32[]{:S(2)}) %collective-permute-start) | collective-permute-done | bytes 393248 | tf_op jit(solution)/shard_map/while/body/eval_jaxpr/ppermute | solution.py:12
  966.0 12.1 %collective-permute-done = bf16[4,48,1024]{2,1,0:T(8,128)(2,1)S(1)} collective-permute-done((bf16[4,48,1024]{2,1,0:T(8,128)(2,1)S(1)}, bf16[4,48,1024]{2,1,0:T(8,128)(2,1)S(1)}, u32[]{:S(2)}, u32[]{:S(2)}) %collective-permute-start) | collective-permute-done | bytes 393248 | tf_op jit(solution)/shard_map/while/body/eval_jaxpr/ppermute | solution.py:12
  978.7 11.4 %collective-permute-done = bf16[4,48,1024]{2,1,0:T(8,128)(2,1)S(1)} collective-permute-done((bf16[4,48,1024]{2,1,0:T(8,128)(2,1)S(1)}, bf16[4,48,1024]{2,1,0:T(8,128)(2,1)S(1)}, u32[]{:S(2)}, u32[]{:S(2)}) %collective-permute-start) | collective-permute-done | bytes 393248 | tf_op jit(solution)/shard_map/while/body/eval_jaxpr/ppermute | solution.py:12
  990.7 11.4 %collective-permute-done = bf16[4,48,1024]{2,1,0:T(8,128)(2,1)S(1)} collective-permute-done((bf16[4,48,1024]{2,1,0:T(8,128)(2,1)S(1)}, bf16[4,48,1024]{2,1,0:T(8,128)(2,1)S(1)}, u32[]{:S(2)}, u32[]{:S(2)}) %collective-permute-start) | collective-permute-done | bytes 393248 | tf_op jit(solution)/shard_map/while/body/eval_jaxpr/ppermute | solution.py:12
  1002.6 11.4 %collective-permute-done = bf16[4,48,1024]{2,1,0:T(8,128)(2,1)S(1)} collective-permute-done((bf16[4,48,1024]{2,1,0:T(8,128)(2,1)S(1)}, bf16[4,48,1024]{2,1,0:T(8,128)(2,1)S(1)}, u32[]{:S(2)}, u32[]{:S(2)}) %collective-permute-start) | collective-permute-done | bytes 393248 | tf_op jit(solution)/shard_map/while/body/eval_jaxpr/ppermute | solution.py:12
  1014.6 11.4 %collective-permute-done = bf16[4,48,1024]{2,1,0:T(8,128)(2,1)S(1)} collective-permute-done((bf16[4,48,1024]{2,1,0:T(8,128)(2,1)S(1)}, bf16[4,48,1024]{2,1,0:T(8,128)(2,1)S(1)}, u32[]{:S(2)}, u32[]{:S(2)}) %collective-permute-start) | collective-permute-done | bytes 393248 | tf_op jit(solution)/shard_map/while/body/eval_jaxpr/ppermute | solution.py:12
  1026.6 0.6 copy.61
  1027.2 7.5 all-to-all-start.1
  1034.7 6.1 all-to-all-done.1
  1041.0 1.3 gather_fusion.1
  (101 shorter events, 9.0 us)
Async XLA Ops:
  7.4 364.6 %reduce-scatter.2.cloned.1.call-start = ((), (), s32[]{:S(2)}) async-start(), calls=%async_computation.3 | async-start | bytes 28311552 | tf_op jit(solution)/shard_map/reduce_scatter | solution.py:36
  97.4 1.2 copy-start.8
  97.4 1.2 copy-start.10
  97.4 1.9 copy-start.12
  97.4 484.8 %all-gather.3.cloned.1.call-start = ((), (), s32[]{:S(2)}) async-start(), calls=%async_computation.4 | async-start | bytes 8454144 | tf_op jit(solution)/shard_map/all_gather | solution.py:47
  98.0 801.0 %all-gather.5.cloned.1.call-start = ((), (), s32[]{:S(2)}) async-start(), calls=%async_computation.5 | async-start | bytes 8454144 | tf_op jit(solution)/shard_map/all_gather | solution.py:54
  98.6 284.1 %copy-start.1 = (f32[16,1024]{1,0:T(8,128)}, f32[16,1024]{1,0:T(8,128)S(1)}, u32[]{:S(2)}) copy-start(f32[16,1024]{1,0:T(8,128)S(1)} %convert_element_type.44) | copy-start | bytes 196612
  374.5 3.1 copy-start.4
  377.6 0.6 copy-start.6
  582.2 316.8 %copy-start = (bf16[1536,1024]{1,0:T(8,128)(2,1)S(1)}, bf16[1536,1024]{1,0:T(8,128)(2,1)}, u32[]{:S(2)}) copy-start(bf16[1536,1024]{1,0:T(8,128)(2,1)} %reduce-scatter.2.cloned.1.call-done) | copy-start | bytes 9437188
  582.2 316.8 %copy-start.2 = (f32[16,1024]{1,0:T(8,128)S(1)}, f32[16,1024]{1,0:T(8,128)}, u32[]{:S(2)}) copy-start(f32[16,1024]{1,0:T(8,128)} %copy-done.1) | copy-start | bytes 196612
  582.2 316.8 %copy-start.5 = (f32[1536]{0:T(1024)S(1)}, f32[1536]{0:T(1024)}, u32[]{:S(2)}) copy-start(f32[1536]{0:T(1024)} %copy-done.4) | copy-start | bytes 18436
  582.2 316.8 %copy-start.7 = (f32[1536]{0:T(1024)S(1)}, f32[1536]{0:T(1024)}, u32[]{:S(2)}) copy-start(f32[1536]{0:T(1024)} %copy-done.6) | copy-start | bytes 18436
  651.1 266.7 %copy-start.3 = (f32[96,16]{1,0:T(8,128)S(1)}, f32[96,16]{1,0:T(8,128)}, u32[]{:S(2)}) copy-start(f32[96,16]{1,0:T(8,128)} %fusion.44) | copy-start | bytes 18436
  651.1 268.0 %copy-start.9 = (f32[96]{0:T(128)S(1)}, f32[96]{0:T(128)}, u32[]{:S(2)}) copy-start(f32[96]{0:T(128)} %convert_element_type.48) | copy-start | bytes 1156
  651.1 268.3 %copy-start.11 = (s32[96,1]{0,1:T(1,128)S(1)}, s32[96,1]{0,1:T(1,128)}, u32[]{:S(2)}) copy-start(s32[96,1]{0,1:T(1,128)} %compare_select_fusion.2) | copy-start | bytes 1156
  921.6 15.3 %all-to-all-start = ((bf16[4,48,1024]{2,0,1:T(4,128)(2,1)}), bf16[4,48,1024]{2,0,1:T(4,128)(2,1)S(1)}, u32[]{:S(2)}, u32[]{:S(2)}) async-start(bf16[4,48,1024]{2,0,1:T(4,128)(2,1)} %copy.55), calls=%async_computation.1 | async-start | bytes 786432 | tf_op jit(solution)/shard_map/all_to_all | solution.py:72
  937.8 14.0 %collective-permute-start = (bf16[4,48,1024]{2,1,0:T(8,128)(2,1)S(1)}, bf16[4,48,1024]{2,1,0:T(8,128)(2,1)S(1)}, u32[]{:S(2)}, u32[]{:S(2)}) collective-permute-start(bf16[4,48,1024]{2,1,0:T(8,128)(2,1)S(1)} %get-tuple-element.87), channel_id=1, source_target_pairs={{0,1},{1,2},{2,3},{3,4},{4,5},{5,6},{6,7},{7,0},{8,9},{9,10},{10,1... | collective-permute-start | bytes 1179656 | tf_op jit(solution)/shard_map/while/body/eval_jaxpr/ppermute | solution.py:12
  952.3 13.1 %collective-permute-start = (bf16[4,48,1024]{2,1,0:T(8,128)(2,1)S(1)}, bf16[4,48,1024]{2,1,0:T(8,128)(2,1)S(1)}, u32[]{:S(2)}, u32[]{:S(2)}) collective-permute-start(bf16[4,48,1024]{2,1,0:T(8,128)(2,1)S(1)} %get-tuple-element.87), channel_id=1, source_target_pairs={{0,1},{1,2},{2,3},{3,4},{4,5},{5,6},{6,7},{7,0},{8,9},{9,10},{10,1... | collective-permute-start | bytes 1179656 | tf_op jit(solution)/shard_map/while/body/eval_jaxpr/ppermute | solution.py:12
  965.9 12.2 %collective-permute-start = (bf16[4,48,1024]{2,1,0:T(8,128)(2,1)S(1)}, bf16[4,48,1024]{2,1,0:T(8,128)(2,1)S(1)}, u32[]{:S(2)}, u32[]{:S(2)}) collective-permute-start(bf16[4,48,1024]{2,1,0:T(8,128)(2,1)S(1)} %get-tuple-element.87), channel_id=1, source_target_pairs={{0,1},{1,2},{2,3},{3,4},{4,5},{5,6},{6,7},{7,0},{8,9},{9,10},{10,1... | collective-permute-start | bytes 1179656 | tf_op jit(solution)/shard_map/while/body/eval_jaxpr/ppermute | solution.py:12
  978.6 11.5 %collective-permute-start = (bf16[4,48,1024]{2,1,0:T(8,128)(2,1)S(1)}, bf16[4,48,1024]{2,1,0:T(8,128)(2,1)S(1)}, u32[]{:S(2)}, u32[]{:S(2)}) collective-permute-start(bf16[4,48,1024]{2,1,0:T(8,128)(2,1)S(1)} %get-tuple-element.87), channel_id=1, source_target_pairs={{0,1},{1,2},{2,3},{3,4},{4,5},{5,6},{6,7},{7,0},{8,9},{9,10},{10,1... | collective-permute-start | bytes 1179656 | tf_op jit(solution)/shard_map/while/body/eval_jaxpr/ppermute | solution.py:12
  990.6 11.5 %collective-permute-start = (bf16[4,48,1024]{2,1,0:T(8,128)(2,1)S(1)}, bf16[4,48,1024]{2,1,0:T(8,128)(2,1)S(1)}, u32[]{:S(2)}, u32[]{:S(2)}) collective-permute-start(bf16[4,48,1024]{2,1,0:T(8,128)(2,1)S(1)} %get-tuple-element.87), channel_id=1, source_target_pairs={{0,1},{1,2},{2,3},{3,4},{4,5},{5,6},{6,7},{7,0},{8,9},{9,10},{10,1... | collective-permute-start | bytes 1179656 | tf_op jit(solution)/shard_map/while/body/eval_jaxpr/ppermute | solution.py:12
  1002.6 11.5 %collective-permute-start = (bf16[4,48,1024]{2,1,0:T(8,128)(2,1)S(1)}, bf16[4,48,1024]{2,1,0:T(8,128)(2,1)S(1)}, u32[]{:S(2)}, u32[]{:S(2)}) collective-permute-start(bf16[4,48,1024]{2,1,0:T(8,128)(2,1)S(1)} %get-tuple-element.87), channel_id=1, source_target_pairs={{0,1},{1,2},{2,3},{3,4},{4,5},{5,6},{6,7},{7,0},{8,9},{9,10},{10,1... | collective-permute-start | bytes 1179656 | tf_op jit(solution)/shard_map/while/body/eval_jaxpr/ppermute | solution.py:12
  1014.5 11.5 %collective-permute-start = (bf16[4,48,1024]{2,1,0:T(8,128)(2,1)S(1)}, bf16[4,48,1024]{2,1,0:T(8,128)(2,1)S(1)}, u32[]{:S(2)}, u32[]{:S(2)}) collective-permute-start(bf16[4,48,1024]{2,1,0:T(8,128)(2,1)S(1)} %get-tuple-element.87), channel_id=1, source_target_pairs={{0,1},{1,2},{2,3},{3,4},{4,5},{5,6},{6,7},{7,0},{8,9},{9,10},{10,1... | collective-permute-start | bytes 1179656 | tf_op jit(solution)/shard_map/while/body/eval_jaxpr/ppermute | solution.py:12
  1027.2 13.6 %all-to-all-start.1 = ((f32[4,16,3]{2,0,1:T(4,128)}), f32[4,16,3]{2,0,1:T(4,128)S(1)}, u32[]{:S(2)}, u32[]{:S(2)}) async-start(f32[4,16,3]{2,0,1:T(4,128)} %copy.61), calls=%async_computation.2 | async-start | bytes 65536 | tf_op jit(solution)/shard_map/all_to_all | solution.py:92
Sparse Core Ops, SparseCore 0:
  97.6 274.3 reduce-scatter.1
Sparse Core Ops, SparseCore 1:
  99.6 482.6 all-gather.2
  583.8 315.2 all-gather.4
where the time goes:
time: 1050 us
  waiting for transfers between devices  818 us (78%)
  matrix products  89.8 us (9%)
  local copies, waits for them, and re-layouts  69.8 us (7%)
  other arithmetic  41.3 us (4%)
  starting transfers between devices  16 us (2%)
  between operations  15.1 us (1%)
    reduce_scatter x1, waiting for transfers between devices, local(): lax.psum_scatter(jnp.where(inside[:, None], picked.astype(jnp.float32), 0...  271 us
    all_gather x1, waiting for transfers between devices, local(): lax.all_gather(w_out, ('owner', 'col'), axis=0, tiled=True)  248 us
    all_gather x1, waiting for transfers between devices, local(): lax.all_gather(w_in, ('owner', 'col'), axis=0, tiled=True)  200 us
    ppermute x7, waiting for transfers between devices, shifted(): return lax.ppermute(value, axis, pairs)  82.7 us
    dot_general x1, matrix products, local(): lax.dot_general(normed_half, lax.all_gather(w_in, ('owner', 'col'), axis=...  68.9 us
    gather x1, local copies, waits for them, and re-layouts, local(): jnp.take(embed_table, jnp.clip(local_ids, 0, vocab_rows - 1), axis=0)  64.7 us
    convert_element_type x1, other arithmetic, local(): jnp.where(inside[:, None], picked.astype(jnp.float32), 0.0)  22.7 us
  transfers between devices with their start and end apart: 12, of which 12 were waited for; matrix products, arithmetic and copies ran while one was open for 8% of the time, Pallas kernels for 0%

commit v1 on v0

v1 whole, which is shorter than its diff:
```python
import jax
import jax.numpy as jnp
from jax import lax
from jax.experimental import pallas as pl
from jax.experimental.pallas import tpu as pltpu
from jax.sharding import Mesh
from jax.sharding import PartitionSpec as P

OWN = ("x_lo", "z", "core")
COL = ("x_hi", "y")
X = ("x_lo", "x_hi")
CHIPS = ("x_lo", "z", "x_hi", "y")
SHARD_CAP = 384
TILE_BITS = 8
TILE = 1 << TILE_BITS
LANES = 128
SUB = 64
NONE = 1 << 30
LIMIT = 5.4 * 5.4
ERF_Q = (
    0.7978853416207131,
    0.03633264203955081,
    -3.271896418592583e-05,
    -5.512179284196367e-05,
    3.917683168513537e-06,
    -1.2794852180568973e-07,
    1.6281616374933989e-09,
)


def step(value, axis, by):
    count = 2 if axis == "core" else 4
    place = (lambda x: (x % 2) * 2 + x // 2) if axis == X else (lambda x: x)
    return lax.ppermute(value, axis, [(place(i), place((i + by) % count)) for i in range(count)])


def ring(value, axis):
    return [value] + [step(value, axis, by) for by in (1, -1, 2)]


def half_gelu(half):
    square = jnp.minimum(half * half, LIMIT / 4)
    total = jnp.full_like(square, ERF_Q[-1] * 4.0 ** (len(ERF_Q) - 1) * 2)
    for power in range(len(ERF_Q) - 2, -1, -1):
        total = total * square + ERF_Q[power] * 4.0**power * 2
    return half * jnp.tanh(half * total) + half


def members_of(docs, tile):
    lane = lax.broadcasted_iota(jnp.int32, docs.shape, 1)
    return (docs == lane + tile * LANES).astype(jnp.bfloat16)


def pool(docs, values, starts, first, tiles, total):
    high = values.astype(jnp.bfloat16)
    low = (values - high.astype(jnp.float32)).astype(jnp.bfloat16)
    for tile in range(tiles):

        @pl.when((starts[tile] < first + TILE) & (starts[tile + 1] > first))
        def _():
            mask = members_of(docs[...], tile)
            rows = pl.ds(tile * LANES, LANES)
            over = (((0,), (0,)), ((), ()))
            total[rows, :] += lax.dot_general(
                mask, high, over, preferred_element_type=jnp.float32
            ) + lax.dot_general(mask, low, over, preferred_element_type=jnp.float32)


def tiles_of(starts, parts):
    return jnp.maximum((starts[parts] + TILE - 1) >> TILE_BITS, 1)


def prepare(keys, counts, starts, table, positions, x_out, docs_out, total, rows32, table32, staged, listed, sems):
    width = table.shape[1]
    pieces = width // LANES
    chunk = staged.shape[1]
    chunks = table.shape[0] // chunk

    def load():
        def fetch(number, slot):
            return pltpu.make_async_copy(
                table.at[pl.ds(number * chunk, chunk), :], staged.at[slot], sems.at[slot]
            )

        fetch(0, 0).start()

        def gather_list(block, offset):
            base = block * SHARD_CAP

            def eight(group, carry):
                for one in range(8):
                    listed[offset + group * 8 + one] = keys[base + group * 8 + one]
                return carry

            lax.fori_loop(0, (counts[block] + 7) >> 3, eight, 0)
            return offset + counts[block]

        end = lax.fori_loop(0, 16, gather_list, 0)

        def tail(one, carry):
            listed[end + one] = NONE
            return carry

        lax.fori_loop(0, TILE, tail, 0)
        total[...] = jnp.zeros_like(total)
        for number in range(chunks):
            slot = number % 2
            if number + 1 < chunks:
                fetch(number + 1, 1 - slot).start()
            fetch(number, slot).wait()

            def widen(group, carry, number=number, slot=slot):
                values = staged[slot, pl.ds(pl.multiple_of(group * 16, 16), 16), :].astype(jnp.float32)
                base = number * chunk * pieces + group * 16 * pieces
                for eight in range(2):
                    for piece in range(pieces):
                        place = pl.multiple_of(base + eight * 8 * pieces + piece * 8, 8)
                        table32[pl.ds(place, 8), :] = values[
                            eight * 8 : eight * 8 + 8, piece * LANES : (piece + 1) * LANES
                        ]
                return carry

            lax.fori_loop(0, chunk // 16, widen, 0)

    load()
    parts = total.shape[0] // LANES

    def tile(x_ref, docs_ref):
        first = pl.program_id(0) * TILE

        def take(group, carry):
            for one in range(8):
                key = listed[first + group * 8 + one]
                place = key & 0x7FFF
                when = pl.multiple_of((key >> 12) & 0x78, 8)
                value = table32[pl.ds(place, pieces, stride=8), :] + positions[pl.ds(when, pieces), :]
                rows32[pl.ds(group * 8 * pieces + one, pieces, stride=8), :] = value
                docs_ref[pl.ds(group * 8 + one, 1), :] = jnp.full((1, LANES), key >> 19, jnp.int32)
            return carry

        lax.fori_loop(0, TILE // 8, take, 0)
        normed = []
        for sub in range(TILE // SUB):
            block = rows32[pl.ds(sub * SUB * pieces, SUB * pieces), :].reshape(SUB // 8, pieces, 8, LANES)
            values = jnp.concatenate([block[:, piece].reshape(SUB, LANES) for piece in range(pieces)], axis=1)
            mean = jnp.mean(values, axis=-1, keepdims=True)
            centred = values - mean
            var = jnp.mean(centred * centred, axis=-1, keepdims=True)
            normal = centred * lax.rsqrt(var + 1e-05)
            x_ref[pl.ds(sub * SUB, SUB), :] = (normal * 0.5).astype(jnp.bfloat16)
            normed.append(normal)
        pool(docs_ref, jnp.concatenate(normed, axis=0), starts, first, parts, total)

    pltpu.emit_pipeline(
        tile,
        grid=(tiles_of(starts, 2 * parts),),
        in_specs=[],
        out_specs=[
            pl.BlockSpec((TILE, width), lambda i: (i, 0)),
            pl.BlockSpec((TILE, LANES), lambda i: (i, 0)),
        ],
    )(x_out, docs_out)


def forward(starts, x_all, docs_all, *refs):
    weights, total = refs[:-1], refs[-1]
    width = x_all.shape[1]
    parts = total.shape[0] // LANES
    total[...] = jnp.zeros_like(total)

    def tile(x_ref, docs_ref):
        x = x_ref[...]
        branch = jnp.zeros(x.shape, jnp.float32)
        for ref in weights:
            rows = ref.shape[0]
            both = ref[...].reshape(rows // 32, 32, width)
            w_in = both[:, :16].reshape(rows // 2, width)
            w_out = both[:, 16:].reshape(rows // 2, width)
            pre = lax.dot_general(x, w_in, (((1,), (1,)), ((), ())), preferred_element_type=jnp.float32)
            hidden = half_gelu(pre).astype(jnp.bfloat16)
            branch = branch + jnp.dot(hidden, w_out, preferred_element_type=jnp.float32)
        pool(docs_ref, branch, starts, pl.program_id(0) * TILE, parts, total)

    pltpu.emit_pipeline(
        tile,
        grid=(tiles_of(starts, parts),),
        in_specs=[
            pl.BlockSpec((TILE, width), lambda i: (i, 0)),
            pl.BlockSpec((TILE, LANES), lambda i: (i, 0)),
        ],
        out_specs=[],
    )(x_all, docs_all)


def local(token_ids, doc_lengths, clusters, embed_table, positions, w_in, w_out):
    doc_dev = doc_lengths.shape[0]
    group, seq = token_ids.shape
    vocab_rows, width = embed_table.shape
    n_col = group // doc_dev
    most = 2 * n_col * SHARD_CAP
    smem, vmem, hbm = (pl.BlockSpec(memory_space=space) for space in (pltpu.SMEM, pltpu.VMEM, pl.ANY))

    units = w_in.shape[0]
    with jax.named_scope("weights"):
        mixed = jnp.concatenate([w_in[:16], w_out[:16], w_in[16:], w_out[16:]], axis=0)
        by_z = lax.all_gather(mixed, "z", axis=0, tiled=False)
        first_half, second_half = by_z[:, :units].reshape(-1, width), by_z[:, units:].reshape(-1, width)
        first_half = jnp.concatenate(ring(first_half, X), axis=0)
        second_half = jnp.concatenate(ring(second_half, "y"), axis=0)
        weights = ring(first_half, "y") + ring(second_half, X)

    with jax.named_scope("keys"):
        lengths = lax.all_gather(doc_lengths, COL, axis=0, tiled=True)
        row = token_ids - lax.axis_index(COL) * vocab_rows
        time = lax.broadcasted_iota(jnp.int32, (group, seq), 1)
        doc = lax.broadcasted_iota(jnp.int32, (group, seq), 0)
        keep = (row >= 0) & (row < vocab_rows) & (time < lengths[:, None])
        place = (row >> 3) * 64 + (row & 7)
        key = jnp.where(keep, (doc << 19) + (time << 15) + place, NONE)
        key = lax.sort(key.reshape(n_col, doc_dev * seq), dimension=1)[:, :SHARD_CAP]
        kept = jnp.sum(keep.astype(jnp.int32), axis=1)
        counts = jnp.sum(kept.reshape(n_col, doc_dev), axis=1)
        parts = jnp.sum(kept.reshape(group // LANES, LANES), axis=1)
        tally = jnp.concatenate([counts, parts, jnp.zeros((SHARD_CAP - n_col - group // LANES,), jnp.int32)])
        mine = jnp.concatenate([key, tally[None]], axis=0)
        other = step(mine, "core", 1)
        other_key = other[:n_col] + jnp.where(other[:n_col] < NONE, group << 19, 0)
        keys = jnp.concatenate([key, other_key], axis=0).reshape(-1)
        counts = jnp.concatenate([counts, other[n_col, :n_col]])
        parts = jnp.concatenate([parts, other[n_col, n_col : n_col + group // LANES]])
        starts = jnp.concatenate([jnp.zeros((1,), jnp.int32), jnp.cumsum(parts)])

    with jax.named_scope("prepare"):
        pieces = width // LANES
        x, docs, normed = pl.pallas_call(
            prepare,
            in_specs=[smem, smem, smem, hbm, vmem],
            out_specs=[hbm, hbm, vmem],
            out_shape=[
                jax.ShapeDtypeStruct((most, width), jnp.bfloat16),
                jax.ShapeDtypeStruct((most, LANES), jnp.int32),
                jax.ShapeDtypeStruct((group, width), jnp.float32),
            ],
            scratch_shapes=[
                pltpu.VMEM((TILE * pieces, LANES), jnp.float32),
                pltpu.VMEM((vocab_rows * pieces, LANES), jnp.float32),
                pltpu.VMEM((2, vocab_rows // 8, width), jnp.bfloat16),
                pltpu.SMEM((most + TILE + 8,), jnp.int32),
                pltpu.SemaphoreType.DMA((2,)),
            ],
            compiler_params=pltpu.CompilerParams(vmem_limit_bytes=44 << 20),
            cost_estimate=pl.CostEstimate(flops=4 << 30, bytes_accessed=32 << 20, transcendentals=0),
        )(keys, counts, starts, embed_table, positions.astype(jnp.float32).reshape(seq * pieces, LANES))

    with jax.named_scope("forward"):
        branch = pl.pallas_call(
            forward,
            in_specs=[smem, hbm, hbm] + [vmem] * len(weights),
            out_specs=vmem,
            out_shape=jax.ShapeDtypeStruct((2 * group, width), jnp.float32),
            compiler_params=pltpu.CompilerParams(vmem_limit_bytes=48 << 20),
            cost_estimate=pl.CostEstimate(flops=16 << 30, bytes_accessed=24 << 20, transcendentals=0),
        )(starts, x, docs, *weights)

    with jax.named_scope("pooled"):
        sums = branch[:group] + normed + step(branch[group:], "core", 1)
        sums = sums.astype(jnp.bfloat16).reshape(n_col, doc_dev, width)
        sums = lax.all_to_all(sums, COL, 0, 0, tiled=True)
        pooled = jnp.sum(sums.astype(jnp.float32), axis=0) / doc_lengths.astype(jnp.float32)[:, None]
        scale = lax.rsqrt(jnp.sum(pooled * pooled, axis=-1, keepdims=True) + 1e-06)
        embedding = (pooled * scale).astype(jnp.bfloat16)

    with jax.named_scope("match"):
        n_clusters = lax.axis_size(CHIPS)
        labels = clusters[:, 0]
        same = labels[:, None] == labels[None, :]
        order = jnp.arange(doc_dev, dtype=jnp.int32)
        rank = jnp.sum((same & (order[:, None] > order[None, :])).astype(jnp.int32), axis=1)
        slot = labels * 4 + rank
        chosen = slot[None, :] == jnp.arange(n_clusters * 4, dtype=jnp.int32)[:, None]
        sizes = jnp.sum((labels[None, :] == jnp.arange(n_clusters)[:, None]).astype(jnp.int32), axis=1)
        fourth = lax.broadcasted_iota(jnp.int32, (n_clusters, 4, width), 1) == 3
        flags = lax.broadcasted_iota(jnp.int32, (n_clusters, 4, width), 2) < sizes[:, None, None]
        outgoing = jnp.dot(chosen.astype(jnp.bfloat16), embedding, preferred_element_type=jnp.float32)
        outgoing = jnp.where(
            fourth, flags.astype(jnp.float32), outgoing.reshape(n_clusters, 4, width)
        ).astype(jnp.bfloat16)
        members = lax.all_to_all(outgoing, CHIPS, 0, 0, tiled=True)
        others = step(members, "core", 1)
        every = jnp.concatenate([members, others], axis=0)
        filled = jnp.pad(every[:, 3, :3], ((0, 0), (0, 1))).reshape(-1) > 0.5
        count = n_clusters * 4
        scores = jnp.dot(
            members.reshape(count, width), every.reshape(2 * count, width).T, preferred_element_type=jnp.float32
        )
        own = jnp.arange(count)[:, None] == jnp.arange(2 * count)[None, :]
        best = jnp.max(jnp.where(filled[None, :] & jnp.logical_not(own), scores, -1.0), axis=1)
        best = jnp.maximum(best, -1.0)
        returned = lax.all_to_all(best.reshape(n_clusters, 4), CHIPS, 0, 0, tiled=True).reshape(-1)
        return jnp.sum(jnp.where(chosen, returned[:, None], 0.0), axis=0)


def solution(mesh):
    fine = Mesh(mesh.devices.reshape(2, 4, 2, 2, 4), ("x_lo", "z", "core", "x_hi", "y"))
    everywhere = OWN + COL
    return jax.shard_map(
        local,
        mesh=fine,
        in_specs=(
            P(OWN, None),
            P(everywhere),
            P(everywhere, None),
            P(COL, None),
            P(),
            P(everywhere, None),
            P(everywhere, None),
        ),
        out_specs=P(everywhere),
        check_vma=False,
    )
```

time: 1050 us -> 259 us (0.25)
  waiting for transfers between devices: 818 us -> 61.8 us
  matrix products: 89.8 us -> 0.97 us
  blocking collectives: 0 us -> 64.8 us
  Pallas kernels: 0 us -> 63 us
  local copies, waits for them, and re-layouts: 69.8 us -> 15.6 us
  other arithmetic: 41.3 us -> 5.64 us
  starting transfers between devices: 16 us -> 30.3 us
    all_gather x2 -> x0, waiting for transfers between devices: 447 us -> none  [the longest x1 248 us: local(): lax.all_gather(w_out, ('owner', 'col'), axis=0, tiled=True)]
    reduce_scatter x1 -> x0, waiting for transfers between devices: 271 us -> none  [local(): lax.psum_scatter(jnp.where(inside[:, None], picked.astype(jnp.float32), 0...]
    dot_general x10 -> x2, matrix products: 89.8 us -> 0.97 us  [the longest x1 0.56 us: local(): jnp.dot(members.reshape(count, width), every.reshape(2 * count, width).T,...]
    gather x2 -> x0, local copies, waits for them, and re-layouts: 66 us -> none  [the longest x1 64.7 us: local(): jnp.take(embed_table, jnp.clip(local_ids, 0, vocab_rows - 1), axis=0)]
    pallas_call x0 -> x2, Pallas kernels: none -> 63 us  [the longest x1 39.7 us: local(): pl.pallas_call(forward, in_specs=[smem, hbm, hbm] + [vmem] * len(weights)...]
    ppermute x7 -> x15, waiting for transfers between devices: 82.7 us -> 41 us  [step(): lax.ppermute(value, axis, [(place(i), place((i + by) % count)) for i in r...]
    all_to_all x0 -> x2, blocking collectives: none -> 34.6 us  [the longest x1 20 us: local(): members = lax.all_to_all(outgoing, CHIPS, 0, 0, tiled=True)]
    convert_element_type x4 -> x2, other arithmetic: 27.8 us -> 2.45 us  [the longest x1 2.02 us: local(): sums = sums.astype(jnp.bfloat16).reshape(n_col, doc_dev, width)]
  transfers between devices with their start and end apart: 12 -> 16, of which waited for: 12 -> 5; matrix products, arithmetic and copies ran while one was open for 8% -> 2% of each run, Pallas kernels for 0% -> 9%
where the time goes in v1:
time: 259 us; the launch traced here: 256 us
  blocking collectives  64.8 us (25%)
  Pallas kernels  63 us (24%)
  waiting for transfers between devices  61.8 us (24%)
  starting transfers between devices  30.3 us (12%)
  local copies, waits for them, and re-layouts  15.6 us (6%)
  between operations  14.4 us (6%)
  other arithmetic  5.64 us (2%)
    ppermute x15, waiting for transfers between devices, step(): lax.ppermute(value, axis, [(place(i), place((i + by) % count)) for i in r...  41 us
    pallas_call x1, Pallas kernels, local(): pl.pallas_call(forward, in_specs=[smem, hbm, hbm] + [vmem] * len(weights)...  39.7 us
    pallas_call x1, Pallas kernels, local(): pl.pallas_call(prepare, in_specs=[smem, smem, smem, hbm, vmem], out_specs...  23.2 us
    all_to_all x1, waiting for transfers between devices, local(): sums = lax.all_to_all(sums, COL, 0, 0, tiled=True)  20.8 us
    all_to_all x1, blocking collectives, local(): members = lax.all_to_all(outgoing, CHIPS, 0, 0, tiled=True)  20 us
    unnamed x1, blocking collectives  16.2 us
    all_to_all x1, starting transfers between devices, local(): sums = lax.all_to_all(sums, COL, 0, 0, tiled=True)  16.1 us
    all_to_all x1, blocking collectives, local(): lax.all_to_all(best.reshape(n_clusters, 4), CHIPS, 0, 0, tiled=True)  14.6 us
  transfers between devices with their start and end apart: 16, of which 5 were waited for; matrix products, arithmetic and copies ran while one was open for 2% of the time, Pallas kernels for 9%

profile of v1, /device:TPU:0, one launch (start us, length us, event | category | flops | bytes accessed | tf_op | source)
XLA Modules:
  0.0 256.4 jit_solution(8543562581190071342)
XLA Ops:
  6.5 0.8 fusion.11
  7.4 14.1 %all-gather = bf16[256,1024]{1,0:T(8,128)(2,1)S(1)} all-gather(bf16[64,1024]{1,0:T(8,128)(2,1)S(1)} %pad_maximum_fusion.2), channel_id=2, replica_groups=mesh['x_lo'=2,'z'=4,'core'=2,'x_hi'=2,'y'=4] {'z'}, dimensions={0}, use_global_device_ids=true | all-gather | bytes 655360 | tf_op jit(solution)/shard_map/weights/all_gather | solution.py:206
  21.5 1.6 collective-permute-start.7
  23.2 1.7 collective-permute-start.8
  24.8 2.0 collective-permute-start.9
  26.8 0.6 dynamic-slice
  28.3 16.2 %all-reduce.1 = s32[768]{0:T(1024)S(1)} all-reduce(s32[768]{0:T(1024)S(1)} %dynamic-update-slice), channel_id=1, replica_groups=mesh['x_lo'=2,'z'=4,'core'=2,'x_hi'=2,'y'=4] {'x_hi','y'}, use_global_device_ids=true, to_apply=%add.1 | all-reduce | flops 768 | bytes 6144
  44.6 0.6 collective-permute-start.10
  45.4 0.8 reshape.107
  46.6 5.9 %sort.9.cloned.1.call-done = s32[8,1536]{1,0:T(8,128)} async-done(((s32[8,1536]{1,0:T(8,128)}), s32[8,1536]{1,0:T(8,128)}) %sort.9.cloned.1.call-update) | async-done | bytes 49168 | tf_op jit(solution)/shard_map/keys/sort | solution.py:220
  52.6 0.7 slice.53
  53.4 3.2 %collective-permute-start.2 = (bf16[128,1024]{1,0:T(8,128)(2,1)S(1)}, bf16[128,1024]{1,0:T(8,128)(2,1)S(1)}, u32[]{:S(2)}, u32[]{:S(2)}) collective-permute-start(bf16[128,1024]{1,0:T(8,128)(2,1)S(1)} %bitcast.22), channel_id=1, source_target_pairs={{0,68},{64,0},{4,64},{68,4},{1,69},{65,1},{5,65},{69,5},{2,70},{66... | collective-permute-start | bytes 786440 | tf_op jit(solution)/shard_map/weights/ppermute | solution.py:34
  56.6 1.0 collective-permute-start.3
  57.7 0.6 collective-permute-start.11
  58.3 30.9 %collective-permute-done.1 = bf16[128,1024]{1,0:T(8,128)(2,1)S(1)} collective-permute-done((bf16[128,1024]{1,0:T(8,128)(2,1)S(1)}, bf16[128,1024]{1,0:T(8,128)(2,1)S(1)}, u32[]{:S(2)}, u32[]{:S(2)}) %collective-permute-start.1) | collective-permute-done | bytes 262176 | tf_op jit(solution)/shard_map/weights/ppermute | solution.py:34
  89.3 3.2 %collective-permute-start.5 = (bf16[512,1024]{1,0:T(8,128)(2,1)S(1)}, bf16[512,1024]{1,0:T(8,128)(2,1)}, u32[]{:S(2)}, u32[]{:S(2)}) collective-permute-start(bf16[512,1024]{1,0:T(8,128)(2,1)S(1)} %pad_maximum_fusion.refs_0_), channel_id=1, source_target_pairs={{0,3},{1,0},{2,1},{3,2},{4,7},{5,4},{6,5},{7,6},{8,11},{9,8},{10,9... | collective-permute-start | bytes 3145736 | tf_op jit(solution)/shard_map/weights/ppermute | solution.py:34
  93.0 23.2 %prepare.1 = (bf16[6144,1024]{1,0:T(8,128)(2,1)}, s32[6144,128]{1,0:T(8,128)S(1)}, f32[768,1024]{1,0:T(8,128)S(1)}) custom-call(s32[6144]{0:T(1024)S(1)} %reshape.111.keys, s32[16]{0:T(128)S(1)} %pad_add_fusion.4.counts, s32[13]{0:T(128)S(1)} %pad_add_fusion.3.starts, bf16[3840,1024]{1,0:T(8,128)(2,1)} %table.1, f32[128,128]{1,0:T(8,128)S(1)} %reshape.121.positions), custom_call_target="tpu_custom_call" | custom-call | flops 4294967296 | bytes 33554432 | tf_op jit(solution)/shard_map/prepare/pallas_call | solution.py:235
  116.3 1.7 copy-done
  118.0 2.9 %collective-permute-done.4.refs_1_ = bf16[512,1024]{1,0:T(8,128)(2,1)S(1)} collective-permute-done((bf16[512,1024]{1,0:T(8,128)(2,1)S(1)}, bf16[512,1024]{1,0:T(8,128)(2,1)S(1)}, u32[]{:S(2)}, u32[]{:S(2)}) %collective-permute-start.4) | collective-permute-done | bytes 1048608 | tf_op jit(solution)/shard_map/weights/ppermute | solution.py:34
  120.9 39.7 %forward.1 = f32[1536,1024]{1,0:T(8,128)} custom-call(s32[13]{0:T(128)S(1)} %pad_add_fusion.3.starts, bf16[6144,1024]{1,0:T(8,128)(2,1)} %get-tuple-element.8.x_all, s32[6144,128]{1,0:T(8,128)} %copy-done, bf16[512,1024]{1,0:T(8,128)(2,1)S(1)} %pad_maximum_fusion.refs_0_, bf16[512,1024]{1,0:T(8,128)(2,1)S(1)} %collective-permute-done.4.refs_1_, ...), custom_call_target="tpu_custom_call" | custom-call | flops 17179869184 | bytes 25165824 | tf_op jit(solution)/shard_map/forward/pallas_call | solution.py:256
  160.6 2.3 slice.60
  162.9 5.6 %collective-permute-done.13 = f32[768,1024]{1,0:T(8,128)S(1)} collective-permute-done((f32[768,1024]{1,0:T(8,128)S(1)}, f32[768,1024]{1,0:T(8,128)S(1)}, u32[]{:S(2)}, u32[]{:S(2)}) %collective-permute-start.13) | collective-permute-done | bytes 3145760 | tf_op jit(solution)/shard_map/pooled/ppermute | solution.py:34
  168.6 2.0 fusion.1
  170.6 16.1 %all-to-all-start = ((bf16[8,96,1024]{2,1,0:T(8,128)(2,1)}), bf16[8,96,1024]{2,1,0:T(8,128)(2,1)S(1)}, u32[]{:S(2)}, u32[]{:S(2)}) async-start(bf16[8,96,1024]{2,1,0:T(8,128)(2,1)} %bitcast.10), calls=%async_computation | async-start | bytes 3145728 | tf_op jit(solution)/shard_map/pooled/all_to_all | solution.py:268
  187.1 20.8 %all-to-all-done = bf16[8,96,1024]{2,1,0:T(8,128)(2,1)S(1)} async-done(((bf16[8,96,1024]{2,1,0:T(8,128)(2,1)}), bf16[8,96,1024]{2,1,0:T(8,128)(2,1)S(1)}, u32[]{:S(2)}, u32[]{:S(2)}) %all-to-all-start) | async-done | bytes 1572896 | tf_op jit(solution)/shard_map/pooled/all_to_all | solution.py:268
  209.4 20.0 %all_to_all.16 = bf16[64,4,1024]{2,1,0:T(4,128)(2,1)S(1)} all-to-all(bf16[64,4,1024]{2,1,0:T(4,128)(2,1)S(1)} %select_convert_fusion), channel_id=1, replica_groups=mesh['x_lo'=2,'z'=4,'core'=2,'x_hi'=2,'y'=4] {'x_lo','z','x_hi','y'}, dimensions={0} | all-to-all | bytes 1048576 | tf_op jit(solution)/shard_map/match/all_to_all | solution.py:288
  229.7 1.6 collective-permute-done.14
  232.3 0.6 fusion.2
  233.0 14.6 %all_to_all.17 = f32[64,1,4]{2,1,0:T(1,128)S(1)} all-to-all(f32[64,1,4]{2,1,0:T(1,128)S(1)} %bitcast.29), channel_id=1, replica_groups=mesh['x_lo'=2,'z'=4,'core'=2,'x_hi'=2,'y'=4] {'x_lo','z','x_hi','y'}, dimensions={0} | all-to-all | bytes 2048 | tf_op jit(solution)/shard_map/match/all_to_all | solution.py:299
  247.5 0.5 broadcast.40
  248.0 0.7 reduce.3
  248.9 0.7 select_reduce_fusion
  (83 shorter events, 5.2 us)
Async XLA Ops:
  6.5 20.3 %copy-start.6 = (u32[128]{0:T(128)S(1)}, u32[128]{0:T(128)}, u32[]{:S(2)}) copy-start(u32[128]{0:T(128)} %constant.61) | copy-start | bytes 1540
  6.5 21.5 %copy-start.4 = (s32[96]{0:T(128)S(1)}, s32[96]{0:T(128)}, u32[]{:S(2)}) copy-start(s32[96]{0:T(128)} %param.8) | copy-start | bytes 1156
  6.5 46.0 %sort.9.cloned.1.call-start = ((), (), s32[]{:S(2)}) async-start(), calls=%async_computation.3 | async-start | bytes 147488 | tf_op jit(solution)/shard_map/keys/sort | solution.py:220
  7.4 37.8 %copy-start.2 = (s32[768,16]{0,1:T(8,128)S(1)}, s32[768,16]{0,1:T(8,128)}, u32[]{:S(2)}) copy-start(s32[768,16]{0,1:T(8,128)} %param.7) | copy-start | bytes 147460
  21.5 36.1 %copy-start.3 = (bf16[16,1024]{1,0:T(8,128)(2,1)S(1)}, bf16[16,1024]{1,0:T(8,128)(2,1)}, u32[]{:S(2)}) copy-start(bf16[16,1024]{1,0:T(8,128)(2,1)} %param.11) | copy-start | bytes 98308
  21.5 23.0 %collective-permute-start.7 = (bf16[128,1024]{1,0:T(8,128)(2,1)S(1)}, bf16[128,1024]{1,0:T(8,128)(2,1)S(1)}, u32[]{:S(2)}, u32[]{:S(2)}) collective-permute-start(bf16[128,1024]{1,0:T(8,128)(2,1)S(1)} %bitcast.25), channel_id=1, source_target_pairs={{0,1},{1,2},{2,3},{3,0},{4,5},{5,6},{6,7},{7,4},{8,9},{9,10},{10,1... | collective-permute-start | bytes 786440 | tf_op jit(solution)/shard_map/weights/ppermute | solution.py:34
  23.2 21.3 %collective-permute-start.8 = (bf16[128,1024]{1,0:T(8,128)(2,1)S(1)}, bf16[128,1024]{1,0:T(8,128)(2,1)S(1)}, u32[]{:S(2)}, u32[]{:S(2)}) collective-permute-start(bf16[128,1024]{1,0:T(8,128)(2,1)S(1)} %bitcast.26), channel_id=1, source_target_pairs={{0,3},{1,0},{2,1},{3,2},{4,7},{5,4},{6,5},{7,6},{8,11},{9,8},{10,9... | collective-permute-start | bytes 786440 | tf_op jit(solution)/shard_map/weights/ppermute | solution.py:34
  24.8 19.7 %collective-permute-start.9 = (bf16[128,1024]{1,0:T(8,128)(2,1)S(1)}, bf16[128,1024]{1,0:T(8,128)(2,1)S(1)}, u32[]{:S(2)}, u32[]{:S(2)}) collective-permute-start(bf16[128,1024]{1,0:T(8,128)(2,1)S(1)} %bitcast.27), channel_id=1, source_target_pairs={{0,2},{1,3},{2,0},{3,1},{4,6},{5,7},{6,4},{7,5},{8,10},{9,11},{10,... | collective-permute-start | bytes 786440 | tf_op jit(solution)/shard_map/weights/ppermute | solution.py:34
  44.6 48.0 %collective-permute-start.10 = (bf16[512,1024]{1,0:T(8,128)(2,1)S(1)}, bf16[512,1024]{1,0:T(8,128)(2,1)}, u32[]{:S(2)}, u32[]{:S(2)}) collective-permute-start(bf16[512,1024]{1,0:T(8,128)(2,1)S(1)} %pad_maximum_fusion.1.refs_4_), channel_id=1, source_target_pairs={{0,64},{64,4},{4,68},{68,0},{1,65},{65,5},{5,69},{69,1},{2,66},{66... | collective-permute-start | bytes 3145736 | tf_op jit(solution)/shard_map/weights/ppermute | solution.py:34
  53.3 4.3 %collective-permute-start = (s32[9,384]{1,0:T(8,128)S(1)}, s32[9,384]{1,0:T(8,128)S(1)}, u32[]{:S(2)}, u32[]{:S(2)}) collective-permute-start(s32[9,384]{1,0:T(8,128)S(1)} %pad_add_fusion), channel_id=1, source_target_pairs={{0,8},{8,0},{1,9},{9,1},{2,10},{10,2},{3,11},{11,3},{4,12},{12,4},... | collective-permute-start | bytes 41480 | tf_op jit(solution)/shard_map/keys/ppermute | solution.py:34
  53.3 35.9 %collective-permute-start.1 = (bf16[128,1024]{1,0:T(8,128)(2,1)S(1)}, bf16[128,1024]{1,0:T(8,128)(2,1)S(1)}, u32[]{:S(2)}, u32[]{:S(2)}) collective-permute-start(bf16[128,1024]{1,0:T(8,128)(2,1)S(1)} %bitcast.21), channel_id=1, source_target_pairs={{0,64},{64,4},{4,68},{68,0},{1,65},{65,5},{5,69},{69,1},{2,66},{66... | collective-permute-start | bytes 786440 | tf_op jit(solution)/shard_map/weights/ppermute | solution.py:34
  53.4 35.8 %collective-permute-start.2 = (bf16[128,1024]{1,0:T(8,128)(2,1)S(1)}, bf16[128,1024]{1,0:T(8,128)(2,1)S(1)}, u32[]{:S(2)}, u32[]{:S(2)}) collective-permute-start(bf16[128,1024]{1,0:T(8,128)(2,1)S(1)} %bitcast.22), channel_id=1, source_target_pairs={{0,68},{64,0},{4,64},{68,4},{1,69},{65,1},{5,65},{69,5},{2,70},{66... | collective-permute-start | bytes 786440 | tf_op jit(solution)/shard_map/weights/ppermute | solution.py:34
  56.6 32.6 %collective-permute-start.3 = (bf16[128,1024]{1,0:T(8,128)(2,1)S(1)}, bf16[128,1024]{1,0:T(8,128)(2,1)S(1)}, u32[]{:S(2)}, u32[]{:S(2)}) collective-permute-start(bf16[128,1024]{1,0:T(8,128)(2,1)S(1)} %bitcast.23), channel_id=1, source_target_pairs={{0,4},{64,68},{4,0},{68,64},{1,5},{65,69},{5,1},{69,65},{2,6},{66,... | collective-permute-start | bytes 786440 | tf_op jit(solution)/shard_map/weights/ppermute | solution.py:34
  57.7 60.3 %collective-permute-start.11 = (bf16[512,1024]{1,0:T(8,128)(2,1)S(1)}, bf16[512,1024]{1,0:T(8,128)(2,1)}, u32[]{:S(2)}, u32[]{:S(2)}) collective-permute-start(bf16[512,1024]{1,0:T(8,128)(2,1)S(1)} %pad_maximum_fusion.1.refs_4_), channel_id=1, source_target_pairs={{0,68},{64,0},{4,64},{68,4},{1,69},{65,1},{5,65},{69,5},{2,70},{66... | collective-permute-start | bytes 3145736 | tf_op jit(solution)/shard_map/weights/ppermute | solution.py:34
  89.2 28.8 %collective-permute-start.12 = (bf16[512,1024]{1,0:T(8,128)(2,1)S(1)}, bf16[512,1024]{1,0:T(8,128)(2,1)}, u32[]{:S(2)}, u32[]{:S(2)}) collective-permute-start(bf16[512,1024]{1,0:T(8,128)(2,1)S(1)} %pad_maximum_fusion.1.refs_4_), channel_id=1, source_target_pairs={{0,4},{64,68},{4,0},{68,64},{1,5},{65,69},{5,1},{69,65},{2,6},{66,... | collective-permute-start | bytes 3145736 | tf_op jit(solution)/shard_map/weights/ppermute | solution.py:34
  89.3 31.6 %collective-permute-start.4 = (bf16[512,1024]{1,0:T(8,128)(2,1)S(1)}, bf16[512,1024]{1,0:T(8,128)(2,1)S(1)}, u32[]{:S(2)}, u32[]{:S(2)}) collective-permute-start(bf16[512,1024]{1,0:T(8,128)(2,1)S(1)} %pad_maximum_fusion.refs_0_), channel_id=1, source_target_pairs={{0,1},{1,2},{2,3},{3,0},{4,5},{5,6},{6,7},{7,4},{8,9},{9,10},{10,1... | collective-permute-start | bytes 3145736 | tf_op jit(solution)/shard_map/weights/ppermute | solution.py:34
  89.3 31.5 %collective-permute-start.5 = (bf16[512,1024]{1,0:T(8,128)(2,1)S(1)}, bf16[512,1024]{1,0:T(8,128)(2,1)}, u32[]{:S(2)}, u32[]{:S(2)}) collective-permute-start(bf16[512,1024]{1,0:T(8,128)(2,1)S(1)} %pad_maximum_fusion.refs_0_), channel_id=1, source_target_pairs={{0,3},{1,0},{2,1},{3,2},{4,7},{5,4},{6,5},{7,6},{8,11},{9,8},{10,9... | collective-permute-start | bytes 3145736 | tf_op jit(solution)/shard_map/weights/ppermute | solution.py:34
  92.6 28.3 %collective-permute-start.6 = (bf16[512,1024]{1,0:T(8,128)(2,1)S(1)}, bf16[512,1024]{1,0:T(8,128)(2,1)}, u32[]{:S(2)}, u32[]{:S(2)}) collective-permute-start(bf16[512,1024]{1,0:T(8,128)(2,1)S(1)} %pad_maximum_fusion.refs_0_), channel_id=1, source_target_pairs={{0,2},{1,3},{2,0},{3,1},{4,6},{5,7},{6,4},{7,5},{8,10},{9,11},{10,... | collective-permute-start | bytes 3145736 | tf_op jit(solution)/shard_map/weights/ppermute | solution.py:34
  116.3 1.7 copy-start
  160.6 8.0 %copy-start.1 = (f32[1536,1024]{1,0:T(8,128)S(1)}, f32[1536,1024]{1,0:T(8,128)}, u32[]{:S(2)}) copy-start(f32[1536,1024]{1,0:T(8,128)} %forward.1) | copy-start | bytes 18874372
  162.9 5.7 %collective-permute-start.13 = (f32[768,1024]{1,0:T(8,128)S(1)}, f32[768,1024]{1,0:T(8,128)S(1)}, u32[]{:S(2)}, u32[]{:S(2)}) collective-permute-start(f32[768,1024]{1,0:T(8,128)S(1)} %slice.60), channel_id=1, source_target_pairs={{0,8},{8,0},{1,9},{9,1},{2,10},{10,2},{3,11},{11,3},{4,12},{12,4},... | collective-permute-start | bytes 9437192 | tf_op jit(solution)/shard_map/pooled/ppermute | solution.py:34
  170.6 16.2 %copy-start.5 = (s32[96,1]{0,1:T(1,128)S(1)}, s32[96,1]{0,1:T(1,128)}, u32[]{:S(2)}) copy-start(s32[96,1]{0,1:T(1,128)} %param.9) | copy-start | bytes 1156
  170.6 37.2 %all-to-all-start = ((bf16[8,96,1024]{2,1,0:T(8,128)(2,1)}), bf16[8,96,1024]{2,1,0:T(8,128)(2,1)S(1)}, u32[]{:S(2)}, u32[]{:S(2)}) async-start(bf16[8,96,1024]{2,1,0:T(8,128)(2,1)} %bitcast.10), calls=%async_computation | async-start | bytes 3145728 | tf_op jit(solution)/shard_map/pooled/all_to_all | solution.py:268
  229.4 1.9 collective-permute-start.14
Sparse Core Ops, SparseCore 0:
  46.4 5.8 sort.11.cloned.1.call-done
  (1 shorter events, 0.0 us)

commit v2 on v1

v2 whole, which is shorter than its diff:
```python
import functools

import jax
import jax.numpy as jnp
from jax import lax
from jax.experimental import pallas as pl
from jax.experimental.pallas import tpu as pltpu
from jax.sharding import Mesh
from jax.sharding import PartitionSpec as P

OWN = ("x_lo", "z", "core")
COL = ("x_hi", "y")
X = ("x_lo", "x_hi")
CHIPS = ("x_lo", "z", "x_hi", "y")
SHARD_CAP = 384
TILE_BITS = 8
TILE = 1 << TILE_BITS
LANES = 128
SUB = 64
SEQ_BITS = 4
NONE = 1 << 30
BOUNDS = 64
CHUNK = 512
WINDOW = 384
LIMIT = 5.4 * 5.4
ERF_Q = (
    0.7978853416207131,
    0.03633264203955081,
    -3.271896418592583e-05,
    -5.512179284196367e-05,
    3.917683168513537e-06,
    -1.2794852180568973e-07,
    1.6281616374933989e-09,
)


def step(value, axis, by):
    count = 2 if axis == "core" else 4
    place = (lambda x: (x % 2) * 2 + x // 2) if axis == X else (lambda x: x)
    return lax.ppermute(value, axis, [(place(i), place((i + by) % count)) for i in range(count)])


def ring(value, axis):
    return [value] + [step(value, axis, by) for by in (1, -1, 2)]


def copied(sources, shapes, moves):
    def kernel(*refs):
        inputs, (*outputs, sems) = refs[: len(sources)], refs[len(sources) :]
        copies = [
            pltpu.make_async_copy(
                inputs[source].at[pl.ds(from_row, rows), :], outputs[result].at[pl.ds(to_row, rows), :], sems.at[number]
            )
            for number, (source, from_row, result, to_row, rows) in enumerate(moves)
        ]
        for copy in copies:
            copy.start()
        for copy in copies:
            copy.wait()

    return pl.pallas_call(
        kernel,
        in_specs=[pl.BlockSpec(memory_space=pl.ANY)] * len(sources),
        out_specs=[pl.BlockSpec(memory_space=pltpu.VMEM)] * len(shapes),
        out_shape=[jax.ShapeDtypeStruct(shape, sources[0].dtype) for shape in shapes],
        scratch_shapes=[pltpu.SemaphoreType.DMA((len(moves),))],
        cost_estimate=pl.CostEstimate(flops=1 << 10, bytes_accessed=1 << 10, transcendentals=0),
    )(*sources)


def joined(rings, starts, rows):
    sources, shapes, moves = [], [], []
    for result, (pieces, start) in enumerate(zip(rings, starts)):
        half = rows // 2
        shapes.append((len(pieces) * rows, pieces[0].shape[1]))
        for number, piece in enumerate(pieces):
            for which in range(2):
                to_row = (which * len(pieces) + number) * half
                moves.append((len(sources) + number, start + which * half, result, to_row, half))
        sources += pieces
    return copied(sources, shapes, moves)


def half_gelu(half):
    square = jnp.minimum(half * half, LIMIT / 4)
    total = jnp.full_like(square, ERF_Q[-1] * 4.0 ** (len(ERF_Q) - 1) * 2)
    for power in range(len(ERF_Q) - 2, -1, -1):
        total = total * square + ERF_Q[power] * 4.0**power * 2
    return half * jnp.tanh(half * total) + half


def pool(docs, both, first, last, total):
    def window(start):
        start = pl.multiple_of(start, 8)
        lane = lax.broadcasted_iota(jnp.int32, docs.shape, 1)
        mask = jnp.concatenate(
            [(docs == lane + (start + part)).astype(jnp.bfloat16) for part in range(0, WINDOW, LANES)], axis=1
        )
        rows = pl.ds(start, WINDOW)
        total[rows, :] += lax.dot_general(
            jnp.concatenate([mask, mask], axis=0),
            both,
            (((0,), (0,)), ((), ())),
            preferred_element_type=jnp.float32,
        )

    window(first)

    @pl.when(last >= first + WINDOW)
    def _():
        lax.fori_loop(
            1, lax.div(last - first, WINDOW) + 1, lambda number, carry: (window(first + number * WINDOW), carry)[1], 0
        )


def split(values):
    high = values.astype(jnp.bfloat16)
    return jnp.concatenate([high, (values - high.astype(jnp.float32)).astype(jnp.bfloat16)], axis=0)


def prepare(keys, counts, table, positions, x_out, docs_out, bounds, total, rows32, table32, listed):
    width = table.shape[1]
    pieces = width // LANES

    def load():
        def gather_list(block, offset):
            base = block * SHARD_CAP

            def eight(group, carry):
                for one in range(8):
                    listed[offset + group * 8 + one] = keys[base + group * 8 + one]
                return carry

            lax.fori_loop(0, (counts[block] + 7) >> 3, eight, 0)
            return offset + counts[block]

        end = lax.fori_loop(0, 16, gather_list, 0)

        def tail(group, carry):
            for one in range(8):
                listed[end + group * 8 + one] = NONE
            return carry

        lax.fori_loop(0, TILE // 8, tail, 0)
        total[...] = jnp.zeros_like(total)

        def widen(group, carry):
            values = table[pl.ds(pl.multiple_of(group * 16, 16), 16), :].astype(jnp.float32)
            for eight in range(2):
                for piece in range(pieces):
                    place = pl.multiple_of((group * 2 + eight) * 8 * pieces + piece * 8, 8)
                    table32[pl.ds(place, 8), :] = values[
                        eight * 8 : eight * 8 + 8, piece * LANES : (piece + 1) * LANES
                    ]
            return carry

        lax.fori_loop(0, table.shape[0] // 16, widen, 0)
        return end

    end = load()
    tiles = jnp.maximum((end + TILE - 1) >> TILE_BITS, 1)
    own = total.shape[0] - WINDOW
    bounds[BOUNDS - 1] = tiles

    def tile(x_ref, docs_ref):
        first = pl.program_id(0) * TILE

        def take(group, carry):
            for one in range(8):
                key = listed[first + group * 8 + one]
                place = key & 0x7FFF
                when = pl.multiple_of((key >> 12) & 0x78, 8)
                value = table32[pl.ds(place, pieces, stride=8), :] + positions[pl.ds(when, pieces), :]
                rows32[pl.ds(group * 8 * pieces + one, pieces, stride=8), :] = value
                docs_ref[pl.ds(group * 8 + one, 1), :] = jnp.full((1, LANES), key >> 19, jnp.int32)
            return carry

        lax.fori_loop(0, TILE // 8, take, 0)
        normed = []
        for sub in range(TILE // SUB):
            block = rows32[pl.ds(sub * SUB * pieces, SUB * pieces), :].reshape(SUB // 8, pieces, 8, LANES)
            values = jnp.concatenate([block[:, piece].reshape(SUB, LANES) for piece in range(pieces)], axis=1)
            mean = jnp.mean(values, axis=-1, keepdims=True)
            centred = values - mean
            var = jnp.mean(centred * centred, axis=-1, keepdims=True)
            normal = centred * lax.rsqrt(var + 1e-05)
            x_ref[pl.ds(sub * SUB, SUB), :] = (normal * 0.5).astype(jnp.bfloat16)
            normed.append(normal)
        low = jnp.minimum((listed[first] >> 22) << 3, 2 * own - 8)
        high = jnp.minimum(listed[jnp.clip(end - 1, first, first + TILE - 1)] >> 19, 2 * own - 1)
        index = pl.program_id(0)
        bounds[2 * index] = low
        bounds[2 * index + 1] = high

        @pl.when(low < own)
        def _():
            pool(docs_ref[...], split(jnp.concatenate(normed, axis=0)), low, jnp.minimum(high, own - 1), total)

    pltpu.emit_pipeline(
        tile,
        grid=(tiles,),
        in_specs=[],
        out_specs=[
            pl.BlockSpec((TILE, width), lambda i: (i, 0)),
            pl.BlockSpec((TILE, LANES), lambda i: (i, 0)),
        ],
    )(x_out, docs_out)


def run_prepare(keys, counts, embed_table, positions, group):
    most = keys.shape[0]
    seq, width = positions.shape
    vocab_rows = embed_table.shape[0]
    pieces = width // LANES
    smem, vmem, hbm = (pl.BlockSpec(memory_space=space) for space in (pltpu.SMEM, pltpu.VMEM, pltpu.HBM))
    return pl.pallas_call(
        prepare,
        in_specs=[smem, smem, vmem, vmem],
        out_specs=[hbm, hbm, smem, vmem],
        out_shape=[
            jax.ShapeDtypeStruct((most, width), jnp.bfloat16),
            jax.ShapeDtypeStruct((most, LANES), jnp.int32),
            jax.ShapeDtypeStruct((BOUNDS,), jnp.int32),
            jax.ShapeDtypeStruct((group + WINDOW, width), jnp.float32),
        ],
        scratch_shapes=[
            pltpu.VMEM((TILE * pieces, LANES), jnp.float32),
            pltpu.VMEM((vocab_rows * pieces, LANES), jnp.float32),
            pltpu.SMEM((most + TILE + 8,), jnp.int32),
        ],
        compiler_params=pltpu.CompilerParams(vmem_limit_bytes=44 << 20),
        cost_estimate=pl.CostEstimate(flops=1 << 30, bytes_accessed=1 << 20, transcendentals=0),
    )(keys, counts, embed_table, positions.astype(jnp.float32).reshape(seq * pieces, LANES))


def over_tiles(tiles, several):
    def pair(number, carry):
        several(number * 2, 2)
        return carry

    lax.fori_loop(0, tiles >> 1, pair, 0)

    @pl.when((tiles & 1) == 1)
    def _():
        several(tiles - 1, 1)


def rows_of(tile, count):
    return pl.ds(pl.multiple_of(tile * TILE, TILE), count * TILE)


def load_pairs(tiles, loads):
    def copies(tile, slot):
        return [
            pltpu.make_async_copy(whole.at[rows_of(tile, 2), :], place.at[slot], sems.at[slot])
            for whole, place, sems in loads
        ]

    for copy in copies(0, 0):
        copy.start()

    def ready(tile):
        slot = (tile >> 1) & 1

        @pl.when(tile + 2 < tiles)
        def _():
            for copy in copies(tile + 2, 1 - slot):
                copy.start()

        for copy in copies(tile, slot):
            copy.wait()
        return slot

    return ready


def activate(inputs, w_in, hidden, first):
    rows = pl.ds(0, inputs.shape[0])
    for number in range(w_in.shape[0] // CHUNK):
        weights = w_in[pl.ds(number * CHUNK, CHUNK), :]
        pre = lax.dot_general(inputs, weights, (((1,), (1,)), ((), ())), preferred_element_type=jnp.float32)
        hidden[rows, pl.ds(first + number * CHUNK, CHUNK)] = half_gelu(pre).astype(jnp.bfloat16)


def first_units(near, bounds, x_all, *refs):
    pieces, (out, x, w_in, hidden, w_sems, x_sems, out_sems) = refs[:near], refs[near:]
    tiles = bounds[BOUNDS - 1]
    units = w_in.shape[0] // near
    copies = [
        pltpu.make_async_copy(piece.at[pl.ds(0, units), :], w_in.at[pl.ds(number * units, units), :], w_sems.at[number])
        for number, piece in enumerate(pieces)
    ]
    for copy in copies:
        copy.start()
    ready = load_pairs(tiles, [(x_all, x, x_sems)])
    for copy in copies:
        copy.wait()

    def store(tile, slot):
        return pltpu.make_async_copy(hidden.at[slot], out.at[rows_of(tile, 2), :], out_sems.at[slot])

    def several(tile, count):
        slot = ready(tile)

        @pl.when(tile >= 4)
        def _():
            store(tile - 4, slot).wait()

        activate(x[slot, pl.ds(0, count * TILE), :], w_in, hidden.at[slot], 0)
        store(tile, slot).start()

    over_tiles(tiles, several)
    last = ((tiles + 1) >> 1) * 2 - 2

    @pl.when(last >= 2)
    def _():
        store(last - 2, 1 - ((last >> 1) & 1)).wait()

    store(last, (last >> 1) & 1).wait()


def second_units(near, far, bounds, x_all, docs_all, normed, hidden_all, *refs):
    pieces, refs = refs[: near + far], refs[near + far :]
    own, other, total, x, docs, w_in, w_out, hidden, w_sems, x_sems, docs_sems, hidden_sems, ends = refs
    tiles = bounds[BOUNDS - 1]
    group = own.shape[0]
    units = pieces[0].shape[0] // 2
    parts = [(piece.at[pl.ds(units, units), :], w_out, number * units) for number, piece in enumerate(pieces)]
    parts += [(piece.at[pl.ds(0, units), :], w_in, number * units) for number, piece in enumerate(pieces[near:])]
    copies = [
        pltpu.make_async_copy(part, whole.at[pl.ds(row, units), :], w_sems.at[number])
        for number, (part, whole, row) in enumerate(parts)
    ]
    copies.append(pltpu.make_async_copy(normed.at[pl.ds(0, group), :], total.at[pl.ds(0, group), :], ends.at[0]))
    for copy in copies:
        copy.start()
    known = hidden.at[:, :, pl.ds(0, near * units)]
    ready = load_pairs(tiles, [(x_all, x, x_sems), (docs_all, docs, docs_sems), (hidden_all, known, hidden_sems)])
    rest = total.shape[0] - group
    total[pl.ds(group, rest), :] = jnp.zeros((rest, total.shape[1]), jnp.float32)
    for copy in copies:
        copy.wait()

    def several(tile, count):
        slot = ready(tile)
        rows = pl.ds(0, count * TILE)
        activate(x[slot, rows, :], w_in, hidden.at[slot], near * units)
        branch = jnp.dot(hidden[slot, rows, :], w_out[...], preferred_element_type=jnp.float32)
        for one in range(count):
            part = slice(one * TILE, (one + 1) * TILE)
            pool(docs[slot, part, :], split(branch[part]), bounds[2 * (tile + one)], bounds[2 * (tile + one) + 1], total)

    over_tiles(tiles, several)
    copies = [
        pltpu.make_async_copy(total.at[pl.ds(0, group), :], own, ends.at[0]),
        pltpu.make_async_copy(total.at[pl.ds(group, group), :], other, ends.at[1]),
    ]
    for copy in copies:
        copy.start()
    for copy in copies:
        copy.wait()


def run_first(near, bounds, x):
    most, width = x.shape
    units = len(near) * near[0].shape[0] // 2
    smem, hbm, anywhere = (pl.BlockSpec(memory_space=space) for space in (pltpu.SMEM, pltpu.HBM, pl.ANY))
    return pl.pallas_call(
        functools.partial(first_units, len(near)),
        in_specs=[smem, hbm] + [anywhere] * len(near),
        out_specs=hbm,
        out_shape=jax.ShapeDtypeStruct((most, units), jnp.bfloat16),
        scratch_shapes=[
            pltpu.VMEM((2, 2 * TILE, width), jnp.bfloat16),
            pltpu.VMEM((units, width), jnp.bfloat16),
            pltpu.VMEM((2, 2 * TILE, units), jnp.bfloat16),
            pltpu.SemaphoreType.DMA((len(near),)),
            pltpu.SemaphoreType.DMA((2,)),
            pltpu.SemaphoreType.DMA((2,)),
        ],
        compiler_params=pltpu.CompilerParams(vmem_limit_bytes=50 << 20),
        cost_estimate=pl.CostEstimate(flops=12 << 30, bytes_accessed=16 << 20, transcendentals=0),
    )(bounds, x, *near)


def run_second(near, far, bounds, x, docs, normed, hidden):
    most, width = x.shape
    group = normed.shape[0] - WINDOW
    units = near[0].shape[0] // 2
    count = len(near) + len(far)
    smem, hbm, anywhere = (pl.BlockSpec(memory_space=space) for space in (pltpu.SMEM, pltpu.HBM, pl.ANY))
    return pl.pallas_call(
        functools.partial(second_units, len(near), len(far)),
        in_specs=[smem, hbm, anywhere, anywhere, hbm] + [anywhere] * count,
        out_specs=[anywhere, anywhere],
        out_shape=[jax.ShapeDtypeStruct((group, width), jnp.float32)] * 2,
        scratch_shapes=[
            pltpu.VMEM((2 * group + WINDOW, width), jnp.float32),
            pltpu.VMEM((2, 2 * TILE, width), jnp.bfloat16),
            pltpu.VMEM((2, 2 * TILE, LANES), jnp.int32),
            pltpu.VMEM((len(far) * units, width), jnp.bfloat16),
            pltpu.VMEM((count * units, width), jnp.bfloat16),
            pltpu.VMEM((2, 2 * TILE, count * units), jnp.bfloat16),
            pltpu.SemaphoreType.DMA((count + len(far),)),
            pltpu.SemaphoreType.DMA((2,)),
            pltpu.SemaphoreType.DMA((2,)),
            pltpu.SemaphoreType.DMA((2,)),
            pltpu.SemaphoreType.DMA((2,)),
        ],
        compiler_params=pltpu.CompilerParams(vmem_limit_bytes=34 << 20),
        cost_estimate=pl.CostEstimate(flops=16 << 30, bytes_accessed=24 << 20, transcendentals=0),
    )(bounds, x, docs, normed, hidden, *near, *far)


def local(token_ids, doc_lengths, clusters, embed_table, positions, w_in, w_out):
    doc_dev = doc_lengths.shape[0]
    group, seq = token_ids.shape
    vocab_rows, width = embed_table.shape
    n_col = group // doc_dev

    with jax.named_scope("weights"):
        half = w_in.shape[0] // 2
        mixed = jnp.concatenate([w_in[:half], w_out[:half], w_in[half:], w_out[half:]], axis=0)
        by_z = ring(mixed, "z")
        ids = token_ids.reshape(n_col, doc_dev * seq)
        ids = jnp.concatenate([ids, step(ids, "core", 1)], axis=0)
        row = ids - lax.axis_index(COL) * vocab_rows
        block = lax.broadcasted_iota(jnp.int32, ids.shape, 0)
        token = lax.broadcasted_iota(jnp.int32, ids.shape, 1)
        keys = ((block * doc_dev + (token >> SEQ_BITS)) << 19) + ((token & (seq - 1)) << 15)
        keys = jnp.where((row >= 0) & (row < vocab_rows), keys + (row >> 3) * 64 + (row & 7), NONE)
        first, second = joined([by_z, by_z], [0, 2 * half], 2 * half)
        first, second, doc_lengths, keys = lax.optimization_barrier((first, second, doc_lengths, keys))
        lengths = lax.all_gather(doc_lengths, ("core",) + COL, axis=0, tiled=False)
        first, second = ring(first, X), ring(second, "y")
        first, second, lengths = lax.optimization_barrier((first, second, lengths))
        rows = first[0].shape[0]
        first, second = joined([first, second], [0, 0], rows)
        units = first.shape[0] // 2
        left, right = step(first, "y", 1), step(first, "y", -1)
        down, up = step(second, X, 1), step(second, X, -1)
        near = [first, left, right, second, down, up]

    with jax.named_scope("keys"):
        blocks, block = 2 * n_col, doc_dev * seq
        lengths = lengths.reshape(2, n_col, doc_dev)
        lengths = jnp.where(lax.axis_index("core") == 0, lengths, lengths[::-1]).reshape(blocks, doc_dev)
        token = jnp.arange(block, dtype=jnp.int32)[None, :]
        of_doc = (jnp.arange(doc_dev, dtype=jnp.int32)[:, None] == token >> SEQ_BITS).astype(jnp.bfloat16)
        used = jnp.dot(lengths.astype(jnp.bfloat16), of_doc, preferred_element_type=jnp.float32)
        keys = jnp.where((token & (seq - 1)).astype(jnp.float32) < used, keys, NONE)
        counts = jnp.sum((keys < NONE).astype(jnp.int32), axis=1)
        keys = lax.sort(keys, dimension=1)[:, :SHARD_CAP].reshape(-1)

    with jax.named_scope("prepare"):
        x, docs, bounds, normed = run_prepare(keys, counts, embed_table, positions, group)

    with jax.named_scope("forward"):
        far = [step(first, "y", 2), step(second, X, 2)]
        hidden = run_first(near, bounds, x)
        own, other = run_second(near, far, bounds, x, docs, normed, hidden)

    with jax.named_scope("pooled"):
        sums = own + step(other, "core", 1)
        sums = sums.astype(jnp.bfloat16).reshape(n_col, doc_dev, width)
        sums = lax.all_to_all(sums, COL, 0, 0, tiled=True)
        pooled = jnp.sum(sums.astype(jnp.float32), axis=0) / doc_lengths.astype(jnp.float32)[:, None]
        scale = lax.rsqrt(jnp.sum(pooled * pooled, axis=-1, keepdims=True) + 1e-06)
        embedding = (pooled * scale).astype(jnp.bfloat16)

    with jax.named_scope("match"):
        n_clusters = lax.axis_size(CHIPS)
        labels = clusters[:, 0]
        same = labels[:, None] == labels[None, :]
        order = jnp.arange(doc_dev, dtype=jnp.int32)
        rank = jnp.sum((same & (order[:, None] > order[None, :])).astype(jnp.int32), axis=1)
        slot = labels * 4 + rank
        chosen = slot[None, :] == jnp.arange(n_clusters * 4, dtype=jnp.int32)[:, None]
        sizes = jnp.sum((labels[None, :] == jnp.arange(n_clusters)[:, None]).astype(jnp.int32), axis=1)
        fourth = lax.broadcasted_iota(jnp.int32, (n_clusters, 4, width), 1) == 3
        flags = lax.broadcasted_iota(jnp.int32, (n_clusters, 4, width), 2) < sizes[:, None, None]
        outgoing = jnp.dot(chosen.astype(jnp.bfloat16), embedding, preferred_element_type=jnp.float32)
        outgoing = jnp.where(
            fourth, flags.astype(jnp.float32), outgoing.reshape(n_clusters, 4, width)
        ).astype(jnp.bfloat16)
        members = lax.all_to_all(outgoing, CHIPS, 0, 0, tiled=True)
        others = step(members, "core", 1)
        every = jnp.concatenate([members, others], axis=0)
        filled = jnp.pad(every[:, 3, :3], ((0, 0), (0, 1))).reshape(-1) > 0.5
        count = n_clusters * 4
        scores = jnp.dot(
            members.reshape(count, width), every.reshape(2 * count, width).T, preferred_element_type=jnp.float32
        )
        own = jnp.arange(count)[:, None] == jnp.arange(2 * count)[None, :]
        best = jnp.max(jnp.where(filled[None, :] & jnp.logical_not(own), scores, -1.0), axis=1)
        best = jnp.maximum(best, -1.0)
        returned = lax.all_to_all(best.reshape(n_clusters, 4), CHIPS, 0, 0, tiled=True).reshape(-1)
        return jnp.sum(jnp.where(chosen, returned[:, None], 0.0), axis=0)


def solution(mesh):
    fine = Mesh(mesh.devices.reshape(2, 4, 2, 2, 4), ("x_lo", "z", "core", "x_hi", "y"))
    everywhere = OWN + COL
    return jax.shard_map(
        local,
        mesh=fine,
        in_specs=(
            P(OWN, None),
            P(everywhere),
            P(everywhere, None),
            P(COL, None),
            P(),
            P(everywhere, None),
            P(everywhere, None),
        ),
        out_specs=P(everywhere),
        check_vma=False,
    )
```

time: 259 us -> 229 us (0.88)
  waiting for transfers between devices: 61.8 us -> 33.6 us
  blocking collectives: 64.8 us -> 50 us
  starting transfers between devices: 30.3 us -> 43.2 us
  local copies, waits for them, and re-layouts: 15.6 us -> 18.6 us
    ppermute x15 -> x18, waiting for transfers between devices: 41 us -> 12.9 us  [step(): lax.ppermute(value, axis, [(place(i), place((i + by) % count)) for i in r...]
    ppermute x15 -> x18, starting transfers between devices: 14.1 us -> 38.6 us  [step(): lax.ppermute(value, axis, [(place(i), place((i + by) % count)) for i in r...]
    all_gather x1 -> x0, blocking collectives: 14.1 us -> none  [local(): by_z = lax.all_gather(mixed, 'z', axis=0, tiled=False)]
    all_to_all x1, starting transfers between devices: 16.1 us -> 4.57 us  [local(): sums = lax.all_to_all(sums, COL, 0, 0, tiled=True)]
    unnamed x19 -> x44, local copies, waits for them, and re-layouts: 2.74 us -> 9.91 us
    unnamed x1, blocking collectives: 16.2 us -> 12.2 us
    all_to_all x1, blocking collectives: 20 us -> 23.3 us  [local(): members = lax.all_to_all(outgoing, CHIPS, 0, 0, tiled=True)]
    pallas_call x2 -> x5, Pallas kernels: 63 us -> 62.6 us  [the longest x1 21.5 us: run_prepare(): pl.pallas_call(prepare, in_specs=[smem, smem, vmem, vmem], out_specs=[hbm...]
  transfers between devices with their start and end apart: 16 -> 19, of which waited for: 5 -> 7; matrix products, arithmetic and copies ran while one was open for 2% -> 3% of each run, Pallas kernels for 9% -> 16%
where the time goes in v2:
time: 229 us
  Pallas kernels  62.6 us (27%)
  blocking collectives  50 us (22%)
  starting transfers between devices  43.2 us (19%)
  waiting for transfers between devices  33.6 us (15%)
  local copies, waits for them, and re-layouts  18.6 us (8%)
  between operations  14.5 us (6%)
  other arithmetic  5.25 us (2%)
    ppermute x18, starting transfers between devices, step(): lax.ppermute(value, axis, [(place(i), place((i + by) % count)) for i in r...  38.6 us
    all_to_all x1, blocking collectives, local(): members = lax.all_to_all(outgoing, CHIPS, 0, 0, tiled=True)  23.3 us
    pallas_call x1, Pallas kernels, run_prepare(): pl.pallas_call(prepare, in_specs=[smem, smem, vmem, vmem], out_specs=[hbm...  21.5 us
    all_to_all x1, waiting for transfers between devices, local(): sums = lax.all_to_all(sums, COL, 0, 0, tiled=True)  20.8 us
    pallas_call x1, Pallas kernels, run_second(): pl.pallas_call(functools.partial(second_units, len(near), len(far)), in_s...  20.2 us
    pallas_call x1, Pallas kernels, run_first(): pl.pallas_call(functools.partial(first_units, len(near)), in_specs=[smem,...  15.9 us
    all_to_all x1, blocking collectives, local(): lax.all_to_all(best.reshape(n_clusters, 4), CHIPS, 0, 0, tiled=True)  14.6 us
    ppermute x18, waiting for transfers between devices, step(): lax.ppermute(value, axis, [(place(i), place((i + by) % count)) for i in r...  12.9 us
  transfers between devices with their start and end apart: 19, of which 7 were waited for; matrix products, arithmetic and copies ran while one was open for 3% of the time, Pallas kernels for 16%

profile of v2, /device:TPU:0, one launch (start us, length us, event | category | flops | bytes accessed | tf_op | source)
XLA Modules:
  0.0 228.9 jit_solution(15273709397564041284)
XLA Ops:
  7.4 2.1 collective-permute-start
  9.5 2.2 collective-permute-start.1
  11.7 1.8 collective-permute-start.2
  16.0 1.2 collective-permute-done.1.refs_2_.refs_6_
  17.3 1.8 collective-permute-done.2.refs_3_.refs_7_
  19.7 1.9 weights.2
  21.7 1.6 collective-permute-start.4
  23.2 1.7 collective-permute-start.5
  25.0 1.8 collective-permute-start.6
  26.8 1.6 collective-permute-start.7
  28.4 1.7 collective-permute-start.8
  30.0 1.4 collective-permute-done.4.refs_1_
  31.4 3.2 %collective-permute-start.9 = (bf16[128,1024]{1,0:T(8,128)(2,1)}, bf16[128,1024]{1,0:T(8,128)(2,1)S(1)}, u32[]{:S(2)}, u32[]{:S(2)}) collective-permute-start(bf16[128,1024]{1,0:T(8,128)(2,1)} %get-tuple-element.43.refs_4_), channel_id=1, source_target_pairs={{0,2},{1,3},{2,0},{3,1},{4,6},{5,7},{6,4},{7,5},{8,10},{9,11},{10,... | collective-permute-start | bytes 786440 | tf_op jit(solution)/shard_map/weights/ppermute | solution.py:40
  34.6 1.2 dynamic-slice
  37.4 12.2 %all-reduce.1 = s32[1536]{0:T(1024)S(1)} all-reduce(s32[1536]{0:T(1024)S(1)} %dynamic-update-slice), channel_id=2, replica_groups=mesh['x_lo'=2,'z'=4,'core'=2,'x_hi'=2,'y'=4] {'core','x_hi','y'}, use_global_device_ids=true, to_apply=%add.1 | all-reduce | flops 1536 | bytes 12288
  51.4 3.1 %weights.3 = (bf16[512,1024]{1,0:T(8,128)(2,1)}, bf16[512,1024]{1,0:T(8,128)(2,1)}) custom-call(bf16[128,1024]{1,0:T(8,128)(2,1)} %get-tuple-element.39.refs_0_, bf16[128,1024]{1,0:T(8,128)(2,1)} %copy-done.10, bf16[128,1024]{1,0:T(8,128)(2,1)} %copy-done.11, bf16[128,1024]{1,0:T(8,128)(2,1)} %copy-done.12, bf16[128,1024]{1,0:T(8,128)(2,1)} %get-tuple-element.43.refs_4_, ...), custom_call_target="tpu_custom_call" | custom-call | flops 1024 | bytes 1024 | tf_op jit(solution)/shard_map/weights/pallas_call | solution.py:61
  55.5 2.3 collective-permute-start.11
  58.1 3.0 %collective-permute-start.13 = (bf16[512,1024]{1,0:T(8,128)(2,1)}, bf16[512,1024]{1,0:T(8,128)(2,1)}, u32[]{:S(2)}, u32[]{:S(2)}) collective-permute-start(bf16[512,1024]{1,0:T(8,128)(2,1)} %get-tuple-element.48.refs_3_), channel_id=1, source_target_pairs={{0,68},{64,0},{4,64},{68,4},{1,69},{65,1},{5,65},{69,5},{2,70},{66... | collective-permute-start | bytes 3145736 | tf_op jit(solution)/shard_map/weights/ppermute | solution.py:40
  62.1 1.5 collective-permute-start.14
  63.6 4.8 %sort.9.cloned.1.call-done = s32[16,1536]{1,0:T(8,128)} async-done(((s32[16,1536]{1,0:T(8,128)}), s32[16,1536]{1,0:T(8,128)}) %sort.9.cloned.1.call-update) | async-done | bytes 98320 | tf_op jit(solution)/shard_map/keys/sort | solution.py:453
  69.2 21.5 %prepare.1 = (bf16[6144,1024]{1,0:T(8,128)(2,1)}, s32[6144,128]{1,0:T(8,128)S(1)}, s32[64]{0:T(128)S(1)}, f32[1152,1024]{1,0:T(8,128)S(1)}) custom-call(s32[6144]{0:T(1024)S(1)} %reshape.86.keys, s32[16]{0:T(128)S(1)} %get-tuple-element.51.counts, bf16[3840,1024]{1,0:T(8,128)(2,1)} %table.1, f32[128,128]{1,0:T(8,128)S(1)} %reshape.94.positions), custom_call_target="tpu_custom_call" | custom-call | flops 1073741824 | bytes 1048576 | tf_op jit(solution)/shard_map/prepare/pallas_call | solution.py:216
  90.7 2.1 copy-done
  92.8 12.8 %collective-permute-start.15 = (bf16[512,1024]{1,0:T(8,128)(2,1)S(1)}, bf16[512,1024]{1,0:T(8,128)(2,1)S(1)}, u32[]{:S(2)}, u32[]{:S(2)}) collective-permute-start(bf16[512,1024]{1,0:T(8,128)(2,1)S(1)} %copy-done.2), channel_id=1, source_target_pairs={{0,4},{64,68},{4,0},{68,64},{1,5},{65,69},{5,1},{69,65},{2,6},{66,... | collective-permute-start | bytes 3145736 | tf_op jit(solution)/shard_map/forward/ppermute | solution.py:40
  106.7 15.9 %forward.2.hidden_all = bf16[6144,1536]{1,0:T(8,128)(2,1)} custom-call(s32[64]{0:T(128)S(1)} %get-tuple-element.35.bounds, bf16[6144,1024]{1,0:T(8,128)(2,1)} %get-tuple-element.36.x_all, bf16[512,1024]{1,0:T(8,128)(2,1)S(1)} %copy-done.1, bf16[512,1024]{1,0:T(8,128)(2,1)S(1)} %collective-permute-done.10.refs_1_, ...), custom_call_target="tpu_custom_call" | custom-call | flops 12884901888 | bytes 16777216 | tf_op jit(solution)/shard_map/forward/pallas_call | solution.py:368
  123.8 20.2 %forward.3 = (f32[768,1024]{1,0:T(8,128)S(1)}, f32[768,1024]{1,0:T(8,128)S(1)}) custom-call(s32[64]{0:T(128)S(1)} %get-tuple-element.35.bounds, bf16[6144,1024]{1,0:T(8,128)(2,1)} %get-tuple-element.36.x_all, s32[6144,128]{1,0:T(8,128)S(1)} %get-tuple-element.37.docs_all, f32[1152,1024]{1,0:T(8,128)} %copy-done, bf16[6144,1536]{1,0:T(8,128)(2,1)} %forward.2.hidden_all, ...), custom_call_target="tpu_custom_call" | custom-call | flops 17179869184 | bytes 25165824 | tf_op jit(solution)/shard_map/forward/pallas_call | solution.py:392
  144.1 5.6 %collective-permute-done.16 = f32[768,1024]{1,0:T(8,128)S(1)} collective-permute-done((f32[768,1024]{1,0:T(8,128)S(1)}, f32[768,1024]{1,0:T(8,128)S(1)}, u32[]{:S(2)}, u32[]{:S(2)}) %collective-permute-start.16) | collective-permute-done | bytes 3145760 | tf_op jit(solution)/shard_map/pooled/ppermute | solution.py:40
  149.7 1.7 add_convert_fusion
  151.4 4.6 %all-to-all-start = ((bf16[8,96,1024]{2,1,0:T(8,128)(2,1)}), bf16[8,96,1024]{2,1,0:T(8,128)(2,1)S(1)}, u32[]{:S(2)}, u32[]{:S(2)}) async-start(bf16[8,96,1024]{2,1,0:T(8,128)(2,1)} %bitcast.4), calls=%async_computation | async-start | bytes 3145728 | tf_op jit(solution)/shard_map/pooled/all_to_all | solution.py:466
  156.3 20.8 %all-to-all-done = bf16[8,96,1024]{2,1,0:T(8,128)(2,1)S(1)} async-done(((bf16[8,96,1024]{2,1,0:T(8,128)(2,1)}), bf16[8,96,1024]{2,1,0:T(8,128)(2,1)S(1)}, u32[]{:S(2)}, u32[]{:S(2)}) %all-to-all-start) | async-done | bytes 1572896 | tf_op jit(solution)/shard_map/pooled/all_to_all | solution.py:466
  178.6 23.3 %all_to_all.16 = bf16[64,4,1024]{2,1,0:T(4,128)(2,1)S(1)} all-to-all(bf16[64,4,1024]{2,1,0:T(4,128)(2,1)S(1)} %select_convert_fusion), channel_id=1, replica_groups=mesh['x_lo'=2,'z'=4,'core'=2,'x_hi'=2,'y'=4] {'x_lo','z','x_hi','y'}, dimensions={0} | all-to-all | bytes 1048576 | tf_op jit(solution)/shard_map/match/all_to_all | solution.py:486
  202.2 1.6 collective-permute-done.17
  205.5 14.6 %all_to_all.17 = f32[64,1,4]{2,1,0:T(1,128)S(1)} all-to-all(f32[64,1,4]{2,1,0:T(1,128)S(1)} %bitcast.12), channel_id=1, replica_groups=mesh['x_lo'=2,'z'=4,'core'=2,'x_hi'=2,'y'=4] {'x_lo','z','x_hi','y'}, dimensions={0} | all-to-all | bytes 2048 | tf_op jit(solution)/shard_map/match/all_to_all | solution.py:497
  (101 shorter events, 17.8 us)
Async XLA Ops:
  6.5 55.5 %copy-start.16 = (bf16[16,1024]{1,0:T(8,128)(2,1)S(1)}, bf16[16,1024]{1,0:T(8,128)(2,1)}, u32[]{:S(2)}) copy-start(bf16[16,1024]{1,0:T(8,128)(2,1)} %param.11) | copy-start | bytes 98308
  6.5 61.9 %sort.9.cloned.1.call-start = ((), (), s32[]{:S(2)}) async-start(), calls=%async_computation.3 | async-start | bytes 294944 | tf_op jit(solution)/shard_map/keys/sort | solution.py:453
  7.4 11.7 %copy-start.6 = (bf16[64,1024]{1,0:T(8,128)(2,1)}, bf16[64,1024]{1,0:T(8,128)(2,1)S(1)}, u32[]{:S(2)}) copy-start(bf16[64,1024]{1,0:T(8,128)(2,1)S(1)} %pad_maximum_fusion.refs_0_.refs_4_) | copy-start | bytes 393220
  7.4 8.6 %collective-permute-start = (bf16[64,1024]{1,0:T(8,128)(2,1)S(1)}, bf16[64,1024]{1,0:T(8,128)(2,1)S(1)}, u32[]{:S(2)}, u32[]{:S(2)}) collective-permute-start(bf16[64,1024]{1,0:T(8,128)(2,1)S(1)} %pad_maximum_fusion.refs_0_.refs_4_), channel_id=1, source_target_pairs={{0,16},{16,32},{32,48},{48,0},{1,17},{17,33},{33,49},{49,1},{2,18}... | collective-permute-start | bytes 393224 | tf_op jit(solution)/shard_map/weights/ppermute | solution.py:40
  9.5 7.8 %collective-permute-start.1 = (bf16[64,1024]{1,0:T(8,128)(2,1)S(1)}, bf16[64,1024]{1,0:T(8,128)(2,1)S(1)}, u32[]{:S(2)}, u32[]{:S(2)}) collective-permute-start(bf16[64,1024]{1,0:T(8,128)(2,1)S(1)} %pad_maximum_fusion.refs_0_.refs_4_), channel_id=1, source_target_pairs={{0,48},{16,0},{32,16},{48,32},{1,49},{17,1},{33,17},{49,33},{2,50}... | collective-permute-start | bytes 393224 | tf_op jit(solution)/shard_map/weights/ppermute | solution.py:40
  11.7 7.4 %collective-permute-start.2 = (bf16[64,1024]{1,0:T(8,128)(2,1)S(1)}, bf16[64,1024]{1,0:T(8,128)(2,1)S(1)}, u32[]{:S(2)}, u32[]{:S(2)}) collective-permute-start(bf16[64,1024]{1,0:T(8,128)(2,1)S(1)} %pad_maximum_fusion.refs_0_.refs_4_), channel_id=1, source_target_pairs={{0,32},{16,48},{32,0},{48,16},{1,33},{17,49},{33,1},{49,17},{2,34}... | collective-permute-start | bytes 393224 | tf_op jit(solution)/shard_map/weights/ppermute | solution.py:40
  14.6 1.3 collective-permute-start.3
  16.0 3.0 %copy-start.7 = (bf16[64,1024]{1,0:T(8,128)(2,1)}, bf16[64,1024]{1,0:T(8,128)(2,1)S(1)}, u32[]{:S(2)}) copy-start(bf16[64,1024]{1,0:T(8,128)(2,1)S(1)} %collective-permute-done.refs_1_.refs_5_) | copy-start | bytes 393220
  17.3 1.8 copy-start.8
  21.7 9.7 %collective-permute-start.4 = (bf16[128,1024]{1,0:T(8,128)(2,1)}, bf16[128,1024]{1,0:T(8,128)(2,1)S(1)}, u32[]{:S(2)}, u32[]{:S(2)}) collective-permute-start(bf16[128,1024]{1,0:T(8,128)(2,1)} %get-tuple-element.39.refs_0_), channel_id=1, source_target_pairs={{0,64},{64,4},{4,68},{68,0},{1,65},{65,5},{5,69},{69,1},{2,66},{66... | collective-permute-start | bytes 786440 | tf_op jit(solution)/shard_map/weights/ppermute | solution.py:40
  23.2 26.4 %collective-permute-start.5 = (bf16[128,1024]{1,0:T(8,128)(2,1)}, bf16[128,1024]{1,0:T(8,128)(2,1)S(1)}, u32[]{:S(2)}, u32[]{:S(2)}) collective-permute-start(bf16[128,1024]{1,0:T(8,128)(2,1)} %get-tuple-element.39.refs_0_), channel_id=1, source_target_pairs={{0,68},{64,0},{4,64},{68,4},{1,69},{65,1},{5,65},{69,5},{2,70},{66... | collective-permute-start | bytes 786440 | tf_op jit(solution)/shard_map/weights/ppermute | solution.py:40
  25.0 24.7 %collective-permute-start.6 = (bf16[128,1024]{1,0:T(8,128)(2,1)}, bf16[128,1024]{1,0:T(8,128)(2,1)S(1)}, u32[]{:S(2)}, u32[]{:S(2)}) collective-permute-start(bf16[128,1024]{1,0:T(8,128)(2,1)} %get-tuple-element.39.refs_0_), channel_id=1, source_target_pairs={{0,4},{64,68},{4,0},{68,64},{1,5},{65,69},{5,1},{69,65},{2,6},{66,... | collective-permute-start | bytes 786440 | tf_op jit(solution)/shard_map/weights/ppermute | solution.py:40
  26.8 22.9 %collective-permute-start.7 = (bf16[128,1024]{1,0:T(8,128)(2,1)}, bf16[128,1024]{1,0:T(8,128)(2,1)S(1)}, u32[]{:S(2)}, u32[]{:S(2)}) collective-permute-start(bf16[128,1024]{1,0:T(8,128)(2,1)} %get-tuple-element.43.refs_4_), channel_id=1, source_target_pairs={{0,1},{1,2},{2,3},{3,0},{4,5},{5,6},{6,7},{7,4},{8,9},{9,10},{10,1... | collective-permute-start | bytes 786440 | tf_op jit(solution)/shard_map/weights/ppermute | solution.py:40
  28.4 21.3 %collective-permute-start.8 = (bf16[128,1024]{1,0:T(8,128)(2,1)}, bf16[128,1024]{1,0:T(8,128)(2,1)S(1)}, u32[]{:S(2)}, u32[]{:S(2)}) collective-permute-start(bf16[128,1024]{1,0:T(8,128)(2,1)} %get-tuple-element.43.refs_4_), channel_id=1, source_target_pairs={{0,3},{1,0},{2,1},{3,2},{4,7},{5,4},{6,5},{7,6},{8,11},{9,8},{10,9... | collective-permute-start | bytes 786440 | tf_op jit(solution)/shard_map/weights/ppermute | solution.py:40
  31.4 18.3 %copy-start.10 = (bf16[128,1024]{1,0:T(8,128)(2,1)}, bf16[128,1024]{1,0:T(8,128)(2,1)S(1)}, u32[]{:S(2)}) copy-start(bf16[128,1024]{1,0:T(8,128)(2,1)S(1)} %collective-permute-done.4.refs_1_) | copy-start | bytes 786436
  31.4 18.3 %collective-permute-start.9 = (bf16[128,1024]{1,0:T(8,128)(2,1)}, bf16[128,1024]{1,0:T(8,128)(2,1)S(1)}, u32[]{:S(2)}, u32[]{:S(2)}) collective-permute-start(bf16[128,1024]{1,0:T(8,128)(2,1)} %get-tuple-element.43.refs_4_), channel_id=1, source_target_pairs={{0,2},{1,3},{2,0},{3,1},{4,6},{5,7},{6,4},{7,5},{8,10},{9,11},{10,... | collective-permute-start | bytes 786440 | tf_op jit(solution)/shard_map/weights/ppermute | solution.py:40
  54.5 38.3 %collective-permute-start.10 = (bf16[512,1024]{1,0:T(8,128)(2,1)}, bf16[512,1024]{1,0:T(8,128)(2,1)S(1)}, u32[]{:S(2)}, u32[]{:S(2)}) collective-permute-start(bf16[512,1024]{1,0:T(8,128)(2,1)} %get-tuple-element.47.refs_0_), channel_id=1, source_target_pairs={{0,1},{1,2},{2,3},{3,0},{4,5},{5,6},{6,7},{7,4},{8,9},{9,10},{10,1... | collective-permute-start | bytes 3145736 | tf_op jit(solution)/shard_map/weights/ppermute | solution.py:40
  55.5 50.1 %collective-permute-start.11 = (bf16[512,1024]{1,0:T(8,128)(2,1)}, bf16[512,1024]{1,0:T(8,128)(2,1)S(1)}, u32[]{:S(2)}, u32[]{:S(2)}) collective-permute-start(bf16[512,1024]{1,0:T(8,128)(2,1)} %get-tuple-element.47.refs_0_), channel_id=1, source_target_pairs={{0,3},{1,0},{2,1},{3,2},{4,7},{5,4},{6,5},{7,6},{8,11},{9,8},{10,9... | collective-permute-start | bytes 3145736 | tf_op jit(solution)/shard_map/weights/ppermute | solution.py:40
  57.8 47.9 %collective-permute-start.12 = (bf16[512,1024]{1,0:T(8,128)(2,1)}, bf16[512,1024]{1,0:T(8,128)(2,1)S(1)}, u32[]{:S(2)}, u32[]{:S(2)}) collective-permute-start(bf16[512,1024]{1,0:T(8,128)(2,1)} %get-tuple-element.48.refs_3_), channel_id=1, source_target_pairs={{0,64},{64,4},{4,68},{68,0},{1,65},{65,5},{5,69},{69,1},{2,66},{66... | collective-permute-start | bytes 3145736 | tf_op jit(solution)/shard_map/weights/ppermute | solution.py:40
  58.1 47.6 %collective-permute-start.13 = (bf16[512,1024]{1,0:T(8,128)(2,1)}, bf16[512,1024]{1,0:T(8,128)(2,1)}, u32[]{:S(2)}, u32[]{:S(2)}) collective-permute-start(bf16[512,1024]{1,0:T(8,128)(2,1)} %get-tuple-element.48.refs_3_), channel_id=1, source_target_pairs={{0,68},{64,0},{4,64},{68,4},{1,69},{65,1},{5,65},{69,5},{2,70},{66... | collective-permute-start | bytes 3145736 | tf_op jit(solution)/shard_map/weights/ppermute | solution.py:40
  62.1 60.4 %collective-permute-start.14 = (bf16[512,1024]{1,0:T(8,128)(2,1)}, bf16[512,1024]{1,0:T(8,128)(2,1)}, u32[]{:S(2)}, u32[]{:S(2)}) collective-permute-start(bf16[512,1024]{1,0:T(8,128)(2,1)} %get-tuple-element.47.refs_0_), channel_id=1, source_target_pairs={{0,2},{1,3},{2,0},{3,1},{4,6},{5,7},{6,4},{7,5},{8,10},{9,11},{10,... | collective-permute-start | bytes 3145736 | tf_op jit(solution)/shard_map/forward/ppermute | solution.py:40
  69.2 23.7 %copy-start.2 = (bf16[512,1024]{1,0:T(8,128)(2,1)S(1)}, bf16[512,1024]{1,0:T(8,128)(2,1)}, u32[]{:S(2)}) copy-start(bf16[512,1024]{1,0:T(8,128)(2,1)} %get-tuple-element.48.refs_3_) | copy-start | bytes 3145732
  69.2 37.5 %copy-start.1 = (bf16[512,1024]{1,0:T(8,128)(2,1)S(1)}, bf16[512,1024]{1,0:T(8,128)(2,1)}, u32[]{:S(2)}) copy-start(bf16[512,1024]{1,0:T(8,128)(2,1)} %get-tuple-element.47.refs_0_) | copy-start | bytes 3145732
  90.7 2.2 copy-start
  92.8 29.7 %collective-permute-start.15 = (bf16[512,1024]{1,0:T(8,128)(2,1)S(1)}, bf16[512,1024]{1,0:T(8,128)(2,1)S(1)}, u32[]{:S(2)}, u32[]{:S(2)}) collective-permute-start(bf16[512,1024]{1,0:T(8,128)(2,1)S(1)} %copy-done.2), channel_id=1, source_target_pairs={{0,4},{64,68},{4,0},{68,64},{1,5},{65,69},{5,1},{69,65},{2,6},{66,... | collective-permute-start | bytes 3145736 | tf_op jit(solution)/shard_map/forward/ppermute | solution.py:40
  106.7 15.9 %copy-start.3 = (bf16[512,1024]{1,0:T(8,128)(2,1)S(1)}, bf16[512,1024]{1,0:T(8,128)(2,1)}, u32[]{:S(2)}) copy-start(bf16[512,1024]{1,0:T(8,128)(2,1)} %get-tuple-element.48.refs_3_) | copy-start | bytes 3145732
  122.6 1.2 copy-start.5
  144.0 5.7 %collective-permute-start.16 = (f32[768,1024]{1,0:T(8,128)S(1)}, f32[768,1024]{1,0:T(8,128)S(1)}, u32[]{:S(2)}, u32[]{:S(2)}) collective-permute-start(f32[768,1024]{1,0:T(8,128)S(1)} %get-tuple-element.50), channel_id=1, source_target_pairs={{0,8},{8,0},{1,9},{9,1},{2,10},{10,2},{3,11},{11,3},{4,12},{12,4},... | collective-permute-start | bytes 9437192 | tf_op jit(solution)/shard_map/pooled/ppermute | solution.py:40
  151.4 4.6 %copy-start.17 = (s32[96,1]{0,1:T(1,128)S(1)}, s32[96,1]{0,1:T(1,128)}, u32[]{:S(2)}) copy-start(s32[96,1]{0,1:T(1,128)} %param.9) | copy-start | bytes 1156
  151.4 4.9 %copy-start.18 = (s32[96]{0:T(128)S(1)}, s32[96]{0:T(128)}, u32[]{:S(2)}) copy-start(s32[96]{0:T(128)} %param.8) | copy-start | bytes 1156
  151.4 25.7 %all-to-all-start = ((bf16[8,96,1024]{2,1,0:T(8,128)(2,1)}), bf16[8,96,1024]{2,1,0:T(8,128)(2,1)S(1)}, u32[]{:S(2)}, u32[]{:S(2)}) async-start(bf16[8,96,1024]{2,1,0:T(8,128)(2,1)} %bitcast.4), calls=%async_computation | async-start | bytes 3145728 | tf_op jit(solution)/shard_map/pooled/all_to_all | solution.py:466
  201.9 1.9 collective-permute-start.17
  (7 other events, 5.7 us)
Sparse Core Ops, SparseCore 0:
  62.2 5.9 sort.11.cloned.1.call-done
  (1 shorter events, 0.0 us)

commit v3 on v2

--- a/solution.py
+++ b/solution.py
@@ -20,7 +20,7 @@
 SEQ_BITS = 4
 NONE = 1 << 30
 BOUNDS = 64
-CHUNK = 512
+CHUNK = 256
 WINDOW = 384
 LIMIT = 5.4 * 5.4
 ERF_Q = (
@@ -68,7 +68,7 @@
     )(*sources)
 
 
-def joined(rings, starts, rows):
+def joined(rings, starts, rows, extra=None):
     sources, shapes, moves = [], [], []
     for result, (pieces, start) in enumerate(zip(rings, starts)):
         half = rows // 2
@@ -78,6 +78,11 @@
                 to_row = (which * len(pieces) + number) * half
                 moves.append((len(sources) + number, start + which * half, result, to_row, half))
         sources += pieces
+    if extra is not None:
+        height, width = shapes[-1]
+        shapes[-1] = (height + extra.shape[0], width)
+        moves.append((len(sources), 0, len(shapes) - 1, height, extra.shape[0]))
+        sources.append(extra)
     return copied(sources, shapes, moves)
 
 
@@ -118,7 +123,7 @@
     return jnp.concatenate([high, (values - high.astype(jnp.float32)).astype(jnp.bfloat16)], axis=0)
 
 
-def prepare(keys, counts, table, positions, x_out, docs_out, bounds, total, rows32, table32, listed):
+def prepare(keys, counts, table, positions, x_out, docs_out, bounds, normed_out, total, rows32, table32, listed, sem):
     width = table.shape[1]
     pieces = width // LANES
 
@@ -205,6 +210,9 @@
             pl.BlockSpec((TILE, LANES), lambda i: (i, 0)),
         ],
     )(x_out, docs_out)
+    copy = pltpu.make_async_copy(total.at[pl.ds(0, own), :], normed_out, sem)
+    copy.start()
+    copy.wait()
 
 
 def run_prepare(keys, counts, embed_table, positions, group):
@@ -216,17 +224,19 @@
     return pl.pallas_call(
         prepare,
         in_specs=[smem, smem, vmem, vmem],
-        out_specs=[hbm, hbm, smem, vmem],
+        out_specs=[hbm, hbm, smem, hbm],
         out_shape=[
             jax.ShapeDtypeStruct((most, width), jnp.bfloat16),
             jax.ShapeDtypeStruct((most, LANES), jnp.int32),
             jax.ShapeDtypeStruct((BOUNDS,), jnp.int32),
-            jax.ShapeDtypeStruct((group + WINDOW, width), jnp.float32),
+            jax.ShapeDtypeStruct((group, width), jnp.float32),
         ],
         scratch_shapes=[
+            pltpu.VMEM((group + WINDOW, width), jnp.float32),
             pltpu.VMEM((TILE * pieces, LANES), jnp.float32),
             pltpu.VMEM((vocab_rows * pieces, LANES), jnp.float32),
             pltpu.SMEM((most + TILE + 8,), jnp.int32),
+            pltpu.SemaphoreType.DMA,
         ],
         compiler_params=pltpu.CompilerParams(vmem_limit_bytes=44 << 20),
         cost_estimate=pl.CostEstimate(flops=1 << 30, bytes_accessed=1 << 20, transcendentals=0),
@@ -274,16 +284,22 @@
     return ready
 
 
-def activate(inputs, w_in, hidden, first):
+def activate(inputs, w_in, hidden, first, staged):
     rows = pl.ds(0, inputs.shape[0])
-    for number in range(w_in.shape[0] // CHUNK):
-        weights = w_in[pl.ds(number * CHUNK, CHUNK), :]
-        pre = lax.dot_general(inputs, weights, (((1,), (1,)), ((), ())), preferred_element_type=jnp.float32)
-        hidden[rows, pl.ds(first + number * CHUNK, CHUNK)] = half_gelu(pre).astype(jnp.bfloat16)
+    steps = w_in.shape[0] // CHUNK
+    for number in range(steps + 1):
+        if number < steps:
+            weights = w_in[pl.ds(number * CHUNK, CHUNK), :]
+            staged[number % 2, rows, :] = lax.dot_general(
+                inputs[...], weights, (((1,), (1,)), ((), ())), preferred_element_type=jnp.float32
+            )
+        if number > 0:
+            columns = pl.ds(first + (number - 1) * CHUNK, CHUNK)
+            hidden[rows, columns] = half_gelu(staged[(number - 1) % 2, rows, :]).astype(jnp.bfloat16)
 
 
 def first_units(near, bounds, x_all, *refs):
-    pieces, (out, x, w_in, hidden, w_sems, x_sems, out_sems) = refs[:near], refs[near:]
+    pieces, (out, x, w_in, hidden, staged, w_sems, x_sems, out_sems) = refs[:near], refs[near:]
     tiles = bounds[BOUNDS - 1]
     units = w_in.shape[0] // near
     copies = [
@@ -306,7 +322,7 @@
         def _():
             store(tile - 4, slot).wait()
 
-        activate(x[slot, pl.ds(0, count * TILE), :], w_in, hidden.at[slot], 0)
+        activate(x.at[slot, pl.ds(0, count * TILE), :], w_in, hidden.at[slot], 0, staged)
         store(tile, slot).start()
 
     over_tiles(tiles, several)
@@ -321,7 +337,7 @@
 
 def second_units(near, far, bounds, x_all, docs_all, normed, hidden_all, *refs):
     pieces, refs = refs[: near + far], refs[near + far :]
-    own, other, total, x, docs, w_in, w_out, hidden, w_sems, x_sems, docs_sems, hidden_sems, ends = refs
+    own, other, total, x, docs, w_in, w_out, hidden, staged, w_sems, x_sems, docs_sems, hidden_sems, ends = refs
     tiles = bounds[BOUNDS - 1]
     group = own.shape[0]
     units = pieces[0].shape[0] // 2
@@ -331,7 +347,7 @@
         pltpu.make_async_copy(part, whole.at[pl.ds(row, units), :], w_sems.at[number])
         for number, (part, whole, row) in enumerate(parts)
     ]
-    copies.append(pltpu.make_async_copy(normed.at[pl.ds(0, group), :], total.at[pl.ds(0, group), :], ends.at[0]))
+    copies.append(pltpu.make_async_copy(normed, total.at[pl.ds(0, group), :], ends.at[0]))
     for copy in copies:
         copy.start()
     known = hidden.at[:, :, pl.ds(0, near * units)]
@@ -344,7 +360,7 @@
     def several(tile, count):
         slot = ready(tile)
         rows = pl.ds(0, count * TILE)
-        activate(x[slot, rows, :], w_in, hidden.at[slot], near * units)
+        activate(x.at[slot, rows, :], w_in, hidden.at[slot], near * units, staged)
         branch = jnp.dot(hidden[slot, rows, :], w_out[...], preferred_element_type=jnp.float32)
         for one in range(count):
             part = slice(one * TILE, (one + 1) * TILE)
@@ -374,24 +390,25 @@
             pltpu.VMEM((2, 2 * TILE, width), jnp.bfloat16),
             pltpu.VMEM((units, width), jnp.bfloat16),
             pltpu.VMEM((2, 2 * TILE, units), jnp.bfloat16),
+            pltpu.VMEM((2, 2 * TILE, CHUNK), jnp.float32),
             pltpu.SemaphoreType.DMA((len(near),)),
             pltpu.SemaphoreType.DMA((2,)),
             pltpu.SemaphoreType.DMA((2,)),
         ],
-        compiler_params=pltpu.CompilerParams(vmem_limit_bytes=50 << 20),
+        compiler_params=pltpu.CompilerParams(vmem_limit_bytes=44 << 20),
         cost_estimate=pl.CostEstimate(flops=12 << 30, bytes_accessed=16 << 20, transcendentals=0),
     )(bounds, x, *near)
 
 
 def run_second(near, far, bounds, x, docs, normed, hidden):
     most, width = x.shape
-    group = normed.shape[0] - WINDOW
+    group = normed.shape[0]
     units = near[0].shape[0] // 2
     count = len(near) + len(far)
     smem, hbm, anywhere = (pl.BlockSpec(memory_space=space) for space in (pltpu.SMEM, pltpu.HBM, pl.ANY))
     return pl.pallas_call(
         functools.partial(second_units, len(near), len(far)),
-        in_specs=[smem, hbm, anywhere, anywhere, hbm] + [anywhere] * count,
+        in_specs=[smem, hbm, hbm, anywhere, hbm] + [anywhere] * count,
         out_specs=[anywhere, anywhere],
         out_shape=[jax.ShapeDtypeStruct((group, width), jnp.float32)] * 2,
         scratch_shapes=[
@@ -401,6 +418,7 @@
             pltpu.VMEM((len(far) * units, width), jnp.bfloat16),
             pltpu.VMEM((count * units, width), jnp.bfloat16),
             pltpu.VMEM((2, 2 * TILE, count * units), jnp.bfloat16),
+            pltpu.VMEM((2, 2 * TILE, CHUNK), jnp.float32),
             pltpu.SemaphoreType.DMA((count + len(far),)),
             pltpu.SemaphoreType.DMA((2,)),
             pltpu.SemaphoreType.DMA((2,)),
@@ -421,7 +439,21 @@
     with jax.named_scope("weights"):
         half = w_in.shape[0] // 2
         mixed = jnp.concatenate([w_in[:half], w_out[:half], w_in[half:], w_out[half:]], axis=0)
+        lengths = jnp.pad(doc_lengths, (0, width - doc_dev))[None].astype(jnp.bfloat16)
+        over = lax.ppermute(lengths, "x_hi", [(0, 1), (1, 0)])
+        cross = lax.ppermute(lengths, ("core", "x_hi"), [(0, 3), (1, 2), (2, 1), (3, 0)])
+        upper = lax.axis_index("x_hi")
+        places = lax.broadcasted_iota(jnp.int32, (16, width), 0)
+        parts = [(0, 0, lengths), (0, 1, over), (1, 0, step(lengths, "core", 1)), (1, 1, cross)]
+        lengths = functools.reduce(
+            lambda known, part: jnp.where(places == 2 * part[0] + (upper ^ part[1]), part[2], known),
+            parts,
+            jnp.zeros((16, width), jnp.bfloat16),
+        )
         by_z = ring(mixed, "z")
+        first, second = joined([by_z, by_z], [0, 2 * half], 2 * half, lengths)
+        rows = first.shape[0]
+        mixed, token_ids = lax.optimization_barrier((mixed, token_ids))
         ids = token_ids.reshape(n_col, doc_dev * seq)
         ids = jnp.concatenate([ids, step(ids, "core", 1)], axis=0)
         row = ids - lax.axis_index(COL) * vocab_rows
@@ -429,12 +461,13 @@
         token = lax.broadcasted_iota(jnp.int32, ids.shape, 1)
         keys = ((block * doc_dev + (token >> SEQ_BITS)) << 19) + ((token & (seq - 1)) << 15)
         keys = jnp.where((row >= 0) & (row < vocab_rows), keys + (row >> 3) * 64 + (row & 7), NONE)
-        first, second = joined([by_z, by_z], [0, 2 * half], 2 * half)
-        first, second, doc_lengths, keys = lax.optimization_barrier((first, second, doc_lengths, keys))
-        lengths = lax.all_gather(doc_lengths, ("core",) + COL, axis=0, tiled=False)
         first, second = ring(first, X), ring(second, "y")
-        first, second, lengths = lax.optimization_barrier((first, second, lengths))
-        rows = first[0].shape[0]
+        lengths = [piece[rows : rows + 4, :doc_dev].reshape(2, 2, 1, doc_dev) for piece in second]
+        away = lax.broadcasted_iota(jnp.int32, (2, 2, 4, doc_dev), 2) - lax.axis_index("y") & 3
+        lengths = functools.reduce(
+            lambda known, by: jnp.where(away == by[0], by[1], known), zip((3, 1, 2), lengths[1:]), lengths[0]
+        ).reshape(2 * n_col, doc_dev)
+        first, second, lengths, keys = lax.optimization_barrier((first, second, lengths, keys))
         first, second = joined([first, second], [0, 0], rows)
         units = first.shape[0] // 2
         left, right = step(first, "y", 1), step(first, "y", -1)
@@ -442,12 +475,9 @@
         near = [first, left, right, second, down, up]
 
     with jax.named_scope("keys"):
-        blocks, block = 2 * n_col, doc_dev * seq
-        lengths = lengths.reshape(2, n_col, doc_dev)
-        lengths = jnp.where(lax.axis_index("core") == 0, lengths, lengths[::-1]).reshape(blocks, doc_dev)
-        token = jnp.arange(block, dtype=jnp.int32)[None, :]
+        token = jnp.arange(doc_dev * seq, dtype=jnp.int32)[None, :]
         of_doc = (jnp.arange(doc_dev, dtype=jnp.int32)[:, None] == token >> SEQ_BITS).astype(jnp.bfloat16)
-        used = jnp.dot(lengths.astype(jnp.bfloat16), of_doc, preferred_element_type=jnp.float32)
+        used = jnp.dot(lengths, of_doc, preferred_element_type=jnp.float32)
         keys = jnp.where((token & (seq - 1)).astype(jnp.float32) < used, keys, NONE)
         counts = jnp.sum((keys < NONE).astype(jnp.int32), axis=1)
         keys = lax.sort(keys, dimension=1)[:, :SHARD_CAP].reshape(-1)

time: 229 us -> 217 us (0.948)
  blocking collectives: 50 us -> 35.1 us
  waiting for transfers between devices: 33.6 us -> 43.2 us
  starting transfers between devices: 43.2 us -> 34.2 us
  Pallas kernels: 62.6 us -> 71 us
  local copies, waits for them, and re-layouts: 18.6 us -> 13.1 us
    unnamed x1 -> x0, blocking collectives: 12.2 us -> none
    ppermute x18 -> x19, starting transfers between devices: 38.6 us -> 27.2 us  [step(): lax.ppermute(value, axis, [(place(i), place((i + by) % count)) for i in r...]
    ppermute x18 -> x19, waiting for transfers between devices: 12.9 us -> 22.5 us  [step(): lax.ppermute(value, axis, [(place(i), place((i + by) % count)) for i in r...]
    unnamed x44 -> x32, local copies, waits for them, and re-layouts: 9.91 us -> 3.19 us
    pallas_call x1, Pallas kernels: 21.5 us -> 26.4 us  [run_prepare(): pl.pallas_call(prepare, in_specs=[smem, smem, vmem, vmem], out_specs=[hbm...]
    ppermute x0 -> x2, starting transfers between devices: none -> 3.05 us  [the longest x1 2.62 us: local(): lax.ppermute(lengths, ('core', 'x_hi'), [(0, 3), (1, 2), (2, 1), (3, 0)])]
    all_to_all x1, blocking collectives: 23.3 us -> 20.6 us  [local(): members = lax.all_to_all(outgoing, CHIPS, 0, 0, tiled=True)]
    pallas_call x1, Pallas kernels: 20.2 us -> 22.7 us  [run_second(): pl.pallas_call(functools.partial(second_units, len(near), len(far)), in_s...]
  transfers between devices with their start and end apart: 19 -> 22, of which waited for: 7 -> 10; matrix products, arithmetic and copies ran while one was open for 3% -> 3% of each run, Pallas kernels for 16% -> 21%
where the time goes in v3:
time: 217 us; the launch traced here: 219 us
  Pallas kernels  71 us (33%)
  waiting for transfers between devices  43.2 us (20%)
  blocking collectives  35.1 us (16%)
  starting transfers between devices  34.2 us (16%)
  between operations  13.8 us (6%)
  local copies, waits for them, and re-layouts  13.1 us (6%)
  other arithmetic  6.08 us (3%)
    ppermute x19, starting transfers between devices, step(): lax.ppermute(value, axis, [(place(i), place((i + by) % count)) for i in r...  27.2 us
    pallas_call x1, Pallas kernels, run_prepare(): pl.pallas_call(prepare, in_specs=[smem, smem, vmem, vmem], out_specs=[hbm...  26.4 us
    pallas_call x1, Pallas kernels, run_second(): pl.pallas_call(functools.partial(second_units, len(near), len(far)), in_s...  22.7 us
    ppermute x19, waiting for transfers between devices, step(): lax.ppermute(value, axis, [(place(i), place((i + by) % count)) for i in r...  22.5 us
    all_to_all x1, waiting for transfers between devices, local(): sums = lax.all_to_all(sums, COL, 0, 0, tiled=True)  20.7 us
    all_to_all x1, blocking collectives, local(): members = lax.all_to_all(outgoing, CHIPS, 0, 0, tiled=True)  20.6 us
    pallas_call x1, Pallas kernels, run_first(): pl.pallas_call(functools.partial(first_units, len(near)), in_specs=[smem,...  16.9 us
    all_to_all x1, blocking collectives, local(): lax.all_to_all(best.reshape(n_clusters, 4), CHIPS, 0, 0, tiled=True)  14.6 us
  transfers between devices with their start and end apart: 22, of which 10 were waited for; matrix products, arithmetic and copies ran while one was open for 3% of the time, Pallas kernels for 21%

profile of v3, /device:TPU:0, one launch (start us, length us, event | category | flops | bytes accessed | tf_op | source)
XLA Modules:
  0.0 218.5 jit_solution(4934793101132661421)
XLA Ops:
  7.3 2.6 %collective-permute-start.3 = (bf16[1,1024]{1,0:T(2,128)(2,1)S(1)}, bf16[1,1024]{1,0:T(2,128)(2,1)S(1)}, u32[]{:S(2)}, u32[]{:S(2)}) collective-permute-start(bf16[1,1024]{1,0:T(2,128)(2,1)S(1)} %convert_element_type.48), channel_id=1, source_target_pairs={{0,12},{4,8},{8,4},{12,0},{1,13},{5,9},{9,5},{13,1},{2,14},{6,10},... | collective-permute-start | bytes 6152 | tf_op jit(solution)/shard_map/weights/ppermute | solution.py:444
  11.9 2.1 collective-permute-start
  13.9 2.2 %collective-permute-start.1 = (bf16[64,1024]{1,0:T(8,128)(2,1)S(1)}, bf16[64,1024]{1,0:T(8,128)(2,1)S(1)}, u32[]{:S(2)}, u32[]{:S(2)}) collective-permute-start(bf16[64,1024]{1,0:T(8,128)(2,1)S(1)} %pad_maximum_fusion.refs_0_.refs_4_), channel_id=1, source_target_pairs={{0,48},{16,0},{32,16},{48,32},{1,49},{17,1},{33,17},{49,33},{2,50}... | collective-permute-start | bytes 393224 | tf_op jit(solution)/shard_map/weights/ppermute | solution.py:40
  17.3 1.9 collective-permute-start.2
  20.1 3.8 %collective-permute-done.2.refs_3_.refs_7_ = bf16[64,1024]{1,0:T(8,128)(2,1)S(1)} collective-permute-done((bf16[64,1024]{1,0:T(8,128)(2,1)S(1)}, bf16[64,1024]{1,0:T(8,128)(2,1)S(1)}, u32[]{:S(2)}, u32[]{:S(2)}) %collective-permute-start.2) | collective-permute-done | bytes 131104 | tf_op jit(solution)/shard_map/weights/ppermute | solution.py:40
  24.5 2.0 weights.2
  26.5 3.3 %collective-permute-start.11 = (bf16[144,1024]{1,0:T(8,128)(2,1)}, bf16[144,1024]{1,0:T(8,128)(2,1)S(1)}, u32[]{:S(2)}, u32[]{:S(2)}) collective-permute-start(bf16[144,1024]{1,0:T(8,128)(2,1)} %get-tuple-element.39.refs_4_), channel_id=1, source_target_pairs={{0,2},{1,3},{2,0},{3,1},{4,6},{5,7},{6,4},{7,5},{8,10},{9,11},{10,... | collective-permute-start | bytes 884744 | tf_op jit(solution)/shard_map/weights/ppermute | solution.py:40
  30.1 1.1 collective-permute-start.10
  32.2 1.5 collective-permute-start.6
  33.6 1.7 collective-permute-start.7
  35.4 2.9 %collective-permute-done.11.refs_7_ = bf16[144,1024]{1,0:T(8,128)(2,1)S(1)} collective-permute-done((bf16[144,1024]{1,0:T(8,128)(2,1)}, bf16[144,1024]{1,0:T(8,128)(2,1)S(1)}, u32[]{:S(2)}, u32[]{:S(2)}) %collective-permute-start.11) | collective-permute-done | bytes 294944 | tf_op jit(solution)/shard_map/weights/ppermute | solution.py:40
  38.3 3.0 %collective-permute-start.8 = (bf16[128,1024]{1,0:T(8,128)(2,1)}, bf16[128,1024]{1,0:T(8,128)(2,1)S(1)}, u32[]{:S(2)}, u32[]{:S(2)}) collective-permute-start(bf16[128,1024]{1,0:T(8,128)(2,1)} %get-tuple-element.35.refs_0_), channel_id=1, source_target_pairs={{0,4},{64,68},{4,0},{68,64},{1,5},{65,69},{5,1},{69,65},{2,6},{66,... | collective-permute-start | bytes 786440 | tf_op jit(solution)/shard_map/weights/ppermute | solution.py:40
  42.9 3.4 %collective-permute-done.8.refs_3_ = bf16[128,1024]{1,0:T(8,128)(2,1)S(1)} collective-permute-done((bf16[128,1024]{1,0:T(8,128)(2,1)}, bf16[128,1024]{1,0:T(8,128)(2,1)S(1)}, u32[]{:S(2)}, u32[]{:S(2)}) %collective-permute-start.8) | collective-permute-done | bytes 262176 | tf_op jit(solution)/shard_map/weights/ppermute | solution.py:40
  47.1 3.1 %weights.3 = (bf16[512,1024]{1,0:T(8,128)(2,1)}, bf16[512,1024]{1,0:T(8,128)(2,1)}) custom-call(bf16[128,1024]{1,0:T(8,128)(2,1)} %get-tuple-element.35.refs_0_, bf16[128,1024]{1,0:T(8,128)(2,1)} %copy-done.10, bf16[128,1024]{1,0:T(8,128)(2,1)} %copy-done.11, bf16[128,1024]{1,0:T(8,128)(2,1)} %copy-done.12, bf16[144,1024]{1,0:T(8,128)(2,1)} %get-tuple-element.39.refs_4_, ...), custom_call_target="tpu_custom_call" | custom-call | flops 1024 | bytes 1024 | tf_op jit(solution)/shard_map/weights/pallas_call | solution.py:61
  50.2 1.7 collective-permute-start.13
  51.8 1.6 collective-permute-start.14
  53.5 1.5 collective-permute-start.15
  55.0 1.7 collective-permute-start.16
  57.7 2.1 collective-permute-start.17
  59.8 4.2 %sort.9.cloned.1.call-done = s32[16,1536]{1,0:T(8,128)} async-done(((s32[16,1536]{1,0:T(8,128)}), s32[16,1536]{1,0:T(8,128)}) %sort.9.cloned.1.call-update) | async-done | bytes 98320 | tf_op jit(solution)/shard_map/keys/sort | solution.py:483
  64.8 26.4 %prepare.1 = (bf16[6144,1024]{1,0:T(8,128)(2,1)}, s32[6144,128]{1,0:T(8,128)S(1)}, s32[64]{0:T(128)S(1)}, f32[768,1024]{1,0:T(8,128)S(1)}) custom-call(s32[6144]{0:T(1024)S(1)} %reshape.104.keys, s32[16]{0:T(128)S(1)} %get-tuple-element.53.counts, bf16[3840,1024]{1,0:T(8,128)(2,1)} %table.1, f32[128,128]{1,0:T(8,128)S(1)} %reshape.112.positions), custom_call_target="tpu_custom_call" | custom-call | flops 1073741824 | bytes 1048576 | tf_op jit(solution)/shard_map/prepare/pallas_call | solution.py:224
  91.2 1.6 copy-done
  92.9 16.9 %forward.2.hidden_all = bf16[6144,1536]{1,0:T(8,128)(2,1)} custom-call(s32[64]{0:T(128)S(1)} %get-tuple-element.31.bounds, bf16[6144,1024]{1,0:T(8,128)(2,1)} %get-tuple-element.32.x_all, bf16[512,1024]{1,0:T(8,128)(2,1)S(1)} %copy-done.1, bf16[512,1024]{1,0:T(8,128)(2,1)S(1)} %collective-permute-done.13.refs_1_, ...), custom_call_target="tpu_custom_call" | custom-call | flops 12884901888 | bytes 16777216 | tf_op jit(solution)/shard_map/forward/pallas_call | solution.py:384
  109.8 4.4 %collective-permute-done.18.refs_7_ = bf16[512,1024]{1,0:T(8,128)(2,1)S(1)} collective-permute-done((bf16[512,1024]{1,0:T(8,128)(2,1)S(1)}, bf16[512,1024]{1,0:T(8,128)(2,1)S(1)}, u32[]{:S(2)}, u32[]{:S(2)}) %collective-permute-start.18) | collective-permute-done | bytes 1048608 | tf_op jit(solution)/shard_map/forward/ppermute | solution.py:40
  114.2 22.7 %forward.3 = (f32[768,1024]{1,0:T(8,128)S(1)}, f32[768,1024]{1,0:T(8,128)S(1)}) custom-call(s32[64]{0:T(128)S(1)} %get-tuple-element.31.bounds, bf16[6144,1024]{1,0:T(8,128)(2,1)} %get-tuple-element.32.x_all, s32[6144,128]{1,0:T(8,128)S(1)} %get-tuple-element.33.docs_all, f32[768,1024]{1,0:T(8,128)} %copy-done, bf16[6144,1536]{1,0:T(8,128)(2,1)} %forward.2.hidden_all, ...), custom_call_target="tpu_custom_call" | custom-call | flops 17179869184 | bytes 25165824 | tf_op jit(solution)/shard_map/forward/pallas_call | solution.py:409
  137.0 5.6 %collective-permute-done.19 = f32[768,1024]{1,0:T(8,128)S(1)} collective-permute-done((f32[768,1024]{1,0:T(8,128)S(1)}, f32[768,1024]{1,0:T(8,128)S(1)}, u32[]{:S(2)}, u32[]{:S(2)}) %collective-permute-start.19) | collective-permute-done | bytes 3145760 | tf_op jit(solution)/shard_map/pooled/ppermute | solution.py:40
  142.7 1.7 add_convert_fusion
  144.4 3.9 %all-to-all-start = ((bf16[8,96,1024]{2,1,0:T(8,128)(2,1)}), bf16[8,96,1024]{2,1,0:T(8,128)(2,1)S(1)}, u32[]{:S(2)}, u32[]{:S(2)}) async-start(bf16[8,96,1024]{2,1,0:T(8,128)(2,1)} %bitcast.9), calls=%async_computation | async-start | bytes 3145728 | tf_op jit(solution)/shard_map/pooled/all_to_all | solution.py:496
  148.6 20.7 %all-to-all-done = bf16[8,96,1024]{2,1,0:T(8,128)(2,1)S(1)} async-done(((bf16[8,96,1024]{2,1,0:T(8,128)(2,1)}), bf16[8,96,1024]{2,1,0:T(8,128)(2,1)S(1)}, u32[]{:S(2)}, u32[]{:S(2)}) %all-to-all-start) | async-done | bytes 1572896 | tf_op jit(solution)/shard_map/pooled/all_to_all | solution.py:496
  170.9 20.6 %all_to_all.16 = bf16[64,4,1024]{2,1,0:T(4,128)(2,1)S(1)} all-to-all(bf16[64,4,1024]{2,1,0:T(4,128)(2,1)S(1)} %select_convert_fusion), channel_id=1, replica_groups=mesh['x_lo'=2,'z'=4,'core'=2,'x_hi'=2,'y'=4] {'x_lo','z','x_hi','y'}, dimensions={0} | all-to-all | bytes 1048576 | tf_op jit(solution)/shard_map/match/all_to_all | solution.py:516
  191.8 1.6 collective-permute-done.20
  195.1 14.6 %all_to_all.17 = f32[64,1,4]{2,1,0:T(1,128)S(1)} all-to-all(f32[64,1,4]{2,1,0:T(1,128)S(1)} %bitcast.16), channel_id=1, replica_groups=mesh['x_lo'=2,'z'=4,'core'=2,'x_hi'=2,'y'=4] {'x_lo','z','x_hi','y'}, dimensions={0} | all-to-all | bytes 2048 | tf_op jit(solution)/shard_map/match/all_to_all | solution.py:527
  (117 shorter events, 16.6 us)
Async XLA Ops:
  6.5 51.2 %copy-start.13 = (bf16[16,1024]{1,0:T(8,128)(2,1)S(1)}, bf16[16,1024]{1,0:T(8,128)(2,1)}, u32[]{:S(2)}) copy-start(bf16[16,1024]{1,0:T(8,128)(2,1)} %param.11) | copy-start | bytes 98308
  6.5 57.5 %sort.9.cloned.1.call-start = ((), (), s32[]{:S(2)}) async-start(), calls=%async_computation.3 | async-start | bytes 294944 | tf_op jit(solution)/shard_map/keys/sort | solution.py:483
  7.3 10.1 %collective-permute-start.3 = (bf16[1,1024]{1,0:T(2,128)(2,1)S(1)}, bf16[1,1024]{1,0:T(2,128)(2,1)S(1)}, u32[]{:S(2)}, u32[]{:S(2)}) collective-permute-start(bf16[1,1024]{1,0:T(2,128)(2,1)S(1)} %convert_element_type.48), channel_id=1, source_target_pairs={{0,12},{4,8},{8,4},{12,0},{1,13},{5,9},{9,5},{13,1},{2,14},{6,10},... | collective-permute-start | bytes 6152 | tf_op jit(solution)/shard_map/weights/ppermute | solution.py:444
  9.9 9.3 %collective-permute-start.4 = (bf16[1,1024]{1,0:T(2,128)(2,1)S(1)}, bf16[1,1024]{1,0:T(2,128)(2,1)S(1)}, u32[]{:S(2)}, u32[]{:S(2)}) collective-permute-start(bf16[1,1024]{1,0:T(2,128)(2,1)S(1)} %convert_element_type.48), channel_id=1, source_target_pairs={{0,8},{8,0},{1,9},{9,1},{2,10},{10,2},{3,11},{11,3},{4,12},{12,4},... | collective-permute-start | bytes 6152 | tf_op jit(solution)/shard_map/weights/ppermute | solution.py:40
  10.6 8.8 %collective-permute-start.5 = (bf16[1,1024]{1,0:T(2,128)(2,1)S(1)}, bf16[1,1024]{1,0:T(2,128)(2,1)S(1)}, u32[]{:S(2)}, u32[]{:S(2)}) collective-permute-start(bf16[1,1024]{1,0:T(2,128)(2,1)S(1)} %convert_element_type.48), channel_id=1, source_target_pairs={{0,4},{4,0},{1,5},{5,1},{2,6},{6,2},{3,7},{7,3},{8,12},{12,8},{9,1... | collective-permute-start | bytes 6152 | tf_op jit(solution)/shard_map/weights/ppermute | solution.py:443
  11.8 12.0 %copy-start.3 = (bf16[64,1024]{1,0:T(8,128)(2,1)}, bf16[64,1024]{1,0:T(8,128)(2,1)S(1)}, u32[]{:S(2)}) copy-start(bf16[64,1024]{1,0:T(8,128)(2,1)S(1)} %pad_maximum_fusion.refs_0_.refs_4_) | copy-start | bytes 393220
  11.9 8.2 %collective-permute-start = (bf16[64,1024]{1,0:T(8,128)(2,1)S(1)}, bf16[64,1024]{1,0:T(8,128)(2,1)S(1)}, u32[]{:S(2)}, u32[]{:S(2)}) collective-permute-start(bf16[64,1024]{1,0:T(8,128)(2,1)S(1)} %pad_maximum_fusion.refs_0_.refs_4_), channel_id=1, source_target_pairs={{0,16},{16,32},{32,48},{48,0},{1,17},{17,33},{33,49},{49,1},{2,18}... | collective-permute-start | bytes 393224 | tf_op jit(solution)/shard_map/weights/ppermute | solution.py:40
  13.9 6.2 %collective-permute-start.1 = (bf16[64,1024]{1,0:T(8,128)(2,1)S(1)}, bf16[64,1024]{1,0:T(8,128)(2,1)S(1)}, u32[]{:S(2)}, u32[]{:S(2)}) collective-permute-start(bf16[64,1024]{1,0:T(8,128)(2,1)S(1)} %pad_maximum_fusion.refs_0_.refs_4_), channel_id=1, source_target_pairs={{0,48},{16,0},{32,16},{48,32},{1,49},{17,1},{33,17},{49,33},{2,50}... | collective-permute-start | bytes 393224 | tf_op jit(solution)/shard_map/weights/ppermute | solution.py:40
  17.3 6.5 %collective-permute-start.2 = (bf16[64,1024]{1,0:T(8,128)(2,1)S(1)}, bf16[64,1024]{1,0:T(8,128)(2,1)S(1)}, u32[]{:S(2)}, u32[]{:S(2)}) collective-permute-start(bf16[64,1024]{1,0:T(8,128)(2,1)S(1)} %pad_maximum_fusion.refs_0_.refs_4_), channel_id=1, source_target_pairs={{0,32},{16,48},{32,0},{48,16},{1,33},{17,49},{33,1},{49,17},{2,34}... | collective-permute-start | bytes 393224 | tf_op jit(solution)/shard_map/weights/ppermute | solution.py:40
  19.2 14.4 %collective-permute-start.12 = (s32[8,1536]{1,0:T(8,128)S(1)}, s32[8,1536]{1,0:T(8,128)S(1)}, u32[]{:S(2)}, u32[]{:S(2)}) collective-permute-start(s32[8,1536]{1,0:T(8,128)S(1)} %reshape.103), channel_id=1, source_target_pairs={{0,8},{8,0},{1,9},{9,1},{2,10},{10,2},{3,11},{11,3},{4,12},{12,4},... | collective-permute-start | bytes 147464 | tf_op jit(solution)/shard_map/weights/ppermute | solution.py:40
  20.1 3.8 %copy-start.4 = (bf16[64,1024]{1,0:T(8,128)(2,1)}, bf16[64,1024]{1,0:T(8,128)(2,1)S(1)}, u32[]{:S(2)}) copy-start(bf16[64,1024]{1,0:T(8,128)(2,1)S(1)} %collective-permute-done.refs_1_.refs_5_) | copy-start | bytes 393220
  26.5 11.7 %collective-permute-start.11 = (bf16[144,1024]{1,0:T(8,128)(2,1)}, bf16[144,1024]{1,0:T(8,128)(2,1)S(1)}, u32[]{:S(2)}, u32[]{:S(2)}) collective-permute-start(bf16[144,1024]{1,0:T(8,128)(2,1)} %get-tuple-element.39.refs_4_), channel_id=1, source_target_pairs={{0,2},{1,3},{2,0},{3,1},{4,6},{5,7},{6,4},{7,5},{8,10},{9,11},{10,... | collective-permute-start | bytes 884744 | tf_op jit(solution)/shard_map/weights/ppermute | solution.py:40
  30.1 12.1 %collective-permute-start.10 = (bf16[144,1024]{1,0:T(8,128)(2,1)}, bf16[144,1024]{1,0:T(8,128)(2,1)S(1)}, u32[]{:S(2)}, u32[]{:S(2)}) collective-permute-start(bf16[144,1024]{1,0:T(8,128)(2,1)} %get-tuple-element.39.refs_4_), channel_id=1, source_target_pairs={{0,3},{1,0},{2,1},{3,2},{4,7},{5,4},{6,5},{7,6},{8,11},{9,8},{10,9... | collective-permute-start | bytes 884744 | tf_op jit(solution)/shard_map/weights/ppermute | solution.py:40
  31.2 11.1 %collective-permute-start.9 = (bf16[144,1024]{1,0:T(8,128)(2,1)}, bf16[144,1024]{1,0:T(8,128)(2,1)S(1)}, u32[]{:S(2)}, u32[]{:S(2)}) collective-permute-start(bf16[144,1024]{1,0:T(8,128)(2,1)} %get-tuple-element.39.refs_4_), channel_id=1, source_target_pairs={{0,1},{1,2},{2,3},{3,0},{4,5},{5,6},{6,7},{7,4},{8,9},{9,10},{10,1... | collective-permute-start | bytes 884744 | tf_op jit(solution)/shard_map/weights/ppermute | solution.py:40
  32.2 10.6 %collective-permute-start.6 = (bf16[128,1024]{1,0:T(8,128)(2,1)}, bf16[128,1024]{1,0:T(8,128)(2,1)S(1)}, u32[]{:S(2)}, u32[]{:S(2)}) collective-permute-start(bf16[128,1024]{1,0:T(8,128)(2,1)} %get-tuple-element.35.refs_0_), channel_id=1, source_target_pairs={{0,64},{64,4},{4,68},{68,0},{1,65},{65,5},{5,69},{69,1},{2,66},{66... | collective-permute-start | bytes 786440 | tf_op jit(solution)/shard_map/weights/ppermute | solution.py:40
  33.6 9.3 %collective-permute-start.7 = (bf16[128,1024]{1,0:T(8,128)(2,1)}, bf16[128,1024]{1,0:T(8,128)(2,1)S(1)}, u32[]{:S(2)}, u32[]{:S(2)}) collective-permute-start(bf16[128,1024]{1,0:T(8,128)(2,1)} %get-tuple-element.35.refs_0_), channel_id=1, source_target_pairs={{0,68},{64,0},{4,64},{68,4},{1,69},{65,1},{5,65},{69,5},{2,70},{66... | collective-permute-start | bytes 786440 | tf_op jit(solution)/shard_map/weights/ppermute | solution.py:40
  38.3 8.1 %copy-start.7 = (bf16[144,1024]{1,0:T(8,128)(2,1)}, bf16[144,1024]{1,0:T(8,128)(2,1)S(1)}, u32[]{:S(2)}) copy-start(bf16[144,1024]{1,0:T(8,128)(2,1)S(1)} %collective-permute-done.11.refs_7_) | copy-start | bytes 884740
  38.3 8.1 %collective-permute-start.8 = (bf16[128,1024]{1,0:T(8,128)(2,1)}, bf16[128,1024]{1,0:T(8,128)(2,1)S(1)}, u32[]{:S(2)}, u32[]{:S(2)}) collective-permute-start(bf16[128,1024]{1,0:T(8,128)(2,1)} %get-tuple-element.35.refs_0_), channel_id=1, source_target_pairs={{0,4},{64,68},{4,0},{68,64},{1,5},{65,69},{5,1},{69,65},{2,6},{66,... | collective-permute-start | bytes 786440 | tf_op jit(solution)/shard_map/weights/ppermute | solution.py:40
  42.2 4.1 %copy-start.8 = (bf16[144,1024]{1,0:T(8,128)(2,1)}, bf16[144,1024]{1,0:T(8,128)(2,1)S(1)}, u32[]{:S(2)}) copy-start(bf16[144,1024]{1,0:T(8,128)(2,1)S(1)} %collective-permute-done.10.refs_6_) | copy-start | bytes 884740
  42.3 4.1 %copy-start.9 = (bf16[144,1024]{1,0:T(8,128)(2,1)}, bf16[144,1024]{1,0:T(8,128)(2,1)S(1)}, u32[]{:S(2)}) copy-start(bf16[144,1024]{1,0:T(8,128)(2,1)S(1)} %collective-permute-done.9.refs_5_) | copy-start | bytes 884740
  50.2 42.7 %collective-permute-start.13 = (bf16[512,1024]{1,0:T(8,128)(2,1)}, bf16[512,1024]{1,0:T(8,128)(2,1)S(1)}, u32[]{:S(2)}, u32[]{:S(2)}) collective-permute-start(bf16[512,1024]{1,0:T(8,128)(2,1)} %get-tuple-element.43.refs_0_), channel_id=1, source_target_pairs={{0,1},{1,2},{2,3},{3,0},{4,5},{5,6},{6,7},{7,4},{8,9},{9,10},{10,1... | collective-permute-start | bytes 3145736 | tf_op jit(solution)/shard_map/weights/ppermute | solution.py:40
  51.8 41.0 %collective-permute-start.14 = (bf16[512,1024]{1,0:T(8,128)(2,1)}, bf16[512,1024]{1,0:T(8,128)(2,1)S(1)}, u32[]{:S(2)}, u32[]{:S(2)}) collective-permute-start(bf16[512,1024]{1,0:T(8,128)(2,1)} %get-tuple-element.43.refs_0_), channel_id=1, source_target_pairs={{0,3},{1,0},{2,1},{3,2},{4,7},{5,4},{6,5},{7,6},{8,11},{9,8},{10,9... | collective-permute-start | bytes 3145736 | tf_op jit(solution)/shard_map/weights/ppermute | solution.py:40
  53.5 39.4 %collective-permute-start.15 = (bf16[512,1024]{1,0:T(8,128)(2,1)}, bf16[512,1024]{1,0:T(8,128)(2,1)S(1)}, u32[]{:S(2)}, u32[]{:S(2)}) collective-permute-start(bf16[512,1024]{1,0:T(8,128)(2,1)} %get-tuple-element.44.refs_3_), channel_id=1, source_target_pairs={{0,64},{64,4},{4,68},{68,0},{1,65},{65,5},{5,69},{69,1},{2,66},{66... | collective-permute-start | bytes 3145736 | tf_op jit(solution)/shard_map/weights/ppermute | solution.py:40
  55.0 37.9 %collective-permute-start.16 = (bf16[512,1024]{1,0:T(8,128)(2,1)}, bf16[512,1024]{1,0:T(8,128)(2,1)}, u32[]{:S(2)}, u32[]{:S(2)}) collective-permute-start(bf16[512,1024]{1,0:T(8,128)(2,1)} %get-tuple-element.44.refs_3_), channel_id=1, source_target_pairs={{0,68},{64,0},{4,64},{68,4},{1,69},{65,1},{5,65},{69,5},{2,70},{66... | collective-permute-start | bytes 3145736 | tf_op jit(solution)/shard_map/weights/ppermute | solution.py:40
  57.7 52.0 %collective-permute-start.17 = (bf16[512,1024]{1,0:T(8,128)(2,1)}, bf16[512,1024]{1,0:T(8,128)(2,1)}, u32[]{:S(2)}, u32[]{:S(2)}) collective-permute-start(bf16[512,1024]{1,0:T(8,128)(2,1)} %get-tuple-element.43.refs_0_), channel_id=1, source_target_pairs={{0,2},{1,3},{2,0},{3,1},{4,6},{5,7},{6,4},{7,5},{8,10},{9,11},{10,... | collective-permute-start | bytes 3145736 | tf_op jit(solution)/shard_map/forward/ppermute | solution.py:40
  64.8 28.0 %copy-start.2 = (bf16[512,1024]{1,0:T(8,128)(2,1)S(1)}, bf16[512,1024]{1,0:T(8,128)(2,1)}, u32[]{:S(2)}) copy-start(bf16[512,1024]{1,0:T(8,128)(2,1)} %get-tuple-element.44.refs_3_) | copy-start | bytes 3145732
  64.8 28.1 %copy-start.1 = (bf16[512,1024]{1,0:T(8,128)(2,1)S(1)}, bf16[512,1024]{1,0:T(8,128)(2,1)}, u32[]{:S(2)}) copy-start(bf16[512,1024]{1,0:T(8,128)(2,1)} %get-tuple-element.43.refs_0_) | copy-start | bytes 3145732
  92.8 21.3 %collective-permute-start.18 = (bf16[512,1024]{1,0:T(8,128)(2,1)S(1)}, bf16[512,1024]{1,0:T(8,128)(2,1)S(1)}, u32[]{:S(2)}, u32[]{:S(2)}) collective-permute-start(bf16[512,1024]{1,0:T(8,128)(2,1)S(1)} %copy-done.2), channel_id=1, source_target_pairs={{0,4},{64,68},{4,0},{68,64},{1,5},{65,69},{5,1},{69,65},{2,6},{66,... | collective-permute-start | bytes 3145736 | tf_op jit(solution)/shard_map/forward/ppermute | solution.py:40
  136.9 5.7 %collective-permute-start.19 = (f32[768,1024]{1,0:T(8,128)S(1)}, f32[768,1024]{1,0:T(8,128)S(1)}, u32[]{:S(2)}, u32[]{:S(2)}) collective-permute-start(f32[768,1024]{1,0:T(8,128)S(1)} %get-tuple-element.46), channel_id=1, source_target_pairs={{0,8},{8,0},{1,9},{9,1},{2,10},{10,2},{3,11},{11,3},{4,12},{12,4},... | collective-permute-start | bytes 9437192 | tf_op jit(solution)/shard_map/pooled/ppermute | solution.py:40
  144.4 4.0 %copy-start.14 = (s32[96,1]{0,1:T(1,128)S(1)}, s32[96,1]{0,1:T(1,128)}, u32[]{:S(2)}) copy-start(s32[96,1]{0,1:T(1,128)} %param.9) | copy-start | bytes 1156
  144.4 25.0 %all-to-all-start = ((bf16[8,96,1024]{2,1,0:T(8,128)(2,1)}), bf16[8,96,1024]{2,1,0:T(8,128)(2,1)S(1)}, u32[]{:S(2)}, u32[]{:S(2)}) async-start(bf16[8,96,1024]{2,1,0:T(8,128)(2,1)} %bitcast.9), calls=%async_computation | async-start | bytes 3145728 | tf_op jit(solution)/shard_map/pooled/all_to_all | solution.py:496
  191.5 1.9 collective-permute-start.20
  (6 other events, 13.9 us)
Sparse Core Ops, SparseCore 0:
  57.8 5.9 sort.11.cloned.1.call-done
  (1 shorter events, 0.0 us)

commit v4 on v3

--- a/solution.py
+++ b/solution.py
@@ -18,6 +18,7 @@
 LANES = 128
 SUB = 64
 SEQ_BITS = 4
+SEQ = 1 << SEQ_BITS
 NONE = 1 << 30
 BOUNDS = 64
 CHUNK = 256
@@ -64,6 +65,7 @@
         out_specs=[pl.BlockSpec(memory_space=pltpu.VMEM)] * len(shapes),
         out_shape=[jax.ShapeDtypeStruct(shape, sources[0].dtype) for shape in shapes],
         scratch_shapes=[pltpu.SemaphoreType.DMA((len(moves),))],
+        compiler_params=pltpu.CompilerParams(vmem_limit_bytes=8 << 20),
         cost_estimate=pl.CostEstimate(flops=1 << 10, bytes_accessed=1 << 10, transcendentals=0),
     )(*sources)
 
@@ -123,44 +125,90 @@
     return jnp.concatenate([high, (values - high.astype(jnp.float32)).astype(jnp.bfloat16)], axis=0)
 
 
-def prepare(keys, counts, table, positions, x_out, docs_out, bounds, normed_out, total, rows32, table32, listed, sem):
+def compressed(keys, docs_of, used):
+    rows = keys.shape[0]
+    kept = (keys < NONE) & (docs_of < used)
+    ones = kept.astype(jnp.bfloat16)
+    row, lane = (lax.broadcasted_iota(jnp.int32, (LANES, LANES), axis) for axis in range(2))
+    before = jnp.dot(ones, (row < lane).astype(jnp.bfloat16), preferred_element_type=jnp.float32)
+    whole = jnp.dot(ones, jnp.ones((LANES, LANES), jnp.bfloat16), preferred_element_type=jnp.float32)
+    row, lane = (lax.broadcasted_iota(jnp.int32, (rows, rows), axis) for axis in range(2))
+    above = (lane < row).astype(jnp.bfloat16)
+    before += jnp.dot(above, whole.astype(jnp.bfloat16), preferred_element_type=jnp.float32)
+    row, lane = (lax.broadcasted_iota(jnp.int32, keys.shape, axis) for axis in range(2))
+    moves = jnp.where(kept, row * LANES + lane - before.astype(jnp.int32), 0)
+    keys = jnp.where(kept, keys, NONE)
+    for bit in range((rows * LANES - 1).bit_length()):
+        step_by = 1 << bit
+
+        def after(values):
+            if step_by >= LANES:
+                return pltpu.roll(values, rows - step_by // LANES, 0)
+            values = pltpu.roll(values, LANES - step_by, 1)
+            return jnp.where(lane < LANES - step_by, values, pltpu.roll(values, rows - 1, 0))
+
+        next_moves, next_keys = after(moves), after(keys)
+        comes, goes = (next_moves & step_by) != 0, (moves & step_by) != 0
+        keys = jnp.where(comes, next_keys, jnp.where(goes, NONE, keys))
+        moves = jnp.where(comes, next_moves, jnp.where(goes, 0, moves))
+    return keys, jnp.sum(ones.astype(jnp.float32), axis=0, keepdims=True)
+
+
+def prepare(place, ids, l0, l1, l2, l3, table, positions, x_out, docs_out, bounds, normed_out, *scratch):
+    total, rows32, table32, lengths, list_buffer, listed, sem, length_sems = scratch
     width = table.shape[1]
     pieces = width // LANES
 
     def load():
-        def gather_list(block, offset):
-            base = block * SHARD_CAP
-
-            def eight(group, carry):
-                for one in range(8):
-                    listed[offset + group * 8 + one] = keys[base + group * 8 + one]
-                return carry
-
-            lax.fori_loop(0, (counts[block] + 7) >> 3, eight, 0)
-            return offset + counts[block]
-
-        end = lax.fori_loop(0, 16, gather_list, 0)
-
-        def tail(group, carry):
-            for one in range(8):
-                listed[end + group * 8 + one] = NONE
-            return carry
-
-        lax.fori_loop(0, TILE // 8, tail, 0)
+        copies = [
+            pltpu.make_async_copy(piece.at[pl.ds(piece.shape[0] - 16, 16), :], lengths.at[number], length_sems.at[number])
+            for number, piece in enumerate((l0, l1, l2, l3))
+        ]
+        for copy in copies:
+            copy.start()
         total[...] = jnp.zeros_like(total)
 
         def widen(group, carry):
             values = table[pl.ds(pl.multiple_of(group * 16, 16), 16), :].astype(jnp.float32)
             for eight in range(2):
                 for piece in range(pieces):
-                    place = pl.multiple_of((group * 2 + eight) * 8 * pieces + piece * 8, 8)
-                    table32[pl.ds(place, 8), :] = values[
-                        eight * 8 : eight * 8 + 8, piece * LANES : (piece + 1) * LANES
-                    ]
+                    at = pl.multiple_of((group * 2 + eight) * 8 * pieces + piece * 8, 8)
+                    table32[pl.ds(at, 8), :] = values[eight * 8 : eight * 8 + 8, piece * LANES : (piece + 1) * LANES]
             return carry
 
         lax.fori_loop(0, table.shape[0] // 16, widen, 0)
-        return end
+        for copy in copies:
+            copy.wait()
+        row, lane = (lax.broadcasted_iota(jnp.int32, (LANES, LANES), axis) for axis in range(2))
+        of_doc = (row == lane >> SEQ_BITS).astype(jnp.bfloat16)
+        used = []
+        for part in range(4):
+            columns = slice(part * LANES, (part + 1) * LANES)
+            around = [
+                jnp.dot(lengths[number, :, columns], of_doc, preferred_element_type=jnp.float32) for number in range(4)
+            ]
+            for y in range(4):
+                away = (y - place[1]) & 3
+                value = around[0]
+                for by, number in ((3, 1), (1, 2), (2, 3)):
+                    value = jnp.where(away == by, around[number], value)
+                used.append(value)
+        used = jnp.concatenate(used, axis=0).astype(jnp.int32)
+        row, lane = (lax.broadcasted_iota(jnp.int32, ids.shape, axis) for axis in range(2))
+        own_row = ids[...] - place[0]
+        doc = (row >> 4) * (12 * 8) + (row & 15) * 8 + (lane >> SEQ_BITS)
+        time = lane & (SEQ - 1)
+        keys = (doc << 19) + (time << 15) + (own_row >> 3) * 64 + (own_row & 7)
+        inside = (own_row >= 0) & (own_row < table.shape[0]) & ((row & 15) < 12)
+        keys, sums = compressed(jnp.where(inside, keys, NONE), time, used)
+        most = listed.shape[0] - 8
+        list_buffer[pl.ds(0, most), :] = keys[:most]
+        count = jnp.sum(sums, axis=1, keepdims=True).astype(jnp.int32)
+        list_buffer[pl.ds(most, 8), :] = jnp.broadcast_to(count, (8, LANES))
+        copy = pltpu.make_async_copy(list_buffer, listed, sem)
+        copy.start()
+        copy.wait()
+        return listed[most, 0]
 
     end = load()
     tiles = jnp.maximum((end + TILE - 1) >> TILE_BITS, 1)
@@ -168,14 +216,18 @@
     bounds[BOUNDS - 1] = tiles
 
     def tile(x_ref, docs_ref):
-        first = pl.program_id(0) * TILE
+        index = pl.program_id(0)
+        first = index * TILE
+
+        def key_at(slot):
+            return listed[slot >> 7, slot & (LANES - 1)]
 
         def take(group, carry):
             for one in range(8):
-                key = listed[first + group * 8 + one]
-                place = key & 0x7FFF
+                key = listed[2 * index + (group >> 4), (group & 15) * 8 + one]
+                at = key & 0x7FFF
                 when = pl.multiple_of((key >> 12) & 0x78, 8)
-                value = table32[pl.ds(place, pieces, stride=8), :] + positions[pl.ds(when, pieces), :]
+                value = table32[pl.ds(at, pieces, stride=8), :] + positions[pl.ds(when, pieces), :]
                 rows32[pl.ds(group * 8 * pieces + one, pieces, stride=8), :] = value
                 docs_ref[pl.ds(group * 8 + one, 1), :] = jnp.full((1, LANES), key >> 19, jnp.int32)
             return carry
@@ -191,9 +243,8 @@
             normal = centred * lax.rsqrt(var + 1e-05)
             x_ref[pl.ds(sub * SUB, SUB), :] = (normal * 0.5).astype(jnp.bfloat16)
             normed.append(normal)
-        low = jnp.minimum((listed[first] >> 22) << 3, 2 * own - 8)
-        high = jnp.minimum(listed[jnp.clip(end - 1, first, first + TILE - 1)] >> 19, 2 * own - 1)
-        index = pl.program_id(0)
+        low = jnp.minimum((key_at(first) >> 22) << 3, 2 * own - 8)
+        high = jnp.minimum(key_at(jnp.clip(end - 1, first, first + TILE - 1)) >> 19, 2 * own - 1)
         bounds[2 * index] = low
         bounds[2 * index + 1] = high
 
@@ -215,15 +266,14 @@
     copy.wait()
 
 
-def run_prepare(keys, counts, embed_table, positions, group):
-    most = keys.shape[0]
+def run_prepare(place, ids, lengths, embed_table, positions, group, most):
     seq, width = positions.shape
     vocab_rows = embed_table.shape[0]
     pieces = width // LANES
     smem, vmem, hbm = (pl.BlockSpec(memory_space=space) for space in (pltpu.SMEM, pltpu.VMEM, pltpu.HBM))
     return pl.pallas_call(
         prepare,
-        in_specs=[smem, smem, vmem, vmem],
+        in_specs=[smem, vmem] + [pl.BlockSpec(memory_space=pl.ANY)] * 4 + [vmem, vmem],
         out_specs=[hbm, hbm, smem, hbm],
         out_shape=[
             jax.ShapeDtypeStruct((most, width), jnp.bfloat16),
@@ -235,12 +285,15 @@
             pltpu.VMEM((group + WINDOW, width), jnp.float32),
             pltpu.VMEM((TILE * pieces, LANES), jnp.float32),
             pltpu.VMEM((vocab_rows * pieces, LANES), jnp.float32),
-            pltpu.SMEM((most + TILE + 8,), jnp.int32),
+            pltpu.VMEM((4, 16, width), jnp.bfloat16),
+            pltpu.VMEM((most // LANES + 8, LANES), jnp.int32),
+            pltpu.SMEM((most // LANES + 8, LANES), jnp.int32),
             pltpu.SemaphoreType.DMA,
+            pltpu.SemaphoreType.DMA((4,)),
         ],
-        compiler_params=pltpu.CompilerParams(vmem_limit_bytes=44 << 20),
+        compiler_params=pltpu.CompilerParams(vmem_limit_bytes=36 << 20),
         cost_estimate=pl.CostEstimate(flops=1 << 30, bytes_accessed=1 << 20, transcendentals=0),
-    )(keys, counts, embed_table, positions.astype(jnp.float32).reshape(seq * pieces, LANES))
+    )(place, ids, *lengths, embed_table, positions.astype(jnp.float32).reshape(seq * pieces, LANES))
 
 
 def over_tiles(tiles, several):
@@ -439,54 +492,37 @@
     with jax.named_scope("weights"):
         half = w_in.shape[0] // 2
         mixed = jnp.concatenate([w_in[:half], w_out[:half], w_in[half:], w_out[half:]], axis=0)
-        lengths = jnp.pad(doc_lengths, (0, width - doc_dev))[None].astype(jnp.bfloat16)
+        mixed, token_ids, doc_lengths = lax.optimization_barrier((mixed, token_ids, doc_lengths))
+        lengths = jnp.pad(doc_lengths.reshape(doc_dev // 8, 8), ((0, 16 - doc_dev // 8), (0, LANES - 8))).astype(jnp.bfloat16)
         over = lax.ppermute(lengths, "x_hi", [(0, 1), (1, 0)])
         cross = lax.ppermute(lengths, ("core", "x_hi"), [(0, 3), (1, 2), (2, 1), (3, 0)])
-        upper = lax.axis_index("x_hi")
-        places = lax.broadcasted_iota(jnp.int32, (16, width), 0)
-        parts = [(0, 0, lengths), (0, 1, over), (1, 0, step(lengths, "core", 1)), (1, 1, cross)]
-        lengths = functools.reduce(
-            lambda known, part: jnp.where(places == 2 * part[0] + (upper ^ part[1]), part[2], known),
-            parts,
-            jnp.zeros((16, width), jnp.bfloat16),
-        )
+        other = step(lengths, "core", 1)
+        lower = lax.axis_index("x_hi") == 0
+        parts = [jnp.where(lower, a, b) for a, b in ((lengths, over), (over, lengths), (other, cross), (cross, other))]
+        lengths = jnp.pad(jnp.concatenate(parts, axis=1), ((0, 0), (0, width - 4 * LANES)))
         by_z = ring(mixed, "z")
         first, second = joined([by_z, by_z], [0, 2 * half], 2 * half, lengths)
         rows = first.shape[0]
-        mixed, token_ids = lax.optimization_barrier((mixed, token_ids))
-        ids = token_ids.reshape(n_col, doc_dev * seq)
+        ids = token_ids.reshape(n_col, doc_dev * seq // LANES, LANES)
+        ids = jnp.pad(ids, ((0, 0), (0, 16 - ids.shape[1]), (0, 0))).reshape(n_col * 16, LANES)
         ids = jnp.concatenate([ids, step(ids, "core", 1)], axis=0)
-        row = ids - lax.axis_index(COL) * vocab_rows
-        block = lax.broadcasted_iota(jnp.int32, ids.shape, 0)
-        token = lax.broadcasted_iota(jnp.int32, ids.shape, 1)
-        keys = ((block * doc_dev + (token >> SEQ_BITS)) << 19) + ((token & (seq - 1)) << 15)
-        keys = jnp.where((row >= 0) & (row < vocab_rows), keys + (row >> 3) * 64 + (row & 7), NONE)
+        place = jnp.stack([lax.axis_index(COL) * vocab_rows, lax.axis_index("y")]).astype(jnp.int32)
+        first, second, ids = lax.optimization_barrier((first, second, ids))
         first, second = ring(first, X), ring(second, "y")
-        lengths = [piece[rows : rows + 4, :doc_dev].reshape(2, 2, 1, doc_dev) for piece in second]
-        away = lax.broadcasted_iota(jnp.int32, (2, 2, 4, doc_dev), 2) - lax.axis_index("y") & 3
-        lengths = functools.reduce(
-            lambda known, by: jnp.where(away == by[0], by[1], known), zip((3, 1, 2), lengths[1:]), lengths[0]
-        ).reshape(2 * n_col, doc_dev)
-        first, second, lengths, keys = lax.optimization_barrier((first, second, lengths, keys))
+        lengths = second
         first, second = joined([first, second], [0, 0], rows)
         units = first.shape[0] // 2
         left, right = step(first, "y", 1), step(first, "y", -1)
         down, up = step(second, X, 1), step(second, X, -1)
         near = [first, left, right, second, down, up]
 
-    with jax.named_scope("keys"):
-        token = jnp.arange(doc_dev * seq, dtype=jnp.int32)[None, :]
-        of_doc = (jnp.arange(doc_dev, dtype=jnp.int32)[:, None] == token >> SEQ_BITS).astype(jnp.bfloat16)
-        used = jnp.dot(lengths, of_doc, preferred_element_type=jnp.float32)
-        keys = jnp.where((token & (seq - 1)).astype(jnp.float32) < used, keys, NONE)
-        counts = jnp.sum((keys < NONE).astype(jnp.int32), axis=1)
-        keys = lax.sort(keys, dimension=1)[:, :SHARD_CAP].reshape(-1)
-
     with jax.named_scope("prepare"):
-        x, docs, bounds, normed = run_prepare(keys, counts, embed_table, positions, group)
+        most = 2 * n_col * SHARD_CAP
+        x, docs, bounds, normed = run_prepare(place, ids, lengths, embed_table, positions, group, most)
 
     with jax.named_scope("forward"):
-        far = [step(first, "y", 2), step(second, X, 2)]
+        near, x = lax.optimization_barrier((near, x))
+        far = [step(near[0], "y", 2), step(near[3], X, 2)]
         hidden = run_first(near, bounds, x)
         own, other = run_second(near, far, bounds, x, docs, normed, hidden)
 

time: 217 us -> 194 us (0.89); the launches traced: 219 us -> 191 us
  between operations: 13.8 us -> 0.34 us
  Pallas kernels: 71 us -> 58.2 us
  local copies, waits for them, and re-layouts: 13.1 us -> 9.06 us
  waiting for transfers between devices: 43.2 us -> 47.1 us
    pallas_call x1, Pallas kernels: 26.4 us -> 20.9 us  [run_prepare(): pl.pallas_call(prepare, in_specs=[smem, vmem] + [pl.BlockSpec(memory_spac...]
    sort x2 -> x0, local copies, waits for them, and re-layouts: 4.24 us -> none  [local(): keys = lax.sort(keys, dimension=1)[:, :SHARD_CAP].reshape(-1)]
    ppermute x19, waiting for transfers between devices: 22.5 us -> 26.4 us  [step(): lax.ppermute(value, axis, [(place(i), place((i + by) % count)) for i in r...]
    pallas_call x1, Pallas kernels: 22.7 us -> 19.3 us  [run_second(): pl.pallas_call(functools.partial(second_units, len(near), len(far)), in_s...]
    ppermute x1, starting transfers between devices: 0.42 us -> 3.19 us  [local(): over = lax.ppermute(lengths, 'x_hi', [(0, 1), (1, 0)])]
    pallas_call x1, Pallas kernels: 16.9 us -> 14.3 us  [run_first(): pl.pallas_call(functools.partial(first_units, len(near)), in_specs=[smem,...]
    unnamed x32 -> x9, local copies, waits for them, and re-layouts: 3.19 us -> 5.04 us
  transfers between devices with their start and end apart: 22 -> 22, of which waited for: 10 -> 9; matrix products, arithmetic and copies ran while one was open for 3% -> 1% of each run, Pallas kernels for 21% -> 18%
where the time goes in v4:
time: 194 us; the launch traced here: 191 us
  Pallas kernels  58.2 us (30%)
  waiting for transfers between devices  47.1 us (24%)
  blocking collectives  35.3 us (18%)
  starting transfers between devices  35.2 us (18%)
  local copies, waits for them, and re-layouts  9.06 us (5%)
  other arithmetic  5.22 us (3%)
    ppermute x19, waiting for transfers between devices, step(): lax.ppermute(value, axis, [(place(i), place((i + by) % count)) for i in r...  26.4 us
    ppermute x19, starting transfers between devices, step(): lax.ppermute(value, axis, [(place(i), place((i + by) % count)) for i in r...  25.7 us
    pallas_call x1, Pallas kernels, run_prepare(): pl.pallas_call(prepare, in_specs=[smem, vmem] + [pl.BlockSpec(memory_spac...  20.9 us
    all_to_all x1, waiting for transfers between devices, local(): sums = lax.all_to_all(sums, COL, 0, 0, tiled=True)  20.8 us
    all_to_all x1, blocking collectives, local(): members = lax.all_to_all(outgoing, CHIPS, 0, 0, tiled=True)  20.7 us
    pallas_call x1, Pallas kernels, run_second(): pl.pallas_call(functools.partial(second_units, len(near), len(far)), in_s...  19.3 us
    all_to_all x1, blocking collectives, local(): lax.all_to_all(best.reshape(n_clusters, 4), CHIPS, 0, 0, tiled=True)  14.6 us
    pallas_call x1, Pallas kernels, run_first(): pl.pallas_call(functools.partial(first_units, len(near)), in_specs=[smem,...  14.3 us
  transfers between devices with their start and end apart: 22, of which 9 were waited for; matrix products, arithmetic and copies ran while one was open for 1% of the time, Pallas kernels for 18%

profile of v4, /device:TPU:0, one launch (start us, length us, event | category | flops | bytes accessed | tf_op | source)
XLA Modules:
  0.0 191.4 jit_solution(7087627405067154176)
XLA Ops:
  1.7 3.2 %collective-permute-start.3 = (bf16[16,128]{1,0:T(8,128)(2,1)S(1)}, bf16[16,128]{1,0:T(8,128)(2,1)S(1)}, u32[]{:S(2)}, u32[]{:S(2)}) collective-permute-start(bf16[16,128]{1,0:T(8,128)(2,1)S(1)} %pad.17), channel_id=1, source_target_pairs={{0,4},{4,0},{1,5},{5,1},{2,6},{6,2},{3,7},{7,3},{8,12},{12,8},{9,1... | collective-permute-start | bytes 12296 | tf_op jit(solution)/shard_map/weights/ppermute | solution.py:497
  5.4 2.0 %collective-permute-start = (bf16[64,1024]{1,0:T(8,128)(2,1)S(1)}, bf16[64,1024]{1,0:T(8,128)(2,1)S(1)}, u32[]{:S(2)}, u32[]{:S(2)}) collective-permute-start(bf16[64,1024]{1,0:T(8,128)(2,1)S(1)} %pad_maximum_fusion.refs_0_.refs_4_), channel_id=1, source_target_pairs={{0,16},{16,32},{32,48},{48,0},{1,17},{17,33},{33,49},{49,1},{2,18}... | collective-permute-start | bytes 393224 | tf_op jit(solution)/shard_map/weights/ppermute | solution.py:41
  7.4 2.1 %collective-permute-start.1 = (bf16[64,1024]{1,0:T(8,128)(2,1)S(1)}, bf16[64,1024]{1,0:T(8,128)(2,1)S(1)}, u32[]{:S(2)}, u32[]{:S(2)}) collective-permute-start(bf16[64,1024]{1,0:T(8,128)(2,1)S(1)} %pad_maximum_fusion.refs_0_.refs_4_), channel_id=1, source_target_pairs={{0,48},{16,0},{32,16},{48,32},{1,49},{17,1},{33,17},{49,33},{2,50}... | collective-permute-start | bytes 393224 | tf_op jit(solution)/shard_map/weights/ppermute | solution.py:41
  9.5 1.0 copy.18
  10.7 1.9 %collective-permute-start.2 = (bf16[64,1024]{1,0:T(8,128)(2,1)S(1)}, bf16[64,1024]{1,0:T(8,128)(2,1)S(1)}, u32[]{:S(2)}, u32[]{:S(2)}) collective-permute-start(bf16[64,1024]{1,0:T(8,128)(2,1)S(1)} %pad_maximum_fusion.refs_0_.refs_4_), channel_id=1, source_target_pairs={{0,32},{16,48},{32,0},{48,16},{1,33},{17,49},{33,1},{49,17},{2,34}... | collective-permute-start | bytes 393224 | tf_op jit(solution)/shard_map/weights/ppermute | solution.py:41
  12.8 1.2 collective-permute-done.6
  14.0 3.4 %collective-permute-done.2.refs_3_.refs_7_ = bf16[64,1024]{1,0:T(8,128)(2,1)S(1)} collective-permute-done((bf16[64,1024]{1,0:T(8,128)(2,1)S(1)}, bf16[64,1024]{1,0:T(8,128)(2,1)S(1)}, u32[]{:S(2)}, u32[]{:S(2)}) %collective-permute-start.2) | collective-permute-done | bytes 131104 | tf_op jit(solution)/shard_map/weights/ppermute | solution.py:41
  18.3 1.6 collective-permute-start.10
  19.9 1.6 collective-permute-start.7
  21.4 1.7 collective-permute-start.8
  23.1 2.0 %collective-permute-start.9 = (bf16[144,1024]{1,0:T(8,128)(2,1)S(1)}, bf16[144,1024]{1,0:T(8,128)(2,1)S(1)}, u32[]{:S(2)}, u32[]{:S(2)}) collective-permute-start(bf16[144,1024]{1,0:T(8,128)(2,1)S(1)} %get-tuple-element.34.l0.refs_4_), channel_id=1, source_target_pairs={{0,2},{1,3},{2,0},{3,1},{4,6},{5,7},{6,4},{7,5},{8,10},{9,11},{10,... | collective-permute-start | bytes 884744 | tf_op jit(solution)/shard_map/weights/ppermute | solution.py:41
  25.1 1.7 collective-permute-start.11
  26.8 1.8 collective-permute-start.12
  28.6 7.3 %collective-permute-done.11.refs_2_ = bf16[128,1024]{1,0:T(8,128)(2,1)S(1)} collective-permute-done((bf16[128,1024]{1,0:T(8,128)(2,1)S(1)}, bf16[128,1024]{1,0:T(8,128)(2,1)S(1)}, u32[]{:S(2)}, u32[]{:S(2)}) %collective-permute-start.11) | collective-permute-done | bytes 262176 | tf_op jit(solution)/shard_map/weights/ppermute | solution.py:41
  36.1 2.8 %weights.3 = (bf16[512,1024]{1,0:T(8,128)(2,1)S(1)}, bf16[512,1024]{1,0:T(8,128)(2,1)S(1)}) custom-call(bf16[128,1024]{1,0:T(8,128)(2,1)S(1)} %get-tuple-element.36.refs_0_, bf16[128,1024]{1,0:T(8,128)(2,1)S(1)} %collective-permute-done.10.refs_1_, bf16[128,1024]{1,0:T(8,128)(2,1)S(1)} %collective-permute-done.11.refs_2_, ...), custom_call_target="tpu_custom_call" | custom-call | flops 1024 | bytes 1024 | tf_op jit(solution)/shard_map/weights/pallas_call | solution.py:62
  38.9 1.2 collective-permute-start.13
  40.1 2.1 %collective-permute-start.14 = (bf16[512,1024]{1,0:T(8,128)(2,1)S(1)}, bf16[512,1024]{1,0:T(8,128)(2,1)}, u32[]{:S(2)}, u32[]{:S(2)}) collective-permute-start(bf16[512,1024]{1,0:T(8,128)(2,1)S(1)} %get-tuple-element.43.refs_0_), channel_id=1, source_target_pairs={{0,3},{1,0},{2,1},{3,2},{4,7},{5,4},{6,5},{7,6},{8,11},{9,8},{10,9... | collective-permute-start | bytes 3145736 | tf_op jit(solution)/shard_map/weights/ppermute | solution.py:41
  42.2 2.7 %collective-permute-start.15 = (bf16[512,1024]{1,0:T(8,128)(2,1)S(1)}, bf16[512,1024]{1,0:T(8,128)(2,1)}, u32[]{:S(2)}, u32[]{:S(2)}) collective-permute-start(bf16[512,1024]{1,0:T(8,128)(2,1)S(1)} %get-tuple-element.46.refs_3_), channel_id=1, source_target_pairs={{0,64},{64,4},{4,68},{68,0},{1,65},{65,5},{5,69},{69,1},{2,66},{66... | collective-permute-start | bytes 3145736 | tf_op jit(solution)/shard_map/weights/ppermute | solution.py:41
  45.9 3.2 %copy-done = bf16[3840,1024]{1,0:T(8,128)(2,1)S(1)} copy-done((bf16[3840,1024]{1,0:T(8,128)(2,1)S(1)}, bf16[3840,1024]{1,0:T(8,128)(2,1)}, u32[]{:S(2)}) %copy-start) | copy-done | bytes 7864344
  49.1 20.9 %prepare.1 = (bf16[6144,1024]{1,0:T(8,128)(2,1)}, s32[6144,128]{1,0:T(8,128)S(1)}, s32[64]{0:T(128)S(1)}, f32[768,1024]{1,0:T(8,128)S(1)}) custom-call(s32[2]{0:T(128)S(1)} %pad_add_fusion.1.place, s32[256,128]{1,0:T(8,128)S(1)} %pad_add_fusion.ids, bf16[144,1024]{1,0:T(8,128)(2,1)S(1)} %get-tuple-element.34.l0.refs_4_, ...), custom_call_target="tpu_custom_call" | custom-call | flops 1073741824 | bytes 1048576 | tf_op jit(solution)/shard_map/prepare/pallas_call | solution.py:274
  70.1 1.6 copy-done.1
  71.8 2.1 %collective-permute-start.18 = (bf16[512,1024]{1,0:T(8,128)(2,1)S(1)}, bf16[512,1024]{1,0:T(8,128)(2,1)S(1)}, u32[]{:S(2)}, u32[]{:S(2)}) collective-permute-start(bf16[512,1024]{1,0:T(8,128)(2,1)S(1)} %get-tuple-element.46.refs_3_), channel_id=1, source_target_pairs={{0,4},{64,68},{4,0},{68,64},{1,5},{65,69},{5,1},{69,65},{2,6},{66,... | collective-permute-start | bytes 3145736 | tf_op jit(solution)/shard_map/forward/ppermute | solution.py:41
  74.0 14.3 %forward.2.hidden_all = bf16[6144,1536]{1,0:T(8,128)(2,1)} custom-call(s32[64]{0:T(128)S(1)} %get-tuple-element.35.bounds, bf16[6144,1024]{1,0:T(8,128)(2,1)} %get-tuple-element.40.x_all, bf16[512,1024]{1,0:T(8,128)(2,1)S(1)} %get-tuple-element.43.refs_0_, bf16[512,1024]{1,0:T(8,128)(2,1)} %collective-permute-done.13.refs_1_, ...), custom_call_target="tpu_custom_call" | custom-call | flops 12884901888 | bytes 16777216 | tf_op jit(solution)/shard_map/forward/pallas_call | solution.py:437
  88.2 7.0 %collective-permute-done.17.refs_6_ = bf16[512,1024]{1,0:T(8,128)(2,1)S(1)} collective-permute-done((bf16[512,1024]{1,0:T(8,128)(2,1)S(1)}, bf16[512,1024]{1,0:T(8,128)(2,1)S(1)}, u32[]{:S(2)}, u32[]{:S(2)}) %collective-permute-start.17) | collective-permute-done | bytes 1048608 | tf_op jit(solution)/shard_map/forward/ppermute | solution.py:41
  95.3 19.3 %forward.3 = (f32[768,1024]{1,0:T(8,128)S(1)}, f32[768,1024]{1,0:T(8,128)S(1)}) custom-call(s32[64]{0:T(128)S(1)} %get-tuple-element.35.bounds, bf16[6144,1024]{1,0:T(8,128)(2,1)} %get-tuple-element.40.x_all, s32[6144,128]{1,0:T(8,128)S(1)} %get-tuple-element.41.docs_all, f32[768,1024]{1,0:T(8,128)} %copy-done.1, bf16[6144,1536]{1,0:T(8,128)(2,1)} %forward.2.hidden_all, ...), custom_call_target="tpu_custom_call" | custom-call | flops 17179869184 | bytes 25165824 | tf_op jit(solution)/shard_map/forward/pallas_call | solution.py:462
  114.7 5.6 %collective-permute-done.19 = f32[768,1024]{1,0:T(8,128)S(1)} collective-permute-done((f32[768,1024]{1,0:T(8,128)S(1)}, f32[768,1024]{1,0:T(8,128)S(1)}, u32[]{:S(2)}, u32[]{:S(2)}) %collective-permute-start.19) | collective-permute-done | bytes 3145760 | tf_op jit(solution)/shard_map/pooled/ppermute | solution.py:41
  120.4 1.7 add_convert_fusion
  122.1 5.8 %all-to-all-start = ((bf16[8,96,1024]{2,1,0:T(8,128)(2,1)}), bf16[8,96,1024]{2,1,0:T(8,128)(2,1)S(1)}, u32[]{:S(2)}, u32[]{:S(2)}) async-start(bf16[8,96,1024]{2,1,0:T(8,128)(2,1)} %bitcast.4), calls=%async_computation | async-start | bytes 3145728 | tf_op jit(solution)/shard_map/pooled/all_to_all | solution.py:532
  128.2 20.8 %all-to-all-done = bf16[8,96,1024]{2,1,0:T(8,128)(2,1)S(1)} async-done(((bf16[8,96,1024]{2,1,0:T(8,128)(2,1)}), bf16[8,96,1024]{2,1,0:T(8,128)(2,1)S(1)}, u32[]{:S(2)}, u32[]{:S(2)}) %all-to-all-start) | async-done | bytes 1572896 | tf_op jit(solution)/shard_map/pooled/all_to_all | solution.py:532
  150.5 20.7 %all_to_all.16 = bf16[64,4,1024]{2,1,0:T(4,128)(2,1)S(1)} all-to-all(bf16[64,4,1024]{2,1,0:T(4,128)(2,1)S(1)} %select_convert_fusion), channel_id=1, replica_groups=mesh['x_lo'=2,'z'=4,'core'=2,'x_hi'=2,'y'=4] {'x_lo','z','x_hi','y'}, dimensions={0} | all-to-all | bytes 1048576 | tf_op jit(solution)/shard_map/match/all_to_all | solution.py:552
  171.6 1.6 collective-permute-done.20
  174.8 14.6 %all_to_all.17 = f32[64,1,4]{2,1,0:T(1,128)S(1)} all-to-all(f32[64,1,4]{2,1,0:T(1,128)S(1)} %bitcast.12), channel_id=1, replica_groups=mesh['x_lo'=2,'z'=4,'core'=2,'x_hi'=2,'y'=4] {'x_lo','z','x_hi','y'}, dimensions={0} | all-to-all | bytes 2048 | tf_op jit(solution)/shard_map/match/all_to_all | solution.py:563
  (68 shorter events, 10.5 us)
Async XLA Ops:
  0.0 45.8 %copy-start.2 = (bf16[16,1024]{1,0:T(8,128)(2,1)S(1)}, bf16[16,1024]{1,0:T(8,128)(2,1)}, u32[]{:S(2)}) copy-start(bf16[16,1024]{1,0:T(8,128)(2,1)} %param.11) | copy-start | bytes 98308
  1.7 9.0 %collective-permute-start.3 = (bf16[16,128]{1,0:T(8,128)(2,1)S(1)}, bf16[16,128]{1,0:T(8,128)(2,1)S(1)}, u32[]{:S(2)}, u32[]{:S(2)}) collective-permute-start(bf16[16,128]{1,0:T(8,128)(2,1)S(1)} %pad.17), channel_id=1, source_target_pairs={{0,4},{4,0},{1,5},{5,1},{2,6},{6,2},{3,7},{7,3},{8,12},{12,8},{9,1... | collective-permute-start | bytes 12296 | tf_op jit(solution)/shard_map/weights/ppermute | solution.py:497
  4.9 7.8 %collective-permute-start.4 = (bf16[16,128]{1,0:T(8,128)(2,1)S(1)}, bf16[16,128]{1,0:T(8,128)(2,1)S(1)}, u32[]{:S(2)}, u32[]{:S(2)}) collective-permute-start(bf16[16,128]{1,0:T(8,128)(2,1)S(1)} %pad.17), channel_id=1, source_target_pairs={{0,8},{8,0},{1,9},{9,1},{2,10},{10,2},{3,11},{11,3},{4,12},{12,4},... | collective-permute-start | bytes 12296 | tf_op jit(solution)/shard_map/weights/ppermute | solution.py:41
  4.9 7.9 %collective-permute-start.5 = (bf16[16,128]{1,0:T(8,128)(2,1)S(1)}, bf16[16,128]{1,0:T(8,128)(2,1)S(1)}, u32[]{:S(2)}, u32[]{:S(2)}) collective-permute-start(bf16[16,128]{1,0:T(8,128)(2,1)S(1)} %pad.17), channel_id=1, source_target_pairs={{0,12},{4,8},{8,4},{12,0},{1,13},{5,9},{9,5},{13,1},{2,14},{6,10},... | collective-permute-start | bytes 12296 | tf_op jit(solution)/shard_map/weights/ppermute | solution.py:498
  5.4 8.6 %collective-permute-start = (bf16[64,1024]{1,0:T(8,128)(2,1)S(1)}, bf16[64,1024]{1,0:T(8,128)(2,1)S(1)}, u32[]{:S(2)}, u32[]{:S(2)}) collective-permute-start(bf16[64,1024]{1,0:T(8,128)(2,1)S(1)} %pad_maximum_fusion.refs_0_.refs_4_), channel_id=1, source_target_pairs={{0,16},{16,32},{32,48},{48,0},{1,17},{17,33},{33,49},{49,1},{2,18}... | collective-permute-start | bytes 393224 | tf_op jit(solution)/shard_map/weights/ppermute | solution.py:41
  7.4 6.6 %collective-permute-start.1 = (bf16[64,1024]{1,0:T(8,128)(2,1)S(1)}, bf16[64,1024]{1,0:T(8,128)(2,1)S(1)}, u32[]{:S(2)}, u32[]{:S(2)}) collective-permute-start(bf16[64,1024]{1,0:T(8,128)(2,1)S(1)} %pad_maximum_fusion.refs_0_.refs_4_), channel_id=1, source_target_pairs={{0,48},{16,0},{32,16},{48,32},{1,49},{17,1},{33,17},{49,33},{2,50}... | collective-permute-start | bytes 393224 | tf_op jit(solution)/shard_map/weights/ppermute | solution.py:41
  10.7 6.7 %collective-permute-start.2 = (bf16[64,1024]{1,0:T(8,128)(2,1)S(1)}, bf16[64,1024]{1,0:T(8,128)(2,1)S(1)}, u32[]{:S(2)}, u32[]{:S(2)}) collective-permute-start(bf16[64,1024]{1,0:T(8,128)(2,1)S(1)} %pad_maximum_fusion.refs_0_.refs_4_), channel_id=1, source_target_pairs={{0,32},{16,48},{32,0},{48,16},{1,33},{17,49},{33,1},{49,17},{2,34}... | collective-permute-start | bytes 393224 | tf_op jit(solution)/shard_map/weights/ppermute | solution.py:41
  12.7 1.3 collective-permute-start.6
  18.3 8.5 %collective-permute-start.10 = (bf16[128,1024]{1,0:T(8,128)(2,1)S(1)}, bf16[128,1024]{1,0:T(8,128)(2,1)S(1)}, u32[]{:S(2)}, u32[]{:S(2)}) collective-permute-start(bf16[128,1024]{1,0:T(8,128)(2,1)S(1)} %get-tuple-element.36.refs_0_), channel_id=1, source_target_pairs={{0,64},{64,4},{4,68},{68,0},{1,65},{65,5},{5,69},{69,1},{2,66},{66... | collective-permute-start | bytes 786440 | tf_op jit(solution)/shard_map/weights/ppermute | solution.py:41
  19.9 16.1 %collective-permute-start.7 = (bf16[144,1024]{1,0:T(8,128)(2,1)S(1)}, bf16[144,1024]{1,0:T(8,128)(2,1)S(1)}, u32[]{:S(2)}, u32[]{:S(2)}) collective-permute-start(bf16[144,1024]{1,0:T(8,128)(2,1)S(1)} %get-tuple-element.34.l0.refs_4_), channel_id=1, source_target_pairs={{0,1},{1,2},{2,3},{3,0},{4,5},{5,6},{6,7},{7,4},{8,9},{9,10},{10,1... | collective-permute-start | bytes 884744 | tf_op jit(solution)/shard_map/weights/ppermute | solution.py:41
  21.4 14.5 %collective-permute-start.8 = (bf16[144,1024]{1,0:T(8,128)(2,1)S(1)}, bf16[144,1024]{1,0:T(8,128)(2,1)S(1)}, u32[]{:S(2)}, u32[]{:S(2)}) collective-permute-start(bf16[144,1024]{1,0:T(8,128)(2,1)S(1)} %get-tuple-element.34.l0.refs_4_), channel_id=1, source_target_pairs={{0,3},{1,0},{2,1},{3,2},{4,7},{5,4},{6,5},{7,6},{8,11},{9,8},{10,9... | collective-permute-start | bytes 884744 | tf_op jit(solution)/shard_map/weights/ppermute | solution.py:41
  23.1 13.0 %collective-permute-start.9 = (bf16[144,1024]{1,0:T(8,128)(2,1)S(1)}, bf16[144,1024]{1,0:T(8,128)(2,1)S(1)}, u32[]{:S(2)}, u32[]{:S(2)}) collective-permute-start(bf16[144,1024]{1,0:T(8,128)(2,1)S(1)} %get-tuple-element.34.l0.refs_4_), channel_id=1, source_target_pairs={{0,2},{1,3},{2,0},{3,1},{4,6},{5,7},{6,4},{7,5},{8,10},{9,11},{10,... | collective-permute-start | bytes 884744 | tf_op jit(solution)/shard_map/weights/ppermute | solution.py:41
  25.1 10.8 %collective-permute-start.11 = (bf16[128,1024]{1,0:T(8,128)(2,1)S(1)}, bf16[128,1024]{1,0:T(8,128)(2,1)S(1)}, u32[]{:S(2)}, u32[]{:S(2)}) collective-permute-start(bf16[128,1024]{1,0:T(8,128)(2,1)S(1)} %get-tuple-element.36.refs_0_), channel_id=1, source_target_pairs={{0,68},{64,0},{4,64},{68,4},{1,69},{65,1},{5,65},{69,5},{2,70},{66... | collective-permute-start | bytes 786440 | tf_op jit(solution)/shard_map/weights/ppermute | solution.py:41
  26.8 9.1 %collective-permute-start.12 = (bf16[128,1024]{1,0:T(8,128)(2,1)S(1)}, bf16[128,1024]{1,0:T(8,128)(2,1)S(1)}, u32[]{:S(2)}, u32[]{:S(2)}) collective-permute-start(bf16[128,1024]{1,0:T(8,128)(2,1)S(1)} %get-tuple-element.36.refs_0_), channel_id=1, source_target_pairs={{0,4},{64,68},{4,0},{68,64},{1,5},{65,69},{5,1},{69,65},{2,6},{66,... | collective-permute-start | bytes 786440 | tf_op jit(solution)/shard_map/weights/ppermute | solution.py:41
  38.9 32.8 %collective-permute-start.13 = (bf16[512,1024]{1,0:T(8,128)(2,1)S(1)}, bf16[512,1024]{1,0:T(8,128)(2,1)}, u32[]{:S(2)}, u32[]{:S(2)}) collective-permute-start(bf16[512,1024]{1,0:T(8,128)(2,1)S(1)} %get-tuple-element.43.refs_0_), channel_id=1, source_target_pairs={{0,1},{1,2},{2,3},{3,0},{4,5},{5,6},{6,7},{7,4},{8,9},{9,10},{10,1... | collective-permute-start | bytes 3145736 | tf_op jit(solution)/shard_map/weights/ppermute | solution.py:41
  40.1 31.6 %collective-permute-start.14 = (bf16[512,1024]{1,0:T(8,128)(2,1)S(1)}, bf16[512,1024]{1,0:T(8,128)(2,1)}, u32[]{:S(2)}, u32[]{:S(2)}) collective-permute-start(bf16[512,1024]{1,0:T(8,128)(2,1)S(1)} %get-tuple-element.43.refs_0_), channel_id=1, source_target_pairs={{0,3},{1,0},{2,1},{3,2},{4,7},{5,4},{6,5},{7,6},{8,11},{9,8},{10,9... | collective-permute-start | bytes 3145736 | tf_op jit(solution)/shard_map/weights/ppermute | solution.py:41
  42.2 29.5 %collective-permute-start.15 = (bf16[512,1024]{1,0:T(8,128)(2,1)S(1)}, bf16[512,1024]{1,0:T(8,128)(2,1)}, u32[]{:S(2)}, u32[]{:S(2)}) collective-permute-start(bf16[512,1024]{1,0:T(8,128)(2,1)S(1)} %get-tuple-element.46.refs_3_), channel_id=1, source_target_pairs={{0,64},{64,4},{4,68},{68,0},{1,65},{65,5},{5,69},{69,1},{2,66},{66... | collective-permute-start | bytes 3145736 | tf_op jit(solution)/shard_map/weights/ppermute | solution.py:41
  44.9 26.8 %collective-permute-start.16 = (bf16[512,1024]{1,0:T(8,128)(2,1)S(1)}, bf16[512,1024]{1,0:T(8,128)(2,1)}, u32[]{:S(2)}, u32[]{:S(2)}) collective-permute-start(bf16[512,1024]{1,0:T(8,128)(2,1)S(1)} %get-tuple-element.46.refs_3_), channel_id=1, source_target_pairs={{0,68},{64,0},{4,64},{68,4},{1,69},{65,1},{5,65},{69,5},{2,70},{66... | collective-permute-start | bytes 3145736 | tf_op jit(solution)/shard_map/weights/ppermute | solution.py:41
  45.9 3.2 %copy-start = (bf16[3840,1024]{1,0:T(8,128)(2,1)S(1)}, bf16[3840,1024]{1,0:T(8,128)(2,1)}, u32[]{:S(2)}) copy-start(bf16[3840,1024]{1,0:T(8,128)(2,1)} %table.1) | copy-start | bytes 23592964
  70.1 1.6 copy-start.1
  71.7 23.5 %collective-permute-start.17 = (bf16[512,1024]{1,0:T(8,128)(2,1)S(1)}, bf16[512,1024]{1,0:T(8,128)(2,1)S(1)}, u32[]{:S(2)}, u32[]{:S(2)}) collective-permute-start(bf16[512,1024]{1,0:T(8,128)(2,1)S(1)} %get-tuple-element.43.refs_0_), channel_id=1, source_target_pairs={{0,2},{1,3},{2,0},{3,1},{4,6},{5,7},{6,4},{7,5},{8,10},{9,11},{10,... | collective-permute-start | bytes 3145736 | tf_op jit(solution)/shard_map/forward/ppermute | solution.py:41
  71.8 23.5 %collective-permute-start.18 = (bf16[512,1024]{1,0:T(8,128)(2,1)S(1)}, bf16[512,1024]{1,0:T(8,128)(2,1)S(1)}, u32[]{:S(2)}, u32[]{:S(2)}) collective-permute-start(bf16[512,1024]{1,0:T(8,128)(2,1)S(1)} %get-tuple-element.46.refs_3_), channel_id=1, source_target_pairs={{0,4},{64,68},{4,0},{68,64},{1,5},{65,69},{5,1},{69,65},{2,6},{66,... | collective-permute-start | bytes 3145736 | tf_op jit(solution)/shard_map/forward/ppermute | solution.py:41
  114.6 5.7 %collective-permute-start.19 = (f32[768,1024]{1,0:T(8,128)S(1)}, f32[768,1024]{1,0:T(8,128)S(1)}, u32[]{:S(2)}, u32[]{:S(2)}) collective-permute-start(f32[768,1024]{1,0:T(8,128)S(1)} %get-tuple-element.50), channel_id=1, source_target_pairs={{0,8},{8,0},{1,9},{9,1},{2,10},{10,2},{3,11},{11,3},{4,12},{12,4},... | collective-permute-start | bytes 9437192 | tf_op jit(solution)/shard_map/pooled/ppermute | solution.py:41
  122.1 5.8 %copy-start.3 = (s32[96,1]{0,1:T(1,128)S(1)}, s32[96,1]{0,1:T(1,128)}, u32[]{:S(2)}) copy-start(s32[96,1]{0,1:T(1,128)} %param.9) | copy-start | bytes 1156
  122.1 26.9 %all-to-all-start = ((bf16[8,96,1024]{2,1,0:T(8,128)(2,1)}), bf16[8,96,1024]{2,1,0:T(8,128)(2,1)S(1)}, u32[]{:S(2)}, u32[]{:S(2)}) async-start(bf16[8,96,1024]{2,1,0:T(8,128)(2,1)} %bitcast.4), calls=%async_computation | async-start | bytes 3145728 | tf_op jit(solution)/shard_map/pooled/all_to_all | solution.py:532
  171.2 1.9 collective-permute-start.20

commit v5 on v4

--- a/solution.py
+++ b/solution.py
@@ -89,7 +89,7 @@
 
 
 def half_gelu(half):
-    square = jnp.minimum(half * half, LIMIT / 4)
+    square = half * half
     total = jnp.full_like(square, ERF_Q[-1] * 4.0 ** (len(ERF_Q) - 1) * 2)
     for power in range(len(ERF_Q) - 2, -1, -1):
         total = total * square + ERF_Q[power] * 4.0**power * 2
@@ -154,18 +154,14 @@
     return keys, jnp.sum(ones.astype(jnp.float32), axis=0, keepdims=True)
 
 
-def prepare(place, ids, l0, l1, l2, l3, table, positions, x_out, docs_out, bounds, normed_out, *scratch):
-    total, rows32, table32, lengths, list_buffer, listed, sem, length_sems = scratch
+def prepare(place, own_ids, other_ids, own_lengths, other_lengths, table_all, positions, x_out, docs_out, bounds, normed_out, *scratch):
+    total, rows32, table32, table, list_buffer, listed, sem, table_sem = scratch
     width = table.shape[1]
     pieces = width // LANES
+    table_copy = pltpu.make_async_copy(table_all, table, table_sem)
+    table_copy.start()
 
     def load():
-        copies = [
-            pltpu.make_async_copy(piece.at[pl.ds(piece.shape[0] - 16, 16), :], lengths.at[number], length_sems.at[number])
-            for number, piece in enumerate((l0, l1, l2, l3))
-        ]
-        for copy in copies:
-            copy.start()
         total[...] = jnp.zeros_like(total)
 
         def widen(group, carry):
@@ -176,26 +172,26 @@
                     table32[pl.ds(at, 8), :] = values[eight * 8 : eight * 8 + 8, piece * LANES : (piece + 1) * LANES]
             return carry
 
-        lax.fori_loop(0, table.shape[0] // 16, widen, 0)
-        for copy in copies:
-            copy.wait()
         row, lane = (lax.broadcasted_iota(jnp.int32, (LANES, LANES), axis) for axis in range(2))
         of_doc = (row == lane >> SEQ_BITS).astype(jnp.bfloat16)
         used = []
-        for part in range(4):
-            columns = slice(part * LANES, (part + 1) * LANES)
-            around = [
-                jnp.dot(lengths[number, :, columns], of_doc, preferred_element_type=jnp.float32) for number in range(4)
-            ]
-            for y in range(4):
-                away = (y - place[1]) & 3
-                value = around[0]
-                for by, number in ((3, 1), (1, 2), (2, 3)):
-                    value = jnp.where(away == by, around[number], value)
-                used.append(value)
+        for lengths in (own_lengths, other_lengths):
+            for half in range(2):
+                columns = slice(half * LANES, (half + 1) * LANES)
+                around = [
+                    jnp.dot(lengths[16 * number : 16 * number + 16, columns], of_doc, preferred_element_type=jnp.float32)
+                    for number in range(4)
+                ]
+                for y in range(4):
+                    away = (y - place[1]) & 3
+                    value = around[0]
+                    for by, number in ((3, 1), (1, 2), (2, 3)):
+                        value = jnp.where(away == by, around[number], value)
+                    used.append(value)
         used = jnp.concatenate(used, axis=0).astype(jnp.int32)
+        ids = jnp.concatenate([own_ids[...], other_ids[...]], axis=0)
         row, lane = (lax.broadcasted_iota(jnp.int32, ids.shape, axis) for axis in range(2))
-        own_row = ids[...] - place[0]
+        own_row = ids - place[0]
         doc = (row >> 4) * (12 * 8) + (row & 15) * 8 + (lane >> SEQ_BITS)
         time = lane & (SEQ - 1)
         keys = (doc << 19) + (time << 15) + (own_row >> 3) * 64 + (own_row & 7)
@@ -207,6 +203,8 @@
         list_buffer[pl.ds(most, 8), :] = jnp.broadcast_to(count, (8, LANES))
         copy = pltpu.make_async_copy(list_buffer, listed, sem)
         copy.start()
+        table_copy.wait()
+        lax.fori_loop(0, table.shape[0] // 16, widen, 0)
         copy.wait()
         return listed[most, 0]
 
@@ -222,17 +220,19 @@
         def key_at(slot):
             return listed[slot >> 7, slot & (LANES - 1)]
 
-        def take(group, carry):
-            for one in range(8):
-                key = listed[2 * index + (group >> 4), (group & 15) * 8 + one]
-                at = key & 0x7FFF
-                when = pl.multiple_of((key >> 12) & 0x78, 8)
-                value = table32[pl.ds(at, pieces, stride=8), :] + positions[pl.ds(when, pieces), :]
-                rows32[pl.ds(group * 8 * pieces + one, pieces, stride=8), :] = value
-                docs_ref[pl.ds(group * 8 + one, 1), :] = jnp.full((1, LANES), key >> 19, jnp.int32)
-            return carry
-
-        lax.fori_loop(0, TILE // 8, take, 0)
+        for half in range(TILE // LANES):
+
+            def take(group, carry, half=half):
+                for one in range(8):
+                    key = listed[TILE // LANES * index + half, group * 8 + one]
+                    at = key & 0x7FFF
+                    when = pl.multiple_of((key >> 12) & 0x78, 8)
+                    value = table32[pl.ds(at, pieces, stride=8), :] + positions[pl.ds(when, pieces), :]
+                    rows32[pl.ds((half * 16 + group) * 8 * pieces + one, pieces, stride=8), :] = value
+                    docs_ref[pl.ds((half * 16 + group) * 8 + one, 1), :] = jnp.full((1, LANES), key >> 19, jnp.int32)
+                return carry
+
+            lax.fori_loop(0, LANES // 8, take, 0, unroll=True)
         normed = []
         for sub in range(TILE // SUB):
             block = rows32[pl.ds(sub * SUB * pieces, SUB * pieces), :].reshape(SUB // 8, pieces, 8, LANES)
@@ -266,14 +266,14 @@
     copy.wait()
 
 
-def run_prepare(place, ids, lengths, embed_table, positions, group, most):
+def run_prepare(place, ids, other_ids, lengths, other_lengths, embed_table, positions, group, most):
     seq, width = positions.shape
     vocab_rows = embed_table.shape[0]
     pieces = width // LANES
     smem, vmem, hbm = (pl.BlockSpec(memory_space=space) for space in (pltpu.SMEM, pltpu.VMEM, pltpu.HBM))
     return pl.pallas_call(
         prepare,
-        in_specs=[smem, vmem] + [pl.BlockSpec(memory_space=pl.ANY)] * 4 + [vmem, vmem],
+        in_specs=[smem] + [vmem] * 4 + [hbm, vmem],
         out_specs=[hbm, hbm, smem, hbm],
         out_shape=[
             jax.ShapeDtypeStruct((most, width), jnp.bfloat16),
@@ -285,15 +285,15 @@
             pltpu.VMEM((group + WINDOW, width), jnp.float32),
             pltpu.VMEM((TILE * pieces, LANES), jnp.float32),
             pltpu.VMEM((vocab_rows * pieces, LANES), jnp.float32),
-            pltpu.VMEM((4, 16, width), jnp.bfloat16),
+            pltpu.VMEM((vocab_rows, width), jnp.bfloat16),
             pltpu.VMEM((most // LANES + 8, LANES), jnp.int32),
             pltpu.SMEM((most // LANES + 8, LANES), jnp.int32),
             pltpu.SemaphoreType.DMA,
-            pltpu.SemaphoreType.DMA((4,)),
+            pltpu.SemaphoreType.DMA,
         ],
-        compiler_params=pltpu.CompilerParams(vmem_limit_bytes=36 << 20),
+        compiler_params=pltpu.CompilerParams(vmem_limit_bytes=52 << 20),
         cost_estimate=pl.CostEstimate(flops=1 << 30, bytes_accessed=1 << 20, transcendentals=0),
-    )(place, ids, *lengths, embed_table, positions.astype(jnp.float32).reshape(seq * pieces, LANES))
+    )(place, ids, other_ids, lengths, other_lengths, embed_table, positions.astype(jnp.float32).reshape(seq * pieces, LANES))
 
 
 def over_tiles(tiles, several):
@@ -351,22 +351,29 @@
             hidden[rows, columns] = half_gelu(staged[(number - 1) % 2, rows, :]).astype(jnp.bfloat16)
 
 
-def first_units(near, bounds, x_all, *refs):
-    pieces, (out, x, w_in, hidden, staged, w_sems, x_sems, out_sems) = refs[:near], refs[near:]
-    tiles = bounds[BOUNDS - 1]
-    units = w_in.shape[0] // near
-    copies = [
-        pltpu.make_async_copy(piece.at[pl.ds(0, units), :], w_in.at[pl.ds(number * units, units), :], w_sems.at[number])
-        for number, piece in enumerate(pieces)
-    ]
+def load_units(pieces, w_in, w_out, sems):
+    units = pieces[0].shape[0] // 2
+    copies = []
+    for number, piece in enumerate(pieces):
+        for which, whole in enumerate((w_in, w_out)):
+            part = piece.at[pl.ds(which * units, units), :]
+            place = whole.at[pl.ds(number * units, units), :]
+            copies.append(pltpu.make_async_copy(part, place, sems.at[2 * number + which]))
     for copy in copies:
         copy.start()
+    return copies
+
+
+def first_units(near, bounds, x_all, *refs):
+    pieces, (out, x, w_in, w_out, hidden, staged, sums, w_sems, x_sems, out_sems) = refs[:near], refs[near:]
+    tiles = bounds[BOUNDS - 1]
+    copies = load_units(pieces, w_in, w_out, w_sems)
     ready = load_pairs(tiles, [(x_all, x, x_sems)])
     for copy in copies:
         copy.wait()
 
     def store(tile, slot):
-        return pltpu.make_async_copy(hidden.at[slot], out.at[rows_of(tile, 2), :], out_sems.at[slot])
+        return pltpu.make_async_copy(sums.at[slot], out.at[rows_of(tile, 2), :], out_sems.at[slot])
 
     def several(tile, count):
         slot = ready(tile)
@@ -375,7 +382,9 @@
         def _():
             store(tile - 4, slot).wait()
 
-        activate(x.at[slot, pl.ds(0, count * TILE), :], w_in, hidden.at[slot], 0, staged)
+        rows = pl.ds(0, count * TILE)
+        activate(x.at[slot, rows, :], w_in, hidden, 0, staged)
+        sums[slot, rows, :] = jnp.dot(hidden[rows, :], w_out[...], preferred_element_type=jnp.float32)
         store(tile, slot).start()
 
     over_tiles(tiles, several)
@@ -388,23 +397,15 @@
     store(last, (last >> 1) & 1).wait()
 
 
-def second_units(near, far, bounds, x_all, docs_all, normed, hidden_all, *refs):
-    pieces, refs = refs[: near + far], refs[near + far :]
-    own, other, total, x, docs, w_in, w_out, hidden, staged, w_sems, x_sems, docs_sems, hidden_sems, ends = refs
+def second_units(far, bounds, x_all, docs_all, normed, sums_all, *refs):
+    pieces, refs = refs[:far], refs[far:]
+    own, other, total, x, docs, w_in, w_out, hidden, staged, sums, w_sems, x_sems, docs_sems, sums_sems, ends = refs
     tiles = bounds[BOUNDS - 1]
     group = own.shape[0]
-    units = pieces[0].shape[0] // 2
-    parts = [(piece.at[pl.ds(units, units), :], w_out, number * units) for number, piece in enumerate(pieces)]
-    parts += [(piece.at[pl.ds(0, units), :], w_in, number * units) for number, piece in enumerate(pieces[near:])]
-    copies = [
-        pltpu.make_async_copy(part, whole.at[pl.ds(row, units), :], w_sems.at[number])
-        for number, (part, whole, row) in enumerate(parts)
-    ]
+    copies = load_units(pieces, w_in, w_out, w_sems)
     copies.append(pltpu.make_async_copy(normed, total.at[pl.ds(0, group), :], ends.at[0]))
-    for copy in copies:
-        copy.start()
-    known = hidden.at[:, :, pl.ds(0, near * units)]
-    ready = load_pairs(tiles, [(x_all, x, x_sems), (docs_all, docs, docs_sems), (hidden_all, known, hidden_sems)])
+    copies[-1].start()
+    ready = load_pairs(tiles, [(x_all, x, x_sems), (docs_all, docs, docs_sems), (sums_all, sums, sums_sems)])
     rest = total.shape[0] - group
     total[pl.ds(group, rest), :] = jnp.zeros((rest, total.shape[1]), jnp.float32)
     for copy in copies:
@@ -413,8 +414,8 @@
     def several(tile, count):
         slot = ready(tile)
         rows = pl.ds(0, count * TILE)
-        activate(x.at[slot, rows, :], w_in, hidden.at[slot], near * units, staged)
-        branch = jnp.dot(hidden[slot, rows, :], w_out[...], preferred_element_type=jnp.float32)
+        activate(x.at[slot, rows, :], w_in, hidden, 0, staged)
+        branch = sums[slot, rows, :] + jnp.dot(hidden[rows, :], w_out[...], preferred_element_type=jnp.float32)
         for one in range(count):
             part = slice(one * TILE, (one + 1) * TILE)
             pool(docs[slot, part, :], split(branch[part]), bounds[2 * (tile + one)], bounds[2 * (tile + one) + 1], total)
@@ -438,49 +439,51 @@
         functools.partial(first_units, len(near)),
         in_specs=[smem, hbm] + [anywhere] * len(near),
         out_specs=hbm,
-        out_shape=jax.ShapeDtypeStruct((most, units), jnp.bfloat16),
+        out_shape=jax.ShapeDtypeStruct((most, width), jnp.float32),
         scratch_shapes=[
             pltpu.VMEM((2, 2 * TILE, width), jnp.bfloat16),
             pltpu.VMEM((units, width), jnp.bfloat16),
-            pltpu.VMEM((2, 2 * TILE, units), jnp.bfloat16),
+            pltpu.VMEM((units, width), jnp.bfloat16),
+            pltpu.VMEM((2 * TILE, units), jnp.bfloat16),
             pltpu.VMEM((2, 2 * TILE, CHUNK), jnp.float32),
-            pltpu.SemaphoreType.DMA((len(near),)),
+            pltpu.VMEM((2, 2 * TILE, width), jnp.float32),
+            pltpu.SemaphoreType.DMA((2 * len(near),)),
             pltpu.SemaphoreType.DMA((2,)),
             pltpu.SemaphoreType.DMA((2,)),
         ],
         compiler_params=pltpu.CompilerParams(vmem_limit_bytes=44 << 20),
-        cost_estimate=pl.CostEstimate(flops=12 << 30, bytes_accessed=16 << 20, transcendentals=0),
+        cost_estimate=pl.CostEstimate(flops=20 << 30, bytes_accessed=16 << 20, transcendentals=0),
     )(bounds, x, *near)
 
 
-def run_second(near, far, bounds, x, docs, normed, hidden):
+def run_second(far, bounds, x, docs, normed, sums):
     most, width = x.shape
     group = normed.shape[0]
-    units = near[0].shape[0] // 2
-    count = len(near) + len(far)
+    units = len(far) * far[0].shape[0] // 2
     smem, hbm, anywhere = (pl.BlockSpec(memory_space=space) for space in (pltpu.SMEM, pltpu.HBM, pl.ANY))
     return pl.pallas_call(
-        functools.partial(second_units, len(near), len(far)),
-        in_specs=[smem, hbm, hbm, anywhere, hbm] + [anywhere] * count,
+        functools.partial(second_units, len(far)),
+        in_specs=[smem, hbm, hbm, anywhere, hbm] + [anywhere] * len(far),
         out_specs=[anywhere, anywhere],
         out_shape=[jax.ShapeDtypeStruct((group, width), jnp.float32)] * 2,
         scratch_shapes=[
             pltpu.VMEM((2 * group + WINDOW, width), jnp.float32),
             pltpu.VMEM((2, 2 * TILE, width), jnp.bfloat16),
             pltpu.VMEM((2, 2 * TILE, LANES), jnp.int32),
-            pltpu.VMEM((len(far) * units, width), jnp.bfloat16),
-            pltpu.VMEM((count * units, width), jnp.bfloat16),
-            pltpu.VMEM((2, 2 * TILE, count * units), jnp.bfloat16),
+            pltpu.VMEM((units, width), jnp.bfloat16),
+            pltpu.VMEM((units, width), jnp.bfloat16),
+            pltpu.VMEM((2 * TILE, units), jnp.bfloat16),
             pltpu.VMEM((2, 2 * TILE, CHUNK), jnp.float32),
-            pltpu.SemaphoreType.DMA((count + len(far),)),
+            pltpu.VMEM((2, 2 * TILE, width), jnp.float32),
+            pltpu.SemaphoreType.DMA((2 * len(far),)),
             pltpu.SemaphoreType.DMA((2,)),
             pltpu.SemaphoreType.DMA((2,)),
             pltpu.SemaphoreType.DMA((2,)),
             pltpu.SemaphoreType.DMA((2,)),
         ],
-        compiler_params=pltpu.CompilerParams(vmem_limit_bytes=34 << 20),
-        cost_estimate=pl.CostEstimate(flops=16 << 30, bytes_accessed=24 << 20, transcendentals=0),
-    )(bounds, x, docs, normed, hidden, *near, *far)
+        compiler_params=pltpu.CompilerParams(vmem_limit_bytes=36 << 20),
+        cost_estimate=pl.CostEstimate(flops=12 << 30, bytes_accessed=24 << 20, transcendentals=0),
+    )(bounds, x, docs, normed, sums, *far)
 
 
 def local(token_ids, doc_lengths, clusters, embed_table, positions, w_in, w_out):
@@ -492,24 +495,23 @@
     with jax.named_scope("weights"):
         half = w_in.shape[0] // 2
         mixed = jnp.concatenate([w_in[:half], w_out[:half], w_in[half:], w_out[half:]], axis=0)
-        mixed, token_ids, doc_lengths = lax.optimization_barrier((mixed, token_ids, doc_lengths))
+        mixed, doc_lengths = lax.optimization_barrier((mixed, doc_lengths))
+        by_z = ring(mixed, "z")
         lengths = jnp.pad(doc_lengths.reshape(doc_dev // 8, 8), ((0, 16 - doc_dev // 8), (0, LANES - 8))).astype(jnp.bfloat16)
         over = lax.ppermute(lengths, "x_hi", [(0, 1), (1, 0)])
-        cross = lax.ppermute(lengths, ("core", "x_hi"), [(0, 3), (1, 2), (2, 1), (3, 0)])
-        other = step(lengths, "core", 1)
         lower = lax.axis_index("x_hi") == 0
-        parts = [jnp.where(lower, a, b) for a, b in ((lengths, over), (over, lengths), (other, cross), (cross, other))]
-        lengths = jnp.pad(jnp.concatenate(parts, axis=1), ((0, 0), (0, width - 4 * LANES)))
-        by_z = ring(mixed, "z")
+        lengths = jnp.concatenate([jnp.where(lower, lengths, over), jnp.where(lower, over, lengths)], axis=1)
+        lengths = jnp.pad(lengths, ((0, 0), (0, width - 2 * LANES)))
         first, second = joined([by_z, by_z], [0, 2 * half], 2 * half, lengths)
         rows = first.shape[0]
+        place = jnp.stack([lax.axis_index(COL) * vocab_rows, lax.axis_index("y")]).astype(jnp.int32)
+        first, second = ring(first, X), ring(second, "y")
+        first, second, token_ids = lax.optimization_barrier((first, second, token_ids))
+        lengths = jnp.concatenate([piece[rows:, : 2 * LANES] for piece in second], axis=0)
+        lengths = (lengths, step(lengths, "core", 1))
         ids = token_ids.reshape(n_col, doc_dev * seq // LANES, LANES)
         ids = jnp.pad(ids, ((0, 0), (0, 16 - ids.shape[1]), (0, 0))).reshape(n_col * 16, LANES)
-        ids = jnp.concatenate([ids, step(ids, "core", 1)], axis=0)
-        place = jnp.stack([lax.axis_index(COL) * vocab_rows, lax.axis_index("y")]).astype(jnp.int32)
-        first, second, ids = lax.optimization_barrier((first, second, ids))
-        first, second = ring(first, X), ring(second, "y")
-        lengths = second
+        ids = (ids, step(ids, "core", 1))
         first, second = joined([first, second], [0, 0], rows)
         units = first.shape[0] // 2
         left, right = step(first, "y", 1), step(first, "y", -1)
@@ -518,13 +520,13 @@
 
     with jax.named_scope("prepare"):
         most = 2 * n_col * SHARD_CAP
-        x, docs, bounds, normed = run_prepare(place, ids, lengths, embed_table, positions, group, most)
+        x, docs, bounds, normed = run_prepare(place, *ids, *lengths, embed_table, positions, group, most)
 
     with jax.named_scope("forward"):
         near, x = lax.optimization_barrier((near, x))
         far = [step(near[0], "y", 2), step(near[3], X, 2)]
-        hidden = run_first(near, bounds, x)
-        own, other = run_second(near, far, bounds, x, docs, normed, hidden)
+        sums = run_first(near, bounds, x)
+        own, other = run_second(far, bounds, x, docs, normed, sums)
 
     with jax.named_scope("pooled"):
         sums = own + step(other, "core", 1)

time: 194 us -> 184 us (0.948); the launches traced: 191 us -> 184 us
  Pallas kernels: 58.2 us -> 49.9 us
  waiting for transfers between devices: 47.1 us -> 52.8 us
  local copies, waits for them, and re-layouts: 9.06 us -> 5.18 us
    pallas_call x2, Pallas kernels: 40.3 us -> 28.9 us  [the longest x1 16.9 us: run_prepare(): pl.pallas_call(prepare, in_specs=[smem] + [vmem] * 4 + [hbm, vmem], out_s...]
    ppermute x19, waiting for transfers between devices: 26.4 us -> 32.1 us  [step(): lax.ppermute(value, axis, [(place(i), place((i + by) % count)) for i in r...]
    unnamed x9 -> x11, local copies, waits for them, and re-layouts: 5.04 us -> 0.2 us
    pallas_call x1, Pallas kernels: 14.3 us -> 17.2 us  [run_first(): pl.pallas_call(functools.partial(first_units, len(near)), in_specs=[smem,...]
  transfers between devices with their start and end apart: 22 -> 21, of which waited for: 9 -> 10; matrix products, arithmetic and copies ran while one was open for 1% -> 2% of each run, Pallas kernels for 18% -> 19%
where the time goes in v5:
time: 184 us
  waiting for transfers between devices  52.8 us (29%)
  Pallas kernels  49.9 us (27%)
  starting transfers between devices  35.5 us (19%)
  blocking collectives  34.2 us (19%)
  local copies, waits for them, and re-layouts  5.18 us (3%)
  other arithmetic  5.17 us (3%)
    ppermute x19, waiting for transfers between devices, step(): lax.ppermute(value, axis, [(place(i), place((i + by) % count)) for i in r...  32.1 us
    ppermute x19, starting transfers between devices, step(): lax.ppermute(value, axis, [(place(i), place((i + by) % count)) for i in r...  26.1 us
    all_to_all x1, waiting for transfers between devices, local(): sums = lax.all_to_all(sums, COL, 0, 0, tiled=True)  20.8 us
    all_to_all x1, blocking collectives, local(): members = lax.all_to_all(outgoing, CHIPS, 0, 0, tiled=True)  19.6 us
    pallas_call x1, Pallas kernels, run_first(): pl.pallas_call(functools.partial(first_units, len(near)), in_specs=[smem,...  17.2 us
    pallas_call x1, Pallas kernels, run_prepare(): pl.pallas_call(prepare, in_specs=[smem] + [vmem] * 4 + [hbm, vmem], out_s...  16.9 us
    all_to_all x1, blocking collectives, local(): lax.all_to_all(best.reshape(n_clusters, 4), CHIPS, 0, 0, tiled=True)  14.6 us
    pallas_call x1, Pallas kernels, run_second(): pl.pallas_call(functools.partial(second_units, len(far)), in_specs=[smem,...  12 us
  transfers between devices with their start and end apart: 21, of which 10 were waited for; matrix products, arithmetic and copies ran while one was open for 2% of the time, Pallas kernels for 19%

profile of v5, /device:TPU:0, one launch (start us, length us, event | category | flops | bytes accessed | tf_op | source)
XLA Modules:
  0.0 184.0 jit_solution(17310723317608073523)
XLA Ops:
  1.7 3.2 %collective-permute-start.3 = (bf16[16,128]{1,0:T(8,128)(2,1)S(1)}, bf16[16,128]{1,0:T(8,128)(2,1)S(1)}, u32[]{:S(2)}, u32[]{:S(2)}) collective-permute-start(bf16[16,128]{1,0:T(8,128)(2,1)S(1)} %pad.17), channel_id=1, source_target_pairs={{0,4},{4,0},{1,5},{5,1},{2,6},{6,2},{3,7},{7,3},{8,12},{12,8},{9,1... | collective-permute-start | bytes 12296 | tf_op jit(solution)/shard_map/weights/ppermute | solution.py:501
  4.9 1.9 %collective-permute-start = (bf16[64,1024]{1,0:T(8,128)(2,1)S(1)}, bf16[64,1024]{1,0:T(8,128)(2,1)S(1)}, u32[]{:S(2)}, u32[]{:S(2)}) collective-permute-start(bf16[64,1024]{1,0:T(8,128)(2,1)S(1)} %pad_maximum_fusion.refs_0_.refs_4_), channel_id=1, source_target_pairs={{0,16},{16,32},{32,48},{48,0},{1,17},{17,33},{33,49},{49,1},{2,18}... | collective-permute-start | bytes 393224 | tf_op jit(solution)/shard_map/weights/ppermute | solution.py:41
  6.8 2.1 %collective-permute-start.1 = (bf16[64,1024]{1,0:T(8,128)(2,1)S(1)}, bf16[64,1024]{1,0:T(8,128)(2,1)S(1)}, u32[]{:S(2)}, u32[]{:S(2)}) collective-permute-start(bf16[64,1024]{1,0:T(8,128)(2,1)S(1)} %pad_maximum_fusion.refs_0_.refs_4_), channel_id=1, source_target_pairs={{0,48},{16,0},{32,16},{48,32},{1,49},{17,1},{33,17},{49,33},{2,50}... | collective-permute-start | bytes 393224 | tf_op jit(solution)/shard_map/weights/ppermute | solution.py:41
  8.9 1.9 %collective-permute-start.2 = (bf16[64,1024]{1,0:T(8,128)(2,1)S(1)}, bf16[64,1024]{1,0:T(8,128)(2,1)S(1)}, u32[]{:S(2)}, u32[]{:S(2)}) collective-permute-start(bf16[64,1024]{1,0:T(8,128)(2,1)S(1)} %pad_maximum_fusion.refs_0_.refs_4_), channel_id=1, source_target_pairs={{0,32},{16,48},{32,0},{48,16},{1,33},{17,49},{33,1},{49,17},{2,34}... | collective-permute-start | bytes 393224 | tf_op jit(solution)/shard_map/weights/ppermute | solution.py:41
  10.8 1.3 collective-permute-done.refs_1_.refs_5_
  12.1 2.1 %collective-permute-done.1.refs_2_.refs_6_ = bf16[64,1024]{1,0:T(8,128)(2,1)S(1)} collective-permute-done((bf16[64,1024]{1,0:T(8,128)(2,1)S(1)}, bf16[64,1024]{1,0:T(8,128)(2,1)S(1)}, u32[]{:S(2)}, u32[]{:S(2)}) %collective-permute-start.1) | collective-permute-done | bytes 131104 | tf_op jit(solution)/shard_map/weights/ppermute | solution.py:41
  14.3 1.9 %collective-permute-done.2.refs_3_.refs_7_ = bf16[64,1024]{1,0:T(8,128)(2,1)S(1)} collective-permute-done((bf16[64,1024]{1,0:T(8,128)(2,1)S(1)}, bf16[64,1024]{1,0:T(8,128)(2,1)S(1)}, u32[]{:S(2)}, u32[]{:S(2)}) %collective-permute-start.2) | collective-permute-done | bytes 131104 | tf_op jit(solution)/shard_map/weights/ppermute | solution.py:41
  16.1 0.9 weights.2
  17.7 1.6 collective-permute-start.7
  19.3 1.7 collective-permute-start.8
  20.9 2.0 %collective-permute-start.9 = (bf16[144,1024]{1,0:T(8,128)(2,1)S(1)}, bf16[144,1024]{1,0:T(8,128)(2,1)S(1)}, u32[]{:S(2)}, u32[]{:S(2)}) collective-permute-start(bf16[144,1024]{1,0:T(8,128)(2,1)S(1)} %get-tuple-element.38.refs_4_), channel_id=1, source_target_pairs={{0,2},{1,3},{2,0},{3,1},{4,6},{5,7},{6,4},{7,5},{8,10},{9,11},{10,... | collective-permute-start | bytes 884744 | tf_op jit(solution)/shard_map/weights/ppermute | solution.py:41
  22.9 2.6 %collective-permute-start.5 = (bf16[128,1024]{1,0:T(8,128)(2,1)S(1)}, bf16[128,1024]{1,0:T(8,128)(2,1)S(1)}, u32[]{:S(2)}, u32[]{:S(2)}) collective-permute-start(bf16[128,1024]{1,0:T(8,128)(2,1)S(1)} %get-tuple-element.43.refs_0_), channel_id=1, source_target_pairs={{0,68},{64,0},{4,64},{68,4},{1,69},{65,1},{5,65},{69,5},{2,70},{66... | collective-permute-start | bytes 786440 | tf_op jit(solution)/shard_map/weights/ppermute | solution.py:41
  25.5 9.2 %collective-permute-done.5.refs_2_ = bf16[128,1024]{1,0:T(8,128)(2,1)S(1)} collective-permute-done((bf16[128,1024]{1,0:T(8,128)(2,1)S(1)}, bf16[128,1024]{1,0:T(8,128)(2,1)S(1)}, u32[]{:S(2)}, u32[]{:S(2)}) %collective-permute-start.5) | collective-permute-done | bytes 262176 | tf_op jit(solution)/shard_map/weights/ppermute | solution.py:41
  34.8 2.9 %weights.3 = (bf16[512,1024]{1,0:T(8,128)(2,1)S(1)}, bf16[512,1024]{1,0:T(8,128)(2,1)S(1)}) custom-call(bf16[128,1024]{1,0:T(8,128)(2,1)S(1)} %get-tuple-element.43.refs_0_, bf16[128,1024]{1,0:T(8,128)(2,1)S(1)} %collective-permute-done.4.refs_1_, bf16[128,1024]{1,0:T(8,128)(2,1)S(1)} %collective-permute-done.5.refs_2_, ...), custom_call_target="tpu_custom_call" | custom-call | flops 1024 | bytes 1024 | tf_op jit(solution)/shard_map/weights/pallas_call | solution.py:62
  38.4 2.6 %collective-permute-start.13 = (bf16[512,1024]{1,0:T(8,128)(2,1)S(1)}, bf16[512,1024]{1,0:T(8,128)(2,1)}, u32[]{:S(2)}, u32[]{:S(2)}) collective-permute-start(bf16[512,1024]{1,0:T(8,128)(2,1)S(1)} %get-tuple-element.53.refs_0_), channel_id=1, source_target_pairs={{0,3},{1,0},{2,1},{3,2},{4,7},{5,4},{6,5},{7,6},{8,11},{9,8},{10,9... | collective-permute-start | bytes 3145736 | tf_op jit(solution)/shard_map/weights/ppermute | solution.py:41
  41.0 1.6 collective-permute-start.14
  42.6 2.1 %collective-permute-start.15 = (bf16[512,1024]{1,0:T(8,128)(2,1)S(1)}, bf16[512,1024]{1,0:T(8,128)(2,1)}, u32[]{:S(2)}, u32[]{:S(2)}) collective-permute-start(bf16[512,1024]{1,0:T(8,128)(2,1)S(1)} %get-tuple-element.56.refs_3_), channel_id=1, source_target_pairs={{0,68},{64,0},{4,64},{68,4},{1,69},{65,1},{5,65},{69,5},{2,70},{66... | collective-permute-start | bytes 3145736 | tf_op jit(solution)/shard_map/weights/ppermute | solution.py:41
  44.8 0.9 copy.18
  45.8 1.1 reshape.72
  48.4 16.9 %prepare.1 = (bf16[6144,1024]{1,0:T(8,128)(2,1)}, s32[6144,128]{1,0:T(8,128)}, s32[64]{0:T(128)S(1)}, f32[768,1024]{1,0:T(8,128)}) custom-call(s32[2]{0:T(128)S(1)} %pad_add_fusion.place, s32[128,128]{1,0:T(8,128)S(1)} %bitcast.11, s32[128,128]{1,0:T(8,128)S(1)} %collective-permute-done.10.other_ids, bf16[64,256]{1,0:T(8,128)(2,1)S(1)} %pad_maximum_fusion.1.own_lengths, ...), custom_call_target="tpu_custom_call" | custom-call | flops 1073741824 | bytes 1048576 | tf_op jit(solution)/shard_map/prepare/pallas_call | solution.py:274
  65.4 4.0 %collective-permute-start.16 = (bf16[512,1024]{1,0:T(8,128)(2,1)S(1)}, bf16[512,1024]{1,0:T(8,128)(2,1)S(1)}, u32[]{:S(2)}, u32[]{:S(2)}) collective-permute-start(bf16[512,1024]{1,0:T(8,128)(2,1)S(1)} %get-tuple-element.53.refs_0_), channel_id=1, source_target_pairs={{0,2},{1,3},{2,0},{3,1},{4,6},{5,7},{6,4},{7,5},{8,10},{9,11},{10,... | collective-permute-start | bytes 3145736 | tf_op jit(solution)/shard_map/forward/ppermute | solution.py:41
  69.4 17.2 %forward.2.sums_all = f32[6144,1024]{1,0:T(8,128)} custom-call(s32[64]{0:T(128)S(1)} %get-tuple-element.42.bounds, bf16[6144,1024]{1,0:T(8,128)(2,1)} %get-tuple-element.50.x_all, bf16[512,1024]{1,0:T(8,128)(2,1)S(1)} %get-tuple-element.53.refs_0_, bf16[512,1024]{1,0:T(8,128)(2,1)S(1)} %collective-permute-done.12.refs_1_, ...), custom_call_target="tpu_custom_call" | custom-call | flops 21474836480 | bytes 16777216 | tf_op jit(solution)/shard_map/forward/pallas_call | solution.py:438
  86.6 6.4 %collective-permute-done.16.refs_0_ = bf16[512,1024]{1,0:T(8,128)(2,1)S(1)} collective-permute-done((bf16[512,1024]{1,0:T(8,128)(2,1)S(1)}, bf16[512,1024]{1,0:T(8,128)(2,1)S(1)}, u32[]{:S(2)}, u32[]{:S(2)}) %collective-permute-start.16) | collective-permute-done | bytes 1048608 | tf_op jit(solution)/shard_map/forward/ppermute | solution.py:41
  93.0 3.0 %collective-permute-done.17.refs_1_ = bf16[512,1024]{1,0:T(8,128)(2,1)S(1)} collective-permute-done((bf16[512,1024]{1,0:T(8,128)(2,1)S(1)}, bf16[512,1024]{1,0:T(8,128)(2,1)S(1)}, u32[]{:S(2)}, u32[]{:S(2)}) %collective-permute-start.17) | collective-permute-done | bytes 1048608 | tf_op jit(solution)/shard_map/forward/ppermute | solution.py:41
  96.0 12.0 %forward.3 = (f32[768,1024]{1,0:T(8,128)S(1)}, f32[768,1024]{1,0:T(8,128)S(1)}) custom-call(s32[64]{0:T(128)S(1)} %get-tuple-element.42.bounds, bf16[6144,1024]{1,0:T(8,128)(2,1)} %get-tuple-element.50.x_all, s32[6144,128]{1,0:T(8,128)S(1)} %copy-done, f32[768,1024]{1,0:T(8,128)S(1)} %copy-done.1, f32[6144,1024]{1,0:T(8,128)} %forward.2.sums_all, ...), custom_call_target="tpu_custom_call" | custom-call | flops 12884901888 | bytes 25165824 | tf_op jit(solution)/shard_map/forward/pallas_call | solution.py:464
  108.1 5.6 %collective-permute-done.18 = f32[768,1024]{1,0:T(8,128)S(1)} collective-permute-done((f32[768,1024]{1,0:T(8,128)S(1)}, f32[768,1024]{1,0:T(8,128)S(1)}, u32[]{:S(2)}, u32[]{:S(2)}) %collective-permute-start.18) | collective-permute-done | bytes 3145760 | tf_op jit(solution)/shard_map/pooled/ppermute | solution.py:41
  113.7 1.7 add_convert_fusion
  115.4 6.2 %all-to-all-start = ((bf16[8,96,1024]{2,1,0:T(8,128)(2,1)}), bf16[8,96,1024]{2,1,0:T(8,128)(2,1)S(1)}, u32[]{:S(2)}, u32[]{:S(2)}) async-start(bf16[8,96,1024]{2,1,0:T(8,128)(2,1)} %bitcast.4), calls=%async_computation | async-start | bytes 3145728 | tf_op jit(solution)/shard_map/pooled/all_to_all | solution.py:534
  121.9 20.8 %all-to-all-done = bf16[8,96,1024]{2,1,0:T(8,128)(2,1)S(1)} async-done(((bf16[8,96,1024]{2,1,0:T(8,128)(2,1)}), bf16[8,96,1024]{2,1,0:T(8,128)(2,1)S(1)}, u32[]{:S(2)}, u32[]{:S(2)}) %all-to-all-start) | async-done | bytes 1572896 | tf_op jit(solution)/shard_map/pooled/all_to_all | solution.py:534
  144.2 19.6 %all_to_all.16 = bf16[64,4,1024]{2,1,0:T(4,128)(2,1)S(1)} all-to-all(bf16[64,4,1024]{2,1,0:T(4,128)(2,1)S(1)} %select_convert_fusion), channel_id=1, replica_groups=mesh['x_lo'=2,'z'=4,'core'=2,'x_hi'=2,'y'=4] {'x_lo','z','x_hi','y'}, dimensions={0} | all-to-all | bytes 1048576 | tf_op jit(solution)/shard_map/match/all_to_all | solution.py:554
  164.1 1.6 collective-permute-done.19
  167.4 14.6 %all_to_all.17 = f32[64,1,4]{2,1,0:T(1,128)S(1)} all-to-all(f32[64,1,4]{2,1,0:T(1,128)S(1)} %bitcast.12), channel_id=1, replica_groups=mesh['x_lo'=2,'z'=4,'core'=2,'x_hi'=2,'y'=4] {'x_lo','z','x_hi','y'}, dimensions={0} | all-to-all | bytes 2048 | tf_op jit(solution)/shard_map/match/all_to_all | solution.py:565
  (71 shorter events, 10.6 us)
Async XLA Ops:
  0.0 44.8 %copy-start.2 = (s32[768,16]{0,1:T(8,128)S(1)}, s32[768,16]{0,1:T(8,128)}, u32[]{:S(2)}) copy-start(s32[768,16]{0,1:T(8,128)} %param.7) | copy-start | bytes 147460
  0.0 44.8 %copy-start.3 = (bf16[16,1024]{1,0:T(8,128)(2,1)S(1)}, bf16[16,1024]{1,0:T(8,128)(2,1)}, u32[]{:S(2)}) copy-start(bf16[16,1024]{1,0:T(8,128)(2,1)} %param.11) | copy-start | bytes 98308
  1.7 9.1 %collective-permute-start.3 = (bf16[16,128]{1,0:T(8,128)(2,1)S(1)}, bf16[16,128]{1,0:T(8,128)(2,1)S(1)}, u32[]{:S(2)}, u32[]{:S(2)}) collective-permute-start(bf16[16,128]{1,0:T(8,128)(2,1)S(1)} %pad.17), channel_id=1, source_target_pairs={{0,4},{4,0},{1,5},{5,1},{2,6},{6,2},{3,7},{7,3},{8,12},{12,8},{9,1... | collective-permute-start | bytes 12296 | tf_op jit(solution)/shard_map/weights/ppermute | solution.py:501
  4.9 7.3 %collective-permute-start = (bf16[64,1024]{1,0:T(8,128)(2,1)S(1)}, bf16[64,1024]{1,0:T(8,128)(2,1)S(1)}, u32[]{:S(2)}, u32[]{:S(2)}) collective-permute-start(bf16[64,1024]{1,0:T(8,128)(2,1)S(1)} %pad_maximum_fusion.refs_0_.refs_4_), channel_id=1, source_target_pairs={{0,16},{16,32},{32,48},{48,0},{1,17},{17,33},{33,49},{49,1},{2,18}... | collective-permute-start | bytes 393224 | tf_op jit(solution)/shard_map/weights/ppermute | solution.py:41
  6.8 7.5 %collective-permute-start.1 = (bf16[64,1024]{1,0:T(8,128)(2,1)S(1)}, bf16[64,1024]{1,0:T(8,128)(2,1)S(1)}, u32[]{:S(2)}, u32[]{:S(2)}) collective-permute-start(bf16[64,1024]{1,0:T(8,128)(2,1)S(1)} %pad_maximum_fusion.refs_0_.refs_4_), channel_id=1, source_target_pairs={{0,48},{16,0},{32,16},{48,32},{1,49},{17,1},{33,17},{49,33},{2,50}... | collective-permute-start | bytes 393224 | tf_op jit(solution)/shard_map/weights/ppermute | solution.py:41
  8.9 7.2 %collective-permute-start.2 = (bf16[64,1024]{1,0:T(8,128)(2,1)S(1)}, bf16[64,1024]{1,0:T(8,128)(2,1)S(1)}, u32[]{:S(2)}, u32[]{:S(2)}) collective-permute-start(bf16[64,1024]{1,0:T(8,128)(2,1)S(1)} %pad_maximum_fusion.refs_0_.refs_4_), channel_id=1, source_target_pairs={{0,32},{16,48},{32,0},{48,16},{1,33},{17,49},{33,1},{49,17},{2,34}... | collective-permute-start | bytes 393224 | tf_op jit(solution)/shard_map/weights/ppermute | solution.py:41
  17.0 8.5 %collective-permute-start.4 = (bf16[128,1024]{1,0:T(8,128)(2,1)S(1)}, bf16[128,1024]{1,0:T(8,128)(2,1)S(1)}, u32[]{:S(2)}, u32[]{:S(2)}) collective-permute-start(bf16[128,1024]{1,0:T(8,128)(2,1)S(1)} %get-tuple-element.43.refs_0_), channel_id=1, source_target_pairs={{0,64},{64,4},{4,68},{68,0},{1,65},{65,5},{5,69},{69,1},{2,66},{66... | collective-permute-start | bytes 786440 | tf_op jit(solution)/shard_map/weights/ppermute | solution.py:41
  17.7 17.1 %collective-permute-start.7 = (bf16[144,1024]{1,0:T(8,128)(2,1)S(1)}, bf16[144,1024]{1,0:T(8,128)(2,1)S(1)}, u32[]{:S(2)}, u32[]{:S(2)}) collective-permute-start(bf16[144,1024]{1,0:T(8,128)(2,1)S(1)} %get-tuple-element.38.refs_4_), channel_id=1, source_target_pairs={{0,1},{1,2},{2,3},{3,0},{4,5},{5,6},{6,7},{7,4},{8,9},{9,10},{10,1... | collective-permute-start | bytes 884744 | tf_op jit(solution)/shard_map/weights/ppermute | solution.py:41
  19.3 15.6 %collective-permute-start.8 = (bf16[144,1024]{1,0:T(8,128)(2,1)S(1)}, bf16[144,1024]{1,0:T(8,128)(2,1)S(1)}, u32[]{:S(2)}, u32[]{:S(2)}) collective-permute-start(bf16[144,1024]{1,0:T(8,128)(2,1)S(1)} %get-tuple-element.38.refs_4_), channel_id=1, source_target_pairs={{0,3},{1,0},{2,1},{3,2},{4,7},{5,4},{6,5},{7,6},{8,11},{9,8},{10,9... | collective-permute-start | bytes 884744 | tf_op jit(solution)/shard_map/weights/ppermute | solution.py:41
  20.9 13.9 %collective-permute-start.9 = (bf16[144,1024]{1,0:T(8,128)(2,1)S(1)}, bf16[144,1024]{1,0:T(8,128)(2,1)S(1)}, u32[]{:S(2)}, u32[]{:S(2)}) collective-permute-start(bf16[144,1024]{1,0:T(8,128)(2,1)S(1)} %get-tuple-element.38.refs_4_), channel_id=1, source_target_pairs={{0,2},{1,3},{2,0},{3,1},{4,6},{5,7},{6,4},{7,5},{8,10},{9,11},{10,... | collective-permute-start | bytes 884744 | tf_op jit(solution)/shard_map/weights/ppermute | solution.py:41
  22.9 11.9 %collective-permute-start.5 = (bf16[128,1024]{1,0:T(8,128)(2,1)S(1)}, bf16[128,1024]{1,0:T(8,128)(2,1)S(1)}, u32[]{:S(2)}, u32[]{:S(2)}) collective-permute-start(bf16[128,1024]{1,0:T(8,128)(2,1)S(1)} %get-tuple-element.43.refs_0_), channel_id=1, source_target_pairs={{0,68},{64,0},{4,64},{68,4},{1,69},{65,1},{5,65},{69,5},{2,70},{66... | collective-permute-start | bytes 786440 | tf_op jit(solution)/shard_map/weights/ppermute | solution.py:41
  25.5 9.3 %collective-permute-start.6 = (bf16[128,1024]{1,0:T(8,128)(2,1)S(1)}, bf16[128,1024]{1,0:T(8,128)(2,1)S(1)}, u32[]{:S(2)}, u32[]{:S(2)}) collective-permute-start(bf16[128,1024]{1,0:T(8,128)(2,1)S(1)} %get-tuple-element.43.refs_0_), channel_id=1, source_target_pairs={{0,4},{64,68},{4,0},{68,64},{1,5},{65,69},{5,1},{69,65},{2,6},{66,... | collective-permute-start | bytes 786440 | tf_op jit(solution)/shard_map/weights/ppermute | solution.py:41
  37.7 27.6 %collective-permute-start.12 = (bf16[512,1024]{1,0:T(8,128)(2,1)S(1)}, bf16[512,1024]{1,0:T(8,128)(2,1)S(1)}, u32[]{:S(2)}, u32[]{:S(2)}) collective-permute-start(bf16[512,1024]{1,0:T(8,128)(2,1)S(1)} %get-tuple-element.53.refs_0_), channel_id=1, source_target_pairs={{0,1},{1,2},{2,3},{3,0},{4,5},{5,6},{6,7},{7,4},{8,9},{9,10},{10,1... | collective-permute-start | bytes 3145736 | tf_op jit(solution)/shard_map/weights/ppermute | solution.py:41
  38.4 26.9 %collective-permute-start.13 = (bf16[512,1024]{1,0:T(8,128)(2,1)S(1)}, bf16[512,1024]{1,0:T(8,128)(2,1)}, u32[]{:S(2)}, u32[]{:S(2)}) collective-permute-start(bf16[512,1024]{1,0:T(8,128)(2,1)S(1)} %get-tuple-element.53.refs_0_), channel_id=1, source_target_pairs={{0,3},{1,0},{2,1},{3,2},{4,7},{5,4},{6,5},{7,6},{8,11},{9,8},{10,9... | collective-permute-start | bytes 3145736 | tf_op jit(solution)/shard_map/weights/ppermute | solution.py:41
  41.0 24.4 %collective-permute-start.14 = (bf16[512,1024]{1,0:T(8,128)(2,1)S(1)}, bf16[512,1024]{1,0:T(8,128)(2,1)}, u32[]{:S(2)}, u32[]{:S(2)}) collective-permute-start(bf16[512,1024]{1,0:T(8,128)(2,1)S(1)} %get-tuple-element.56.refs_3_), channel_id=1, source_target_pairs={{0,64},{64,4},{4,68},{68,0},{1,65},{65,5},{5,69},{69,1},{2,66},{66... | collective-permute-start | bytes 3145736 | tf_op jit(solution)/shard_map/weights/ppermute | solution.py:41
  42.6 22.8 %collective-permute-start.15 = (bf16[512,1024]{1,0:T(8,128)(2,1)S(1)}, bf16[512,1024]{1,0:T(8,128)(2,1)}, u32[]{:S(2)}, u32[]{:S(2)}) collective-permute-start(bf16[512,1024]{1,0:T(8,128)(2,1)S(1)} %get-tuple-element.56.refs_3_), channel_id=1, source_target_pairs={{0,68},{64,0},{4,64},{68,4},{1,69},{65,1},{5,65},{69,5},{2,70},{66... | collective-permute-start | bytes 3145736 | tf_op jit(solution)/shard_map/weights/ppermute | solution.py:41
  44.7 2.2 %collective-permute-start.11 = (bf16[64,256]{1,0:T(8,128)(2,1)S(1)}, bf16[64,256]{1,0:T(8,128)(2,1)S(1)}, u32[]{:S(2)}, u32[]{:S(2)}) collective-permute-start(bf16[64,256]{1,0:T(8,128)(2,1)S(1)} %pad_maximum_fusion.1.own_lengths), channel_id=1, source_target_pairs={{0,8},{8,0},{1,9},{9,1},{2,10},{10,2},{3,11},{11,3},{4,12},{12,4},... | collective-permute-start | bytes 98312 | tf_op jit(solution)/shard_map/weights/ppermute | solution.py:41
  46.9 1.5 collective-permute-start.10
  65.4 27.6 %collective-permute-start.16 = (bf16[512,1024]{1,0:T(8,128)(2,1)S(1)}, bf16[512,1024]{1,0:T(8,128)(2,1)S(1)}, u32[]{:S(2)}, u32[]{:S(2)}) collective-permute-start(bf16[512,1024]{1,0:T(8,128)(2,1)S(1)} %get-tuple-element.53.refs_0_), channel_id=1, source_target_pairs={{0,2},{1,3},{2,0},{3,1},{4,6},{5,7},{6,4},{7,5},{8,10},{9,11},{10,... | collective-permute-start | bytes 3145736 | tf_op jit(solution)/shard_map/forward/ppermute | solution.py:41
  69.3 26.6 %collective-permute-start.17 = (bf16[512,1024]{1,0:T(8,128)(2,1)S(1)}, bf16[512,1024]{1,0:T(8,128)(2,1)S(1)}, u32[]{:S(2)}, u32[]{:S(2)}) collective-permute-start(bf16[512,1024]{1,0:T(8,128)(2,1)S(1)} %get-tuple-element.56.refs_3_), channel_id=1, source_target_pairs={{0,4},{64,68},{4,0},{68,64},{1,5},{65,69},{5,1},{69,65},{2,6},{66,... | collective-permute-start | bytes 3145736 | tf_op jit(solution)/shard_map/forward/ppermute | solution.py:41
  69.3 26.6 %copy-start = (s32[6144,128]{1,0:T(8,128)S(1)}, s32[6144,128]{1,0:T(8,128)}, u32[]{:S(2)}) copy-start(s32[6144,128]{1,0:T(8,128)} %get-tuple-element.51.docs_all) | copy-start | bytes 9437188
  69.3 26.6 %copy-start.1 = (f32[768,1024]{1,0:T(8,128)S(1)}, f32[768,1024]{1,0:T(8,128)}, u32[]{:S(2)}) copy-start(f32[768,1024]{1,0:T(8,128)} %get-tuple-element.52.normed) | copy-start | bytes 9437188
  108.0 5.7 %collective-permute-start.18 = (f32[768,1024]{1,0:T(8,128)S(1)}, f32[768,1024]{1,0:T(8,128)S(1)}, u32[]{:S(2)}, u32[]{:S(2)}) collective-permute-start(f32[768,1024]{1,0:T(8,128)S(1)} %get-tuple-element.60), channel_id=1, source_target_pairs={{0,8},{8,0},{1,9},{9,1},{2,10},{10,2},{3,11},{11,3},{4,12},{12,4},... | collective-permute-start | bytes 9437192 | tf_op jit(solution)/shard_map/pooled/ppermute | solution.py:41
  115.4 6.2 %copy-start.4 = (s32[96,1]{0,1:T(1,128)S(1)}, s32[96,1]{0,1:T(1,128)}, u32[]{:S(2)}) copy-start(s32[96,1]{0,1:T(1,128)} %param.9) | copy-start | bytes 1156
  115.4 27.3 %all-to-all-start = ((bf16[8,96,1024]{2,1,0:T(8,128)(2,1)}), bf16[8,96,1024]{2,1,0:T(8,128)(2,1)S(1)}, u32[]{:S(2)}, u32[]{:S(2)}) async-start(bf16[8,96,1024]{2,1,0:T(8,128)(2,1)} %bitcast.4), calls=%async_computation | async-start | bytes 3145728 | tf_op jit(solution)/shard_map/pooled/all_to_all | solution.py:534
  163.8 1.9 %collective-permute-start.19 = (bf16[64,4,1024]{2,1,0:T(4,128)(2,1)S(1)}, bf16[64,4,1024]{2,1,0:T(4,128)(2,1)S(1)}, u32[]{:S(2)}, u32[]{:S(2)}) collective-permute-start(bf16[64,4,1024]{2,1,0:T(4,128)(2,1)S(1)} %all_to_all.16), channel_id=1, source_target_pairs={{0,8},{8,0},{1,9},{9,1},{2,10},{10,2},{3,11},{11,3},{4,12},{12,4},... | collective-permute-start | bytes 1572872 | tf_op jit(solution)/shard_map/match/ppermute | solution.py:41

commit v6 on v5

--- a/solution.py
+++ b/solution.py
@@ -47,24 +47,16 @@
 
 def copied(sources, shapes, moves):
     def kernel(*refs):
-        inputs, (*outputs, sems) = refs[: len(sources)], refs[len(sources) :]
-        copies = [
-            pltpu.make_async_copy(
-                inputs[source].at[pl.ds(from_row, rows), :], outputs[result].at[pl.ds(to_row, rows), :], sems.at[number]
-            )
-            for number, (source, from_row, result, to_row, rows) in enumerate(moves)
-        ]
-        for copy in copies:
-            copy.start()
-        for copy in copies:
-            copy.wait()
-
+        inputs, outputs = refs[: len(sources)], refs[len(sources) :]
+        for source, from_row, result, to_row, rows in moves:
+            outputs[result][to_row : to_row + rows, :] = inputs[source][from_row : from_row + rows, :]
+
+    vmem = pl.BlockSpec(memory_space=pltpu.VMEM)
     return pl.pallas_call(
         kernel,
-        in_specs=[pl.BlockSpec(memory_space=pl.ANY)] * len(sources),
-        out_specs=[pl.BlockSpec(memory_space=pltpu.VMEM)] * len(shapes),
+        in_specs=[vmem] * len(sources),
+        out_specs=[vmem] * len(shapes),
         out_shape=[jax.ShapeDtypeStruct(shape, sources[0].dtype) for shape in shapes],
-        scratch_shapes=[pltpu.SemaphoreType.DMA((len(moves),))],
         compiler_params=pltpu.CompilerParams(vmem_limit_bytes=8 << 20),
         cost_estimate=pl.CostEstimate(flops=1 << 10, bytes_accessed=1 << 10, transcendentals=0),
     )(*sources)
@@ -88,6 +80,27 @@
     return copied(sources, shapes, moves)
 
 
+def with_lengths(ids, pieces):
+    def kernel(ids_ref, *refs):
+        pieces, out = refs[:-1], refs[-1]
+        out[: ids_ref.shape[0], :] = ids_ref[...]
+        for half in range(2):
+            for number, piece in enumerate(pieces):
+                at = ids_ref.shape[0] + (half * len(pieces) + number) * 16
+                part = piece[piece.shape[0] - 16 :, half * LANES : (half + 1) * LANES]
+                out[at : at + 16, :] = part.astype(jnp.float32).astype(jnp.int32)
+
+    vmem = pl.BlockSpec(memory_space=pltpu.VMEM)
+    return pl.pallas_call(
+        kernel,
+        in_specs=[vmem] * (1 + len(pieces)),
+        out_specs=vmem,
+        out_shape=jax.ShapeDtypeStruct((ids.shape[0] + 32 * len(pieces), LANES), jnp.int32),
+        compiler_params=pltpu.CompilerParams(vmem_limit_bytes=4 << 20),
+        cost_estimate=pl.CostEstimate(flops=1 << 10, bytes_accessed=1 << 10, transcendentals=0),
+    )(ids, *pieces)
+
+
 def half_gelu(half):
     square = half * half
     total = jnp.full_like(square, ERF_Q[-1] * 4.0 ** (len(ERF_Q) - 1) * 2)
@@ -154,7 +167,7 @@
     return keys, jnp.sum(ones.astype(jnp.float32), axis=0, keepdims=True)
 
 
-def prepare(place, own_ids, other_ids, own_lengths, other_lengths, table_all, positions, x_out, docs_out, bounds, normed_out, *scratch):
+def prepare(place, own_ids, other_ids, table_all, positions, x_out, docs_out, bounds, normed_out, *scratch):
     total, rows32, table32, table, list_buffer, listed, sem, table_sem = scratch
     width = table.shape[1]
     pieces = width // LANES
@@ -175,13 +188,14 @@
         row, lane = (lax.broadcasted_iota(jnp.int32, (LANES, LANES), axis) for axis in range(2))
         of_doc = (row == lane >> SEQ_BITS).astype(jnp.bfloat16)
         used = []
-        for lengths in (own_lengths, other_lengths):
+        half_rows = own_ids.shape[0] // 2
+        for tokens in (own_ids, other_ids):
             for half in range(2):
-                columns = slice(half * LANES, (half + 1) * LANES)
-                around = [
-                    jnp.dot(lengths[16 * number : 16 * number + 16, columns], of_doc, preferred_element_type=jnp.float32)
-                    for number in range(4)
-                ]
+                around = []
+                for number in range(4):
+                    at = half_rows + (half * 4 + number) * 16
+                    lengths = tokens[at : at + 16, :].astype(jnp.float32).astype(jnp.bfloat16)
+                    around.append(jnp.dot(lengths, of_doc, preferred_element_type=jnp.float32))
                 for y in range(4):
                     away = (y - place[1]) & 3
                     value = around[0]
@@ -189,7 +203,7 @@
                         value = jnp.where(away == by, around[number], value)
                     used.append(value)
         used = jnp.concatenate(used, axis=0).astype(jnp.int32)
-        ids = jnp.concatenate([own_ids[...], other_ids[...]], axis=0)
+        ids = jnp.concatenate([own_ids[:half_rows, :], other_ids[:half_rows, :]], axis=0)
         row, lane = (lax.broadcasted_iota(jnp.int32, ids.shape, axis) for axis in range(2))
         own_row = ids - place[0]
         doc = (row >> 4) * (12 * 8) + (row & 15) * 8 + (lane >> SEQ_BITS)
@@ -266,14 +280,14 @@
     copy.wait()
 
 
-def run_prepare(place, ids, other_ids, lengths, other_lengths, embed_table, positions, group, most):
+def run_prepare(place, own_ids, other_ids, embed_table, positions, group, most):
     seq, width = positions.shape
     vocab_rows = embed_table.shape[0]
     pieces = width // LANES
     smem, vmem, hbm = (pl.BlockSpec(memory_space=space) for space in (pltpu.SMEM, pltpu.VMEM, pltpu.HBM))
     return pl.pallas_call(
         prepare,
-        in_specs=[smem] + [vmem] * 4 + [hbm, vmem],
+        in_specs=[smem, vmem, vmem, hbm, vmem],
         out_specs=[hbm, hbm, smem, hbm],
         out_shape=[
             jax.ShapeDtypeStruct((most, width), jnp.bfloat16),
@@ -293,7 +307,7 @@
         ],
         compiler_params=pltpu.CompilerParams(vmem_limit_bytes=52 << 20),
         cost_estimate=pl.CostEstimate(flops=1 << 30, bytes_accessed=1 << 20, transcendentals=0),
-    )(place, ids, other_ids, lengths, other_lengths, embed_table, positions.astype(jnp.float32).reshape(seq * pieces, LANES))
+    )(place, own_ids, other_ids, embed_table, positions.astype(jnp.float32).reshape(seq * pieces, LANES))
 
 
 def over_tiles(tiles, several):
@@ -507,11 +521,10 @@
         place = jnp.stack([lax.axis_index(COL) * vocab_rows, lax.axis_index("y")]).astype(jnp.int32)
         first, second = ring(first, X), ring(second, "y")
         first, second, token_ids = lax.optimization_barrier((first, second, token_ids))
-        lengths = jnp.concatenate([piece[rows:, : 2 * LANES] for piece in second], axis=0)
-        lengths = (lengths, step(lengths, "core", 1))
         ids = token_ids.reshape(n_col, doc_dev * seq // LANES, LANES)
         ids = jnp.pad(ids, ((0, 0), (0, 16 - ids.shape[1]), (0, 0))).reshape(n_col * 16, LANES)
-        ids = (ids, step(ids, "core", 1))
+        own_ids = with_lengths(ids, second)
+        other_ids = step(own_ids, "core", 1)
         first, second = joined([first, second], [0, 0], rows)
         units = first.shape[0] // 2
         left, right = step(first, "y", 1), step(first, "y", -1)
@@ -520,7 +533,7 @@
 
     with jax.named_scope("prepare"):
         most = 2 * n_col * SHARD_CAP
-        x, docs, bounds, normed = run_prepare(place, *ids, *lengths, embed_table, positions, group, most)
+        x, docs, bounds, normed = run_prepare(place, own_ids, other_ids, embed_table, positions, group, most)
 
     with jax.named_scope("forward"):
         near, x = lax.optimization_barrier((near, x))
@@ -562,8 +575,10 @@
         own = jnp.arange(count)[:, None] == jnp.arange(2 * count)[None, :]
         best = jnp.max(jnp.where(filled[None, :] & jnp.logical_not(own), scores, -1.0), axis=1)
         best = jnp.maximum(best, -1.0)
-        returned = lax.all_to_all(best.reshape(n_clusters, 4), CHIPS, 0, 0, tiled=True).reshape(-1)
-        return jnp.sum(jnp.where(chosen, returned[:, None], 0.0), axis=0)
+        returned = lax.all_to_all(best.reshape(n_clusters, 4), CHIPS, 0, 0, tiled=True)
+        of_cluster = (labels[:, None] == jnp.arange(n_clusters)[None, :]).astype(jnp.float32)
+        rows = jnp.dot(of_cluster, returned, precision=lax.Precision.HIGHEST, preferred_element_type=jnp.float32)
+        return jnp.sum(jnp.where(rank[:, None] == jnp.arange(4)[None, :], rows, 0.0), axis=1)
 
 
 def solution(mesh):

time: 184 us -> 179 us (0.973)
  starting transfers between devices: 35.5 us -> 30.9 us
  waiting for transfers between devices: 52.8 us -> 49.2 us
    ppermute x19 -> x18, waiting for transfers between devices: 32.1 us -> 28.4 us  [step(): lax.ppermute(value, axis, [(place(i), place((i + by) % count)) for i in r...]
    ppermute x19 -> x18, starting transfers between devices: 26.1 us -> 23.2 us  [step(): lax.ppermute(value, axis, [(place(i), place((i + by) % count)) for i in r...]
    pallas_call x1, Pallas kernels: 17.2 us -> 19.8 us  [run_first(): pl.pallas_call(functools.partial(first_units, len(near)), in_specs=[smem,...]
    pallas_call x3 -> x4, Pallas kernels: 20.7 us -> 18.4 us  [the longest x1 18.2 us: run_prepare(): pl.pallas_call(prepare, in_specs=[smem, vmem, vmem, hbm, vmem], out_specs...]
  transfers between devices with their start and end apart: 21 -> 20, of which waited for: 10 -> 10; matrix products, arithmetic and copies ran while one was open for 2% -> 2% of each run, Pallas kernels for 19% -> 21%
where the time goes in v6:
time: 179 us; the launch traced here: 178 us
  Pallas kernels  51.7 us (29%)
  waiting for transfers between devices  49.2 us (27%)
  blocking collectives  35.9 us (20%)
  starting transfers between devices  30.9 us (17%)
  local copies, waits for them, and re-layouts  4.56 us (3%)
  other arithmetic  3.74 us (2%)
    ppermute x18, waiting for transfers between devices, step(): lax.ppermute(value, axis, [(place(i), place((i + by) % count)) for i in r...  28.4 us
    ppermute x18, starting transfers between devices, step(): lax.ppermute(value, axis, [(place(i), place((i + by) % count)) for i in r...  23.2 us
    all_to_all x1, blocking collectives, local(): members = lax.all_to_all(outgoing, CHIPS, 0, 0, tiled=True)  21.4 us
    all_to_all x1, waiting for transfers between devices, local(): sums = lax.all_to_all(sums, COL, 0, 0, tiled=True)  20.8 us
    pallas_call x1, Pallas kernels, run_first(): pl.pallas_call(functools.partial(first_units, len(near)), in_specs=[smem,...  19.8 us
    pallas_call x1, Pallas kernels, run_prepare(): pl.pallas_call(prepare, in_specs=[smem, vmem, vmem, hbm, vmem], out_specs...  18.2 us
    all_to_all x1, blocking collectives, local(): lax.all_to_all(best.reshape(n_clusters, 4), CHIPS, 0, 0, tiled=True)  14.6 us
    pallas_call x1, Pallas kernels, run_second(): pl.pallas_call(functools.partial(second_units, len(far)), in_specs=[smem,...  13.5 us
  transfers between devices with their start and end apart: 20, of which 10 were waited for; matrix products, arithmetic and copies ran while one was open for 2% of the time, Pallas kernels for 21%

profile of v6, /device:TPU:0, one launch (start us, length us, event | category | flops | bytes accessed | tf_op | source)
XLA Modules:
  0.0 178.1 jit_solution(17413300934161591157)
XLA Ops:
  0.0 0.8 fusion.12
  1.7 3.2 %collective-permute-start.3 = (bf16[16,128]{1,0:T(8,128)(2,1)S(1)}, bf16[16,128]{1,0:T(8,128)(2,1)S(1)}, u32[]{:S(2)}, u32[]{:S(2)}) collective-permute-start(bf16[16,128]{1,0:T(8,128)(2,1)S(1)} %pad.17), channel_id=1, source_target_pairs={{0,4},{4,0},{1,5},{5,1},{2,6},{6,2},{3,7},{7,3},{8,12},{12,8},{9,1... | collective-permute-start | bytes 12296 | tf_op jit(solution)/shard_map/weights/ppermute | solution.py:515
  4.9 1.9 %collective-permute-start = (bf16[64,1024]{1,0:T(8,128)(2,1)S(1)}, bf16[64,1024]{1,0:T(8,128)(2,1)S(1)}, u32[]{:S(2)}, u32[]{:S(2)}) collective-permute-start(bf16[64,1024]{1,0:T(8,128)(2,1)S(1)} %pad_maximum_fusion.refs_0_.refs_4_), channel_id=1, source_target_pairs={{0,16},{16,32},{32,48},{48,0},{1,17},{17,33},{33,49},{49,1},{2,18}... | collective-permute-start | bytes 393224 | tf_op jit(solution)/shard_map/weights/ppermute | solution.py:41
  6.8 2.1 %collective-permute-start.1 = (bf16[64,1024]{1,0:T(8,128)(2,1)S(1)}, bf16[64,1024]{1,0:T(8,128)(2,1)S(1)}, u32[]{:S(2)}, u32[]{:S(2)}) collective-permute-start(bf16[64,1024]{1,0:T(8,128)(2,1)S(1)} %pad_maximum_fusion.refs_0_.refs_4_), channel_id=1, source_target_pairs={{0,48},{16,0},{32,16},{48,32},{1,49},{17,1},{33,17},{49,33},{2,50}... | collective-permute-start | bytes 393224 | tf_op jit(solution)/shard_map/weights/ppermute | solution.py:41
  8.9 1.9 %collective-permute-start.2 = (bf16[64,1024]{1,0:T(8,128)(2,1)S(1)}, bf16[64,1024]{1,0:T(8,128)(2,1)S(1)}, u32[]{:S(2)}, u32[]{:S(2)}) collective-permute-start(bf16[64,1024]{1,0:T(8,128)(2,1)S(1)} %pad_maximum_fusion.refs_0_.refs_4_), channel_id=1, source_target_pairs={{0,32},{16,48},{32,0},{48,16},{1,33},{17,49},{33,1},{49,17},{2,34}... | collective-permute-start | bytes 393224 | tf_op jit(solution)/shard_map/weights/ppermute | solution.py:41
  10.8 1.3 collective-permute-done.refs_1_.refs_5_
  12.1 2.1 %collective-permute-done.1.refs_2_.refs_6_ = bf16[64,1024]{1,0:T(8,128)(2,1)S(1)} collective-permute-done((bf16[64,1024]{1,0:T(8,128)(2,1)S(1)}, bf16[64,1024]{1,0:T(8,128)(2,1)S(1)}, u32[]{:S(2)}, u32[]{:S(2)}) %collective-permute-start.1) | collective-permute-done | bytes 131104 | tf_op jit(solution)/shard_map/weights/ppermute | solution.py:41
  14.2 1.9 %collective-permute-done.2.refs_3_.refs_7_ = bf16[64,1024]{1,0:T(8,128)(2,1)S(1)} collective-permute-done((bf16[64,1024]{1,0:T(8,128)(2,1)S(1)}, bf16[64,1024]{1,0:T(8,128)(2,1)S(1)}, u32[]{:S(2)}, u32[]{:S(2)}) %collective-permute-start.2) | collective-permute-done | bytes 131104 | tf_op jit(solution)/shard_map/weights/ppermute | solution.py:41
  16.8 1.6 collective-permute-start.7
  18.4 1.7 collective-permute-start.8
  20.1 2.0 %collective-permute-start.9 = (bf16[144,1024]{1,0:T(8,128)(2,1)S(1)}, bf16[144,1024]{1,0:T(8,128)(2,1)S(1)}, u32[]{:S(2)}, u32[]{:S(2)}) collective-permute-start(bf16[144,1024]{1,0:T(8,128)(2,1)S(1)} %get-tuple-element.38.refs_0_.refs_4_), channel_id=1, source_target_pairs={{0,2},{1,3},{2,0},{3,1},{4,6},{5,7},{6,4},{7,5},{8,10},{9,11},{10,... | collective-permute-start | bytes 884744 | tf_op jit(solution)/shard_map/weights/ppermute | solution.py:41
  22.1 2.6 %collective-permute-start.5 = (bf16[128,1024]{1,0:T(8,128)(2,1)S(1)}, bf16[128,1024]{1,0:T(8,128)(2,1)S(1)}, u32[]{:S(2)}, u32[]{:S(2)}) collective-permute-start(bf16[128,1024]{1,0:T(8,128)(2,1)S(1)} %get-tuple-element.43.refs_0_), channel_id=1, source_target_pairs={{0,68},{64,0},{4,64},{68,4},{1,69},{65,1},{5,65},{69,5},{2,70},{66... | collective-permute-start | bytes 786440 | tf_op jit(solution)/shard_map/weights/ppermute | solution.py:41
  24.7 9.2 %collective-permute-done.5.refs_2_ = bf16[128,1024]{1,0:T(8,128)(2,1)S(1)} collective-permute-done((bf16[128,1024]{1,0:T(8,128)(2,1)S(1)}, bf16[128,1024]{1,0:T(8,128)(2,1)S(1)}, u32[]{:S(2)}, u32[]{:S(2)}) %collective-permute-start.5) | collective-permute-done | bytes 262176 | tf_op jit(solution)/shard_map/weights/ppermute | solution.py:41
  34.9 2.6 %collective-permute-start.12 = (bf16[512,1024]{1,0:T(8,128)(2,1)S(1)}, bf16[512,1024]{1,0:T(8,128)(2,1)}, u32[]{:S(2)}, u32[]{:S(2)}) collective-permute-start(bf16[512,1024]{1,0:T(8,128)(2,1)S(1)} %get-tuple-element.53.refs_0_), channel_id=1, source_target_pairs={{0,3},{1,0},{2,1},{3,2},{4,7},{5,4},{6,5},{7,6},{8,11},{9,8},{10,9... | collective-permute-start | bytes 3145736 | tf_op jit(solution)/shard_map/weights/ppermute | solution.py:41
  37.4 1.6 collective-permute-start.13
  39.0 2.1 %collective-permute-start.14 = (bf16[512,1024]{1,0:T(8,128)(2,1)S(1)}, bf16[512,1024]{1,0:T(8,128)(2,1)}, u32[]{:S(2)}, u32[]{:S(2)}) collective-permute-start(bf16[512,1024]{1,0:T(8,128)(2,1)S(1)} %get-tuple-element.56.refs_3_), channel_id=1, source_target_pairs={{0,68},{64,0},{4,64},{68,4},{1,69},{65,1},{5,65},{69,5},{2,70},{66... | collective-permute-start | bytes 3145736 | tf_op jit(solution)/shard_map/weights/ppermute | solution.py:41
  41.1 0.9 copy.18
  42.0 1.1 reshape.70
  43.4 1.2 collective-permute-done.10.other_ids
  44.6 18.2 %prepare.1 = (bf16[6144,1024]{1,0:T(8,128)(2,1)}, s32[6144,128]{1,0:T(8,128)}, s32[64]{0:T(128)S(1)}, f32[768,1024]{1,0:T(8,128)}) custom-call(s32[2]{0:T(128)S(1)} %pad_add_fusion.place, s32[256,128]{1,0:T(8,128)S(1)} %weights.4.own_ids, s32[256,128]{1,0:T(8,128)S(1)} %collective-permute-done.10.other_ids, bf16[3840,1024]{1,0:T(8,128)(2,1)} %table_all.1, ...), custom_call_target="tpu_custom_call" | custom-call | flops 1073741824 | bytes 1048576 | tf_op jit(solution)/shard_map/prepare/pallas_call | solution.py:288
  63.0 1.5 collective-permute-start.16
  64.5 19.8 %forward.2.sums_all = f32[6144,1024]{1,0:T(8,128)} custom-call(s32[64]{0:T(128)S(1)} %get-tuple-element.42.bounds, bf16[6144,1024]{1,0:T(8,128)(2,1)} %get-tuple-element.50.x_all, bf16[512,1024]{1,0:T(8,128)(2,1)S(1)} %get-tuple-element.53.refs_0_, bf16[512,1024]{1,0:T(8,128)(2,1)} %collective-permute-done.11.refs_1_, ...), custom_call_target="tpu_custom_call" | custom-call | flops 21474836480 | bytes 16777216 | tf_op jit(solution)/shard_map/forward/pallas_call | solution.py:452
  84.4 5.3 %collective-permute-done.15.refs_0_ = bf16[512,1024]{1,0:T(8,128)(2,1)S(1)} collective-permute-done((bf16[512,1024]{1,0:T(8,128)(2,1)S(1)}, bf16[512,1024]{1,0:T(8,128)(2,1)S(1)}, u32[]{:S(2)}, u32[]{:S(2)}) %collective-permute-start.15) | collective-permute-done | bytes 1048608 | tf_op jit(solution)/shard_map/forward/ppermute | solution.py:41
  89.8 13.5 %forward.3 = (f32[768,1024]{1,0:T(8,128)S(1)}, f32[768,1024]{1,0:T(8,128)S(1)}) custom-call(s32[64]{0:T(128)S(1)} %get-tuple-element.42.bounds, bf16[6144,1024]{1,0:T(8,128)(2,1)} %get-tuple-element.50.x_all, s32[6144,128]{1,0:T(8,128)S(1)} %copy-done, f32[768,1024]{1,0:T(8,128)S(1)} %copy-done.1, f32[6144,1024]{1,0:T(8,128)} %forward.2.sums_all, ...), custom_call_target="tpu_custom_call" | custom-call | flops 12884901888 | bytes 25165824 | tf_op jit(solution)/shard_map/forward/pallas_call | solution.py:478
  103.4 5.6 %collective-permute-done.17 = f32[768,1024]{1,0:T(8,128)S(1)} collective-permute-done((f32[768,1024]{1,0:T(8,128)S(1)}, f32[768,1024]{1,0:T(8,128)S(1)}, u32[]{:S(2)}, u32[]{:S(2)}) %collective-permute-start.17) | collective-permute-done | bytes 3145760 | tf_op jit(solution)/shard_map/pooled/ppermute | solution.py:41
  109.0 1.7 add_convert_fusion
  110.7 4.5 %all-to-all-start = ((bf16[8,96,1024]{2,1,0:T(8,128)(2,1)}), bf16[8,96,1024]{2,1,0:T(8,128)(2,1)S(1)}, u32[]{:S(2)}, u32[]{:S(2)}) async-start(bf16[8,96,1024]{2,1,0:T(8,128)(2,1)} %bitcast.4), calls=%async_computation | async-start | bytes 3145728 | tf_op jit(solution)/shard_map/pooled/all_to_all | solution.py:547
  115.6 20.8 %all-to-all-done = bf16[8,96,1024]{2,1,0:T(8,128)(2,1)S(1)} async-done(((bf16[8,96,1024]{2,1,0:T(8,128)(2,1)}), bf16[8,96,1024]{2,1,0:T(8,128)(2,1)S(1)}, u32[]{:S(2)}, u32[]{:S(2)}) %all-to-all-start) | async-done | bytes 1572896 | tf_op jit(solution)/shard_map/pooled/all_to_all | solution.py:547
  137.8 21.4 %all_to_all.19 = bf16[64,4,1024]{2,1,0:T(4,128)(2,1)S(1)} all-to-all(bf16[64,4,1024]{2,1,0:T(4,128)(2,1)S(1)} %select_convert_fusion), channel_id=1, replica_groups=mesh['x_lo'=2,'z'=4,'core'=2,'x_hi'=2,'y'=4] {'x_lo','z','x_hi','y'}, dimensions={0} | all-to-all | bytes 1048576 | tf_op jit(solution)/shard_map/match/all_to_all | solution.py:567
  159.5 1.6 collective-permute-done.18
  162.8 14.6 %all_to_all.20 = f32[64,1,4]{2,1,0:T(1,128)S(1)} all-to-all(f32[64,1,4]{2,1,0:T(1,128)S(1)} %bitcast.13), channel_id=1, replica_groups=mesh['x_lo'=2,'z'=4,'core'=2,'x_hi'=2,'y'=4] {'x_lo','z','x_hi','y'}, dimensions={0} | all-to-all | bytes 2048 | tf_op jit(solution)/shard_map/match/all_to_all | solution.py:578
  177.4 0.8 fusion.1
  (62 shorter events, 6.6 us)
Async XLA Ops:
  0.0 41.1 %copy-start.2 = (s32[768,16]{0,1:T(8,128)S(1)}, s32[768,16]{0,1:T(8,128)}, u32[]{:S(2)}) copy-start(s32[768,16]{0,1:T(8,128)} %param.7) | copy-start | bytes 147460
  0.0 43.3 %copy-start.3 = (bf16[16,1024]{1,0:T(8,128)(2,1)S(1)}, bf16[16,1024]{1,0:T(8,128)(2,1)}, u32[]{:S(2)}) copy-start(bf16[16,1024]{1,0:T(8,128)(2,1)} %param.11) | copy-start | bytes 98308
  1.7 9.1 %collective-permute-start.3 = (bf16[16,128]{1,0:T(8,128)(2,1)S(1)}, bf16[16,128]{1,0:T(8,128)(2,1)S(1)}, u32[]{:S(2)}, u32[]{:S(2)}) collective-permute-start(bf16[16,128]{1,0:T(8,128)(2,1)S(1)} %pad.17), channel_id=1, source_target_pairs={{0,4},{4,0},{1,5},{5,1},{2,6},{6,2},{3,7},{7,3},{8,12},{12,8},{9,1... | collective-permute-start | bytes 12296 | tf_op jit(solution)/shard_map/weights/ppermute | solution.py:515
  4.9 7.3 %collective-permute-start = (bf16[64,1024]{1,0:T(8,128)(2,1)S(1)}, bf16[64,1024]{1,0:T(8,128)(2,1)S(1)}, u32[]{:S(2)}, u32[]{:S(2)}) collective-permute-start(bf16[64,1024]{1,0:T(8,128)(2,1)S(1)} %pad_maximum_fusion.refs_0_.refs_4_), channel_id=1, source_target_pairs={{0,16},{16,32},{32,48},{48,0},{1,17},{17,33},{33,49},{49,1},{2,18}... | collective-permute-start | bytes 393224 | tf_op jit(solution)/shard_map/weights/ppermute | solution.py:41
  6.8 7.5 %collective-permute-start.1 = (bf16[64,1024]{1,0:T(8,128)(2,1)S(1)}, bf16[64,1024]{1,0:T(8,128)(2,1)S(1)}, u32[]{:S(2)}, u32[]{:S(2)}) collective-permute-start(bf16[64,1024]{1,0:T(8,128)(2,1)S(1)} %pad_maximum_fusion.refs_0_.refs_4_), channel_id=1, source_target_pairs={{0,48},{16,0},{32,16},{48,32},{1,49},{17,1},{33,17},{49,33},{2,50}... | collective-permute-start | bytes 393224 | tf_op jit(solution)/shard_map/weights/ppermute | solution.py:41
  8.9 7.2 %collective-permute-start.2 = (bf16[64,1024]{1,0:T(8,128)(2,1)S(1)}, bf16[64,1024]{1,0:T(8,128)(2,1)S(1)}, u32[]{:S(2)}, u32[]{:S(2)}) collective-permute-start(bf16[64,1024]{1,0:T(8,128)(2,1)S(1)} %pad_maximum_fusion.refs_0_.refs_4_), channel_id=1, source_target_pairs={{0,32},{16,48},{32,0},{48,16},{1,33},{17,49},{33,1},{49,17},{2,34}... | collective-permute-start | bytes 393224 | tf_op jit(solution)/shard_map/weights/ppermute | solution.py:41
  16.2 8.5 %collective-permute-start.4 = (bf16[128,1024]{1,0:T(8,128)(2,1)S(1)}, bf16[128,1024]{1,0:T(8,128)(2,1)S(1)}, u32[]{:S(2)}, u32[]{:S(2)}) collective-permute-start(bf16[128,1024]{1,0:T(8,128)(2,1)S(1)} %get-tuple-element.43.refs_0_), channel_id=1, source_target_pairs={{0,64},{64,4},{4,68},{68,0},{1,65},{65,5},{5,69},{69,1},{2,66},{66... | collective-permute-start | bytes 786440 | tf_op jit(solution)/shard_map/weights/ppermute | solution.py:41
  16.8 17.1 %collective-permute-start.7 = (bf16[144,1024]{1,0:T(8,128)(2,1)S(1)}, bf16[144,1024]{1,0:T(8,128)(2,1)S(1)}, u32[]{:S(2)}, u32[]{:S(2)}) collective-permute-start(bf16[144,1024]{1,0:T(8,128)(2,1)S(1)} %get-tuple-element.38.refs_0_.refs_4_), channel_id=1, source_target_pairs={{0,1},{1,2},{2,3},{3,0},{4,5},{5,6},{6,7},{7,4},{8,9},{9,10},{10,1... | collective-permute-start | bytes 884744 | tf_op jit(solution)/shard_map/weights/ppermute | solution.py:41
  18.4 15.6 %collective-permute-start.8 = (bf16[144,1024]{1,0:T(8,128)(2,1)S(1)}, bf16[144,1024]{1,0:T(8,128)(2,1)S(1)}, u32[]{:S(2)}, u32[]{:S(2)}) collective-permute-start(bf16[144,1024]{1,0:T(8,128)(2,1)S(1)} %get-tuple-element.38.refs_0_.refs_4_), channel_id=1, source_target_pairs={{0,3},{1,0},{2,1},{3,2},{4,7},{5,4},{6,5},{7,6},{8,11},{9,8},{10,9... | collective-permute-start | bytes 884744 | tf_op jit(solution)/shard_map/weights/ppermute | solution.py:41
  20.1 13.9 %collective-permute-start.9 = (bf16[144,1024]{1,0:T(8,128)(2,1)S(1)}, bf16[144,1024]{1,0:T(8,128)(2,1)S(1)}, u32[]{:S(2)}, u32[]{:S(2)}) collective-permute-start(bf16[144,1024]{1,0:T(8,128)(2,1)S(1)} %get-tuple-element.38.refs_0_.refs_4_), channel_id=1, source_target_pairs={{0,2},{1,3},{2,0},{3,1},{4,6},{5,7},{6,4},{7,5},{8,10},{9,11},{10,... | collective-permute-start | bytes 884744 | tf_op jit(solution)/shard_map/weights/ppermute | solution.py:41
  22.1 11.9 %collective-permute-start.5 = (bf16[128,1024]{1,0:T(8,128)(2,1)S(1)}, bf16[128,1024]{1,0:T(8,128)(2,1)S(1)}, u32[]{:S(2)}, u32[]{:S(2)}) collective-permute-start(bf16[128,1024]{1,0:T(8,128)(2,1)S(1)} %get-tuple-element.43.refs_0_), channel_id=1, source_target_pairs={{0,68},{64,0},{4,64},{68,4},{1,69},{65,1},{5,65},{69,5},{2,70},{66... | collective-permute-start | bytes 786440 | tf_op jit(solution)/shard_map/weights/ppermute | solution.py:41
  24.7 9.3 %collective-permute-start.6 = (bf16[128,1024]{1,0:T(8,128)(2,1)S(1)}, bf16[128,1024]{1,0:T(8,128)(2,1)S(1)}, u32[]{:S(2)}, u32[]{:S(2)}) collective-permute-start(bf16[128,1024]{1,0:T(8,128)(2,1)S(1)} %get-tuple-element.43.refs_0_), channel_id=1, source_target_pairs={{0,4},{64,68},{4,0},{68,64},{1,5},{65,69},{5,1},{69,65},{2,6},{66,... | collective-permute-start | bytes 786440 | tf_op jit(solution)/shard_map/weights/ppermute | solution.py:41
  34.1 28.7 %collective-permute-start.11 = (bf16[512,1024]{1,0:T(8,128)(2,1)S(1)}, bf16[512,1024]{1,0:T(8,128)(2,1)}, u32[]{:S(2)}, u32[]{:S(2)}) collective-permute-start(bf16[512,1024]{1,0:T(8,128)(2,1)S(1)} %get-tuple-element.53.refs_0_), channel_id=1, source_target_pairs={{0,1},{1,2},{2,3},{3,0},{4,5},{5,6},{6,7},{7,4},{8,9},{9,10},{10,1... | collective-permute-start | bytes 3145736 | tf_op jit(solution)/shard_map/weights/ppermute | solution.py:41
  34.9 28.0 %collective-permute-start.12 = (bf16[512,1024]{1,0:T(8,128)(2,1)S(1)}, bf16[512,1024]{1,0:T(8,128)(2,1)}, u32[]{:S(2)}, u32[]{:S(2)}) collective-permute-start(bf16[512,1024]{1,0:T(8,128)(2,1)S(1)} %get-tuple-element.53.refs_0_), channel_id=1, source_target_pairs={{0,3},{1,0},{2,1},{3,2},{4,7},{5,4},{6,5},{7,6},{8,11},{9,8},{10,9... | collective-permute-start | bytes 3145736 | tf_op jit(solution)/shard_map/weights/ppermute | solution.py:41
  37.4 25.5 %collective-permute-start.13 = (bf16[512,1024]{1,0:T(8,128)(2,1)S(1)}, bf16[512,1024]{1,0:T(8,128)(2,1)}, u32[]{:S(2)}, u32[]{:S(2)}) collective-permute-start(bf16[512,1024]{1,0:T(8,128)(2,1)S(1)} %get-tuple-element.56.refs_3_), channel_id=1, source_target_pairs={{0,64},{64,4},{4,68},{68,0},{1,65},{65,5},{5,69},{69,1},{2,66},{66... | collective-permute-start | bytes 3145736 | tf_op jit(solution)/shard_map/weights/ppermute | solution.py:41
  39.0 23.9 %collective-permute-start.14 = (bf16[512,1024]{1,0:T(8,128)(2,1)S(1)}, bf16[512,1024]{1,0:T(8,128)(2,1)}, u32[]{:S(2)}, u32[]{:S(2)}) collective-permute-start(bf16[512,1024]{1,0:T(8,128)(2,1)S(1)} %get-tuple-element.56.refs_3_), channel_id=1, source_target_pairs={{0,68},{64,0},{4,64},{68,4},{1,69},{65,1},{5,65},{69,5},{2,70},{66... | collective-permute-start | bytes 3145736 | tf_op jit(solution)/shard_map/weights/ppermute | solution.py:41
  43.2 1.4 collective-permute-start.10
  62.9 26.8 %collective-permute-start.15 = (bf16[512,1024]{1,0:T(8,128)(2,1)S(1)}, bf16[512,1024]{1,0:T(8,128)(2,1)S(1)}, u32[]{:S(2)}, u32[]{:S(2)}) collective-permute-start(bf16[512,1024]{1,0:T(8,128)(2,1)S(1)} %get-tuple-element.53.refs_0_), channel_id=1, source_target_pairs={{0,2},{1,3},{2,0},{3,1},{4,6},{5,7},{6,4},{7,5},{8,10},{9,11},{10,... | collective-permute-start | bytes 3145736 | tf_op jit(solution)/shard_map/forward/ppermute | solution.py:41
  63.0 26.8 %collective-permute-start.16 = (bf16[512,1024]{1,0:T(8,128)(2,1)S(1)}, bf16[512,1024]{1,0:T(8,128)(2,1)S(1)}, u32[]{:S(2)}, u32[]{:S(2)}) collective-permute-start(bf16[512,1024]{1,0:T(8,128)(2,1)S(1)} %get-tuple-element.56.refs_3_), channel_id=1, source_target_pairs={{0,4},{64,68},{4,0},{68,64},{1,5},{65,69},{5,1},{69,65},{2,6},{66,... | collective-permute-start | bytes 3145736 | tf_op jit(solution)/shard_map/forward/ppermute | solution.py:41
  64.5 25.2 %copy-start = (s32[6144,128]{1,0:T(8,128)S(1)}, s32[6144,128]{1,0:T(8,128)}, u32[]{:S(2)}) copy-start(s32[6144,128]{1,0:T(8,128)} %get-tuple-element.51.docs_all) | copy-start | bytes 9437188
  64.5 25.2 %copy-start.1 = (f32[768,1024]{1,0:T(8,128)S(1)}, f32[768,1024]{1,0:T(8,128)}, u32[]{:S(2)}) copy-start(f32[768,1024]{1,0:T(8,128)} %get-tuple-element.52.normed) | copy-start | bytes 9437188
  103.3 5.7 %collective-permute-start.17 = (f32[768,1024]{1,0:T(8,128)S(1)}, f32[768,1024]{1,0:T(8,128)S(1)}, u32[]{:S(2)}, u32[]{:S(2)}) collective-permute-start(f32[768,1024]{1,0:T(8,128)S(1)} %get-tuple-element.60), channel_id=1, source_target_pairs={{0,8},{8,0},{1,9},{9,1},{2,10},{10,2},{3,11},{11,3},{4,12},{12,4},... | collective-permute-start | bytes 9437192 | tf_op jit(solution)/shard_map/pooled/ppermute | solution.py:41
  110.7 4.5 %copy-start.4 = (s32[96,1]{0,1:T(1,128)S(1)}, s32[96,1]{0,1:T(1,128)}, u32[]{:S(2)}) copy-start(s32[96,1]{0,1:T(1,128)} %param.9) | copy-start | bytes 1156
  110.7 25.6 %all-to-all-start = ((bf16[8,96,1024]{2,1,0:T(8,128)(2,1)}), bf16[8,96,1024]{2,1,0:T(8,128)(2,1)S(1)}, u32[]{:S(2)}, u32[]{:S(2)}) async-start(bf16[8,96,1024]{2,1,0:T(8,128)(2,1)} %bitcast.4), calls=%async_computation | async-start | bytes 3145728 | tf_op jit(solution)/shard_map/pooled/all_to_all | solution.py:547
  159.2 1.9 %collective-permute-start.18 = (bf16[64,4,1024]{2,1,0:T(4,128)(2,1)S(1)}, bf16[64,4,1024]{2,1,0:T(4,128)(2,1)S(1)}, u32[]{:S(2)}, u32[]{:S(2)}) collective-permute-start(bf16[64,4,1024]{2,1,0:T(4,128)(2,1)S(1)} %all_to_all.19), channel_id=1, source_target_pairs={{0,8},{8,0},{1,9},{9,1},{2,10},{10,2},{3,11},{11,3},{4,12},{12,4},... | collective-permute-start | bytes 1572872 | tf_op jit(solution)/shard_map/match/ppermute | solution.py:41

commit v7 on v6

--- a/solution.py
+++ b/solution.py
@@ -21,9 +21,8 @@
 SEQ = 1 << SEQ_BITS
 NONE = 1 << 30
 BOUNDS = 64
-CHUNK = 256
+CHUNK = 512
 WINDOW = 384
-LIMIT = 5.4 * 5.4
 ERF_Q = (
     0.7978853416207131,
     0.03633264203955081,
@@ -297,8 +296,8 @@
         ],
         scratch_shapes=[
             pltpu.VMEM((group + WINDOW, width), jnp.float32),
-            pltpu.VMEM((TILE * pieces, LANES), jnp.float32),
-            pltpu.VMEM((vocab_rows * pieces, LANES), jnp.float32),
+            pltpu.VMEM(((TILE + 8) * pieces, LANES), jnp.float32),
+            pltpu.VMEM(((vocab_rows + 8) * pieces, LANES), jnp.float32),
             pltpu.VMEM((vocab_rows, width), jnp.bfloat16),
             pltpu.VMEM((most // LANES + 8, LANES), jnp.int32),
             pltpu.SMEM((most // LANES + 8, LANES), jnp.int32),

time: 179 us -> 179 us (level)
  no operation moved by 1% of the time
where the time goes in v7:
time: 179 us; the launch traced here: 178 us
  Pallas kernels  51 us (28%)
  waiting for transfers between devices  49.1 us (27%)
  blocking collectives  35.6 us (20%)
  starting transfers between devices  32.4 us (18%)
  local copies, waits for them, and re-layouts  4.56 us (3%)
  other arithmetic  3.74 us (2%)
    ppermute x18, waiting for transfers between devices, step(): lax.ppermute(value, axis, [(place(i), place((i + by) % count)) for i in r...  28.3 us
    ppermute x18, starting transfers between devices, step(): lax.ppermute(value, axis, [(place(i), place((i + by) % count)) for i in r...  24.1 us
    all_to_all x1, blocking collectives, local(): members = lax.all_to_all(outgoing, CHIPS, 0, 0, tiled=True)  21 us
    all_to_all x1, waiting for transfers between devices, local(): sums = lax.all_to_all(sums, COL, 0, 0, tiled=True)  20.8 us
    pallas_call x1, Pallas kernels, run_first(): pl.pallas_call(functools.partial(first_units, len(near)), in_specs=[smem,...  19.1 us
    pallas_call x1, Pallas kernels, run_prepare(): pl.pallas_call(prepare, in_specs=[smem, vmem, vmem, hbm, vmem], out_specs...  18.2 us
    all_to_all x1, blocking collectives, local(): lax.all_to_all(best.reshape(n_clusters, 4), CHIPS, 0, 0, tiled=True)  14.6 us
    pallas_call x1, Pallas kernels, run_second(): pl.pallas_call(functools.partial(second_units, len(far)), in_specs=[smem,...  13.5 us
  transfers between devices with their start and end apart: 20, of which 10 were waited for; matrix products, arithmetic and copies ran while one was open for 2% of the time, Pallas kernels for 21%

profile of v7, /device:TPU:0, one launch (start us, length us, event | category | flops | bytes accessed | tf_op | source)
XLA Modules:
  0.0 178.4 jit_solution(3101447338291482668)
XLA Ops:
  0.0 0.8 fusion.12
  1.7 3.2 %collective-permute-start.3 = (bf16[16,128]{1,0:T(8,128)(2,1)S(1)}, bf16[16,128]{1,0:T(8,128)(2,1)S(1)}, u32[]{:S(2)}, u32[]{:S(2)}) collective-permute-start(bf16[16,128]{1,0:T(8,128)(2,1)S(1)} %pad.17), channel_id=1, source_target_pairs={{0,4},{4,0},{1,5},{5,1},{2,6},{6,2},{3,7},{7,3},{8,12},{12,8},{9,1... | collective-permute-start | bytes 12296 | tf_op jit(solution)/shard_map/weights/ppermute | solution.py:514
  4.9 1.9 %collective-permute-start = (bf16[64,1024]{1,0:T(8,128)(2,1)S(1)}, bf16[64,1024]{1,0:T(8,128)(2,1)S(1)}, u32[]{:S(2)}, u32[]{:S(2)}) collective-permute-start(bf16[64,1024]{1,0:T(8,128)(2,1)S(1)} %pad_maximum_fusion.refs_0_.refs_4_), channel_id=1, source_target_pairs={{0,16},{16,32},{32,48},{48,0},{1,17},{17,33},{33,49},{49,1},{2,18}... | collective-permute-start | bytes 393224 | tf_op jit(solution)/shard_map/weights/ppermute | solution.py:40
  6.8 2.1 %collective-permute-start.1 = (bf16[64,1024]{1,0:T(8,128)(2,1)S(1)}, bf16[64,1024]{1,0:T(8,128)(2,1)S(1)}, u32[]{:S(2)}, u32[]{:S(2)}) collective-permute-start(bf16[64,1024]{1,0:T(8,128)(2,1)S(1)} %pad_maximum_fusion.refs_0_.refs_4_), channel_id=1, source_target_pairs={{0,48},{16,0},{32,16},{48,32},{1,49},{17,1},{33,17},{49,33},{2,50}... | collective-permute-start | bytes 393224 | tf_op jit(solution)/shard_map/weights/ppermute | solution.py:40
  8.9 1.9 %collective-permute-start.2 = (bf16[64,1024]{1,0:T(8,128)(2,1)S(1)}, bf16[64,1024]{1,0:T(8,128)(2,1)S(1)}, u32[]{:S(2)}, u32[]{:S(2)}) collective-permute-start(bf16[64,1024]{1,0:T(8,128)(2,1)S(1)} %pad_maximum_fusion.refs_0_.refs_4_), channel_id=1, source_target_pairs={{0,32},{16,48},{32,0},{48,16},{1,33},{17,49},{33,1},{49,17},{2,34}... | collective-permute-start | bytes 393224 | tf_op jit(solution)/shard_map/weights/ppermute | solution.py:40
  10.8 1.3 collective-permute-done.refs_1_.refs_5_
  12.1 2.1 %collective-permute-done.1.refs_2_.refs_6_ = bf16[64,1024]{1,0:T(8,128)(2,1)S(1)} collective-permute-done((bf16[64,1024]{1,0:T(8,128)(2,1)S(1)}, bf16[64,1024]{1,0:T(8,128)(2,1)S(1)}, u32[]{:S(2)}, u32[]{:S(2)}) %collective-permute-start.1) | collective-permute-done | bytes 131104 | tf_op jit(solution)/shard_map/weights/ppermute | solution.py:40
  14.2 1.9 %collective-permute-done.2.refs_3_.refs_7_ = bf16[64,1024]{1,0:T(8,128)(2,1)S(1)} collective-permute-done((bf16[64,1024]{1,0:T(8,128)(2,1)S(1)}, bf16[64,1024]{1,0:T(8,128)(2,1)S(1)}, u32[]{:S(2)}, u32[]{:S(2)}) %collective-permute-start.2) | collective-permute-done | bytes 131104 | tf_op jit(solution)/shard_map/weights/ppermute | solution.py:40
  16.8 1.6 collective-permute-start.7
  18.4 1.7 collective-permute-start.8
  20.1 2.0 %collective-permute-start.9 = (bf16[144,1024]{1,0:T(8,128)(2,1)S(1)}, bf16[144,1024]{1,0:T(8,128)(2,1)S(1)}, u32[]{:S(2)}, u32[]{:S(2)}) collective-permute-start(bf16[144,1024]{1,0:T(8,128)(2,1)S(1)} %get-tuple-element.38.refs_0_.refs_4_), channel_id=1, source_target_pairs={{0,2},{1,3},{2,0},{3,1},{4,6},{5,7},{6,4},{7,5},{8,10},{9,11},{10,... | collective-permute-start | bytes 884744 | tf_op jit(solution)/shard_map/weights/ppermute | solution.py:40
  22.1 2.6 %collective-permute-start.5 = (bf16[128,1024]{1,0:T(8,128)(2,1)S(1)}, bf16[128,1024]{1,0:T(8,128)(2,1)S(1)}, u32[]{:S(2)}, u32[]{:S(2)}) collective-permute-start(bf16[128,1024]{1,0:T(8,128)(2,1)S(1)} %get-tuple-element.43.refs_0_), channel_id=1, source_target_pairs={{0,68},{64,0},{4,64},{68,4},{1,69},{65,1},{5,65},{69,5},{2,70},{66... | collective-permute-start | bytes 786440 | tf_op jit(solution)/shard_map/weights/ppermute | solution.py:40
  24.7 9.2 %collective-permute-done.5.refs_2_ = bf16[128,1024]{1,0:T(8,128)(2,1)S(1)} collective-permute-done((bf16[128,1024]{1,0:T(8,128)(2,1)S(1)}, bf16[128,1024]{1,0:T(8,128)(2,1)S(1)}, u32[]{:S(2)}, u32[]{:S(2)}) %collective-permute-start.5) | collective-permute-done | bytes 262176 | tf_op jit(solution)/shard_map/weights/ppermute | solution.py:40
  34.9 2.6 %collective-permute-start.12 = (bf16[512,1024]{1,0:T(8,128)(2,1)S(1)}, bf16[512,1024]{1,0:T(8,128)(2,1)}, u32[]{:S(2)}, u32[]{:S(2)}) collective-permute-start(bf16[512,1024]{1,0:T(8,128)(2,1)S(1)} %get-tuple-element.53.refs_0_), channel_id=1, source_target_pairs={{0,3},{1,0},{2,1},{3,2},{4,7},{5,4},{6,5},{7,6},{8,11},{9,8},{10,9... | collective-permute-start | bytes 3145736 | tf_op jit(solution)/shard_map/weights/ppermute | solution.py:40
  37.4 1.6 collective-permute-start.13
  39.0 2.1 %collective-permute-start.14 = (bf16[512,1024]{1,0:T(8,128)(2,1)S(1)}, bf16[512,1024]{1,0:T(8,128)(2,1)}, u32[]{:S(2)}, u32[]{:S(2)}) collective-permute-start(bf16[512,1024]{1,0:T(8,128)(2,1)S(1)} %get-tuple-element.56.refs_3_), channel_id=1, source_target_pairs={{0,68},{64,0},{4,64},{68,4},{1,69},{65,1},{5,65},{69,5},{2,70},{66... | collective-permute-start | bytes 3145736 | tf_op jit(solution)/shard_map/weights/ppermute | solution.py:40
  41.1 0.9 copy.18
  42.0 1.1 reshape.70
  43.4 1.2 collective-permute-done.10.other_ids
  44.6 18.2 %prepare.1 = (bf16[6144,1024]{1,0:T(8,128)(2,1)}, s32[6144,128]{1,0:T(8,128)}, s32[64]{0:T(128)S(1)}, f32[768,1024]{1,0:T(8,128)}) custom-call(s32[2]{0:T(128)S(1)} %pad_add_fusion.place, s32[256,128]{1,0:T(8,128)S(1)} %weights.4.own_ids, s32[256,128]{1,0:T(8,128)S(1)} %collective-permute-done.10.other_ids, bf16[3840,1024]{1,0:T(8,128)(2,1)} %table_all.1, ...), custom_call_target="tpu_custom_call" | custom-call | flops 1073741824 | bytes 1048576 | tf_op jit(solution)/shard_map/prepare/pallas_call | solution.py:287
  63.0 2.4 %collective-permute-start.16 = (bf16[512,1024]{1,0:T(8,128)(2,1)S(1)}, bf16[512,1024]{1,0:T(8,128)(2,1)S(1)}, u32[]{:S(2)}, u32[]{:S(2)}) collective-permute-start(bf16[512,1024]{1,0:T(8,128)(2,1)S(1)} %get-tuple-element.56.refs_3_), channel_id=1, source_target_pairs={{0,4},{64,68},{4,0},{68,64},{1,5},{65,69},{5,1},{69,65},{2,6},{66,... | collective-permute-start | bytes 3145736 | tf_op jit(solution)/shard_map/forward/ppermute | solution.py:40
  65.5 19.1 %forward.2.sums_all = f32[6144,1024]{1,0:T(8,128)} custom-call(s32[64]{0:T(128)S(1)} %get-tuple-element.42.bounds, bf16[6144,1024]{1,0:T(8,128)(2,1)} %get-tuple-element.50.x_all, bf16[512,1024]{1,0:T(8,128)(2,1)S(1)} %get-tuple-element.53.refs_0_, bf16[512,1024]{1,0:T(8,128)(2,1)} %collective-permute-done.11.refs_1_, ...), custom_call_target="tpu_custom_call" | custom-call | flops 21474836480 | bytes 16777216 | tf_op jit(solution)/shard_map/forward/pallas_call | solution.py:451
  84.5 5.2 %collective-permute-done.15.refs_0_ = bf16[512,1024]{1,0:T(8,128)(2,1)S(1)} collective-permute-done((bf16[512,1024]{1,0:T(8,128)(2,1)S(1)}, bf16[512,1024]{1,0:T(8,128)(2,1)S(1)}, u32[]{:S(2)}, u32[]{:S(2)}) %collective-permute-start.15) | collective-permute-done | bytes 1048608 | tf_op jit(solution)/shard_map/forward/ppermute | solution.py:40
  89.8 13.5 %forward.3 = (f32[768,1024]{1,0:T(8,128)S(1)}, f32[768,1024]{1,0:T(8,128)S(1)}) custom-call(s32[64]{0:T(128)S(1)} %get-tuple-element.42.bounds, bf16[6144,1024]{1,0:T(8,128)(2,1)} %get-tuple-element.50.x_all, s32[6144,128]{1,0:T(8,128)S(1)} %copy-done, f32[768,1024]{1,0:T(8,128)S(1)} %copy-done.1, f32[6144,1024]{1,0:T(8,128)} %forward.2.sums_all, ...), custom_call_target="tpu_custom_call" | custom-call | flops 12884901888 | bytes 25165824 | tf_op jit(solution)/shard_map/forward/pallas_call | solution.py:477
  103.4 5.6 %collective-permute-done.17 = f32[768,1024]{1,0:T(8,128)S(1)} collective-permute-done((f32[768,1024]{1,0:T(8,128)S(1)}, f32[768,1024]{1,0:T(8,128)S(1)}, u32[]{:S(2)}, u32[]{:S(2)}) %collective-permute-start.17) | collective-permute-done | bytes 3145760 | tf_op jit(solution)/shard_map/pooled/ppermute | solution.py:40
  109.0 1.7 add_convert_fusion
  110.7 5.2 %all-to-all-start = ((bf16[8,96,1024]{2,1,0:T(8,128)(2,1)}), bf16[8,96,1024]{2,1,0:T(8,128)(2,1)S(1)}, u32[]{:S(2)}, u32[]{:S(2)}) async-start(bf16[8,96,1024]{2,1,0:T(8,128)(2,1)} %bitcast.4), calls=%async_computation | async-start | bytes 3145728 | tf_op jit(solution)/shard_map/pooled/all_to_all | solution.py:546
  116.2 20.8 %all-to-all-done = bf16[8,96,1024]{2,1,0:T(8,128)(2,1)S(1)} async-done(((bf16[8,96,1024]{2,1,0:T(8,128)(2,1)}), bf16[8,96,1024]{2,1,0:T(8,128)(2,1)S(1)}, u32[]{:S(2)}, u32[]{:S(2)}) %all-to-all-start) | async-done | bytes 1572896 | tf_op jit(solution)/shard_map/pooled/all_to_all | solution.py:546
  138.5 21.0 %all_to_all.19 = bf16[64,4,1024]{2,1,0:T(4,128)(2,1)S(1)} all-to-all(bf16[64,4,1024]{2,1,0:T(4,128)(2,1)S(1)} %select_convert_fusion), channel_id=1, replica_groups=mesh['x_lo'=2,'z'=4,'core'=2,'x_hi'=2,'y'=4] {'x_lo','z','x_hi','y'}, dimensions={0} | all-to-all | bytes 1048576 | tf_op jit(solution)/shard_map/match/all_to_all | solution.py:566
  159.8 1.6 collective-permute-done.18
  163.1 14.6 %all_to_all.20 = f32[64,1,4]{2,1,0:T(1,128)S(1)} all-to-all(f32[64,1,4]{2,1,0:T(1,128)S(1)} %bitcast.13), channel_id=1, replica_groups=mesh['x_lo'=2,'z'=4,'core'=2,'x_hi'=2,'y'=4] {'x_lo','z','x_hi','y'}, dimensions={0} | all-to-all | bytes 2048 | tf_op jit(solution)/shard_map/match/all_to_all | solution.py:577
  177.6 0.8 fusion.1
  (62 shorter events, 6.6 us)
Async XLA Ops:
  0.0 41.1 %copy-start.2 = (s32[768,16]{0,1:T(8,128)S(1)}, s32[768,16]{0,1:T(8,128)}, u32[]{:S(2)}) copy-start(s32[768,16]{0,1:T(8,128)} %param.7) | copy-start | bytes 147460
  0.0 43.3 %copy-start.3 = (bf16[16,1024]{1,0:T(8,128)(2,1)S(1)}, bf16[16,1024]{1,0:T(8,128)(2,1)}, u32[]{:S(2)}) copy-start(bf16[16,1024]{1,0:T(8,128)(2,1)} %param.11) | copy-start | bytes 98308
  1.7 9.1 %collective-permute-start.3 = (bf16[16,128]{1,0:T(8,128)(2,1)S(1)}, bf16[16,128]{1,0:T(8,128)(2,1)S(1)}, u32[]{:S(2)}, u32[]{:S(2)}) collective-permute-start(bf16[16,128]{1,0:T(8,128)(2,1)S(1)} %pad.17), channel_id=1, source_target_pairs={{0,4},{4,0},{1,5},{5,1},{2,6},{6,2},{3,7},{7,3},{8,12},{12,8},{9,1... | collective-permute-start | bytes 12296 | tf_op jit(solution)/shard_map/weights/ppermute | solution.py:514
  4.9 7.3 %collective-permute-start = (bf16[64,1024]{1,0:T(8,128)(2,1)S(1)}, bf16[64,1024]{1,0:T(8,128)(2,1)S(1)}, u32[]{:S(2)}, u32[]{:S(2)}) collective-permute-start(bf16[64,1024]{1,0:T(8,128)(2,1)S(1)} %pad_maximum_fusion.refs_0_.refs_4_), channel_id=1, source_target_pairs={{0,16},{16,32},{32,48},{48,0},{1,17},{17,33},{33,49},{49,1},{2,18}... | collective-permute-start | bytes 393224 | tf_op jit(solution)/shard_map/weights/ppermute | solution.py:40
  6.8 7.5 %collective-permute-start.1 = (bf16[64,1024]{1,0:T(8,128)(2,1)S(1)}, bf16[64,1024]{1,0:T(8,128)(2,1)S(1)}, u32[]{:S(2)}, u32[]{:S(2)}) collective-permute-start(bf16[64,1024]{1,0:T(8,128)(2,1)S(1)} %pad_maximum_fusion.refs_0_.refs_4_), channel_id=1, source_target_pairs={{0,48},{16,0},{32,16},{48,32},{1,49},{17,1},{33,17},{49,33},{2,50}... | collective-permute-start | bytes 393224 | tf_op jit(solution)/shard_map/weights/ppermute | solution.py:40
  8.9 7.2 %collective-permute-start.2 = (bf16[64,1024]{1,0:T(8,128)(2,1)S(1)}, bf16[64,1024]{1,0:T(8,128)(2,1)S(1)}, u32[]{:S(2)}, u32[]{:S(2)}) collective-permute-start(bf16[64,1024]{1,0:T(8,128)(2,1)S(1)} %pad_maximum_fusion.refs_0_.refs_4_), channel_id=1, source_target_pairs={{0,32},{16,48},{32,0},{48,16},{1,33},{17,49},{33,1},{49,17},{2,34}... | collective-permute-start | bytes 393224 | tf_op jit(solution)/shard_map/weights/ppermute | solution.py:40
  16.2 8.5 %collective-permute-start.4 = (bf16[128,1024]{1,0:T(8,128)(2,1)S(1)}, bf16[128,1024]{1,0:T(8,128)(2,1)S(1)}, u32[]{:S(2)}, u32[]{:S(2)}) collective-permute-start(bf16[128,1024]{1,0:T(8,128)(2,1)S(1)} %get-tuple-element.43.refs_0_), channel_id=1, source_target_pairs={{0,64},{64,4},{4,68},{68,0},{1,65},{65,5},{5,69},{69,1},{2,66},{66... | collective-permute-start | bytes 786440 | tf_op jit(solution)/shard_map/weights/ppermute | solution.py:40
  16.8 17.1 %collective-permute-start.7 = (bf16[144,1024]{1,0:T(8,128)(2,1)S(1)}, bf16[144,1024]{1,0:T(8,128)(2,1)S(1)}, u32[]{:S(2)}, u32[]{:S(2)}) collective-permute-start(bf16[144,1024]{1,0:T(8,128)(2,1)S(1)} %get-tuple-element.38.refs_0_.refs_4_), channel_id=1, source_target_pairs={{0,1},{1,2},{2,3},{3,0},{4,5},{5,6},{6,7},{7,4},{8,9},{9,10},{10,1... | collective-permute-start | bytes 884744 | tf_op jit(solution)/shard_map/weights/ppermute | solution.py:40
  18.4 15.6 %collective-permute-start.8 = (bf16[144,1024]{1,0:T(8,128)(2,1)S(1)}, bf16[144,1024]{1,0:T(8,128)(2,1)S(1)}, u32[]{:S(2)}, u32[]{:S(2)}) collective-permute-start(bf16[144,1024]{1,0:T(8,128)(2,1)S(1)} %get-tuple-element.38.refs_0_.refs_4_), channel_id=1, source_target_pairs={{0,3},{1,0},{2,1},{3,2},{4,7},{5,4},{6,5},{7,6},{8,11},{9,8},{10,9... | collective-permute-start | bytes 884744 | tf_op jit(solution)/shard_map/weights/ppermute | solution.py:40
  20.1 13.9 %collective-permute-start.9 = (bf16[144,1024]{1,0:T(8,128)(2,1)S(1)}, bf16[144,1024]{1,0:T(8,128)(2,1)S(1)}, u32[]{:S(2)}, u32[]{:S(2)}) collective-permute-start(bf16[144,1024]{1,0:T(8,128)(2,1)S(1)} %get-tuple-element.38.refs_0_.refs_4_), channel_id=1, source_target_pairs={{0,2},{1,3},{2,0},{3,1},{4,6},{5,7},{6,4},{7,5},{8,10},{9,11},{10,... | collective-permute-start | bytes 884744 | tf_op jit(solution)/shard_map/weights/ppermute | solution.py:40
  22.1 11.9 %collective-permute-start.5 = (bf16[128,1024]{1,0:T(8,128)(2,1)S(1)}, bf16[128,1024]{1,0:T(8,128)(2,1)S(1)}, u32[]{:S(2)}, u32[]{:S(2)}) collective-permute-start(bf16[128,1024]{1,0:T(8,128)(2,1)S(1)} %get-tuple-element.43.refs_0_), channel_id=1, source_target_pairs={{0,68},{64,0},{4,64},{68,4},{1,69},{65,1},{5,65},{69,5},{2,70},{66... | collective-permute-start | bytes 786440 | tf_op jit(solution)/shard_map/weights/ppermute | solution.py:40
  24.7 9.3 %collective-permute-start.6 = (bf16[128,1024]{1,0:T(8,128)(2,1)S(1)}, bf16[128,1024]{1,0:T(8,128)(2,1)S(1)}, u32[]{:S(2)}, u32[]{:S(2)}) collective-permute-start(bf16[128,1024]{1,0:T(8,128)(2,1)S(1)} %get-tuple-element.43.refs_0_), channel_id=1, source_target_pairs={{0,4},{64,68},{4,0},{68,64},{1,5},{65,69},{5,1},{69,65},{2,6},{66,... | collective-permute-start | bytes 786440 | tf_op jit(solution)/shard_map/weights/ppermute | solution.py:40
  34.1 28.8 %collective-permute-start.11 = (bf16[512,1024]{1,0:T(8,128)(2,1)S(1)}, bf16[512,1024]{1,0:T(8,128)(2,1)}, u32[]{:S(2)}, u32[]{:S(2)}) collective-permute-start(bf16[512,1024]{1,0:T(8,128)(2,1)S(1)} %get-tuple-element.53.refs_0_), channel_id=1, source_target_pairs={{0,1},{1,2},{2,3},{3,0},{4,5},{5,6},{6,7},{7,4},{8,9},{9,10},{10,1... | collective-permute-start | bytes 3145736 | tf_op jit(solution)/shard_map/weights/ppermute | solution.py:40
  34.9 28.0 %collective-permute-start.12 = (bf16[512,1024]{1,0:T(8,128)(2,1)S(1)}, bf16[512,1024]{1,0:T(8,128)(2,1)}, u32[]{:S(2)}, u32[]{:S(2)}) collective-permute-start(bf16[512,1024]{1,0:T(8,128)(2,1)S(1)} %get-tuple-element.53.refs_0_), channel_id=1, source_target_pairs={{0,3},{1,0},{2,1},{3,2},{4,7},{5,4},{6,5},{7,6},{8,11},{9,8},{10,9... | collective-permute-start | bytes 3145736 | tf_op jit(solution)/shard_map/weights/ppermute | solution.py:40
  37.4 25.5 %collective-permute-start.13 = (bf16[512,1024]{1,0:T(8,128)(2,1)S(1)}, bf16[512,1024]{1,0:T(8,128)(2,1)}, u32[]{:S(2)}, u32[]{:S(2)}) collective-permute-start(bf16[512,1024]{1,0:T(8,128)(2,1)S(1)} %get-tuple-element.56.refs_3_), channel_id=1, source_target_pairs={{0,64},{64,4},{4,68},{68,0},{1,65},{65,5},{5,69},{69,1},{2,66},{66... | collective-permute-start | bytes 3145736 | tf_op jit(solution)/shard_map/weights/ppermute | solution.py:40
  39.0 23.9 %collective-permute-start.14 = (bf16[512,1024]{1,0:T(8,128)(2,1)S(1)}, bf16[512,1024]{1,0:T(8,128)(2,1)}, u32[]{:S(2)}, u32[]{:S(2)}) collective-permute-start(bf16[512,1024]{1,0:T(8,128)(2,1)S(1)} %get-tuple-element.56.refs_3_), channel_id=1, source_target_pairs={{0,68},{64,0},{4,64},{68,4},{1,69},{65,1},{5,65},{69,5},{2,70},{66... | collective-permute-start | bytes 3145736 | tf_op jit(solution)/shard_map/weights/ppermute | solution.py:40
  43.2 1.4 collective-permute-start.10
  62.9 26.8 %collective-permute-start.15 = (bf16[512,1024]{1,0:T(8,128)(2,1)S(1)}, bf16[512,1024]{1,0:T(8,128)(2,1)S(1)}, u32[]{:S(2)}, u32[]{:S(2)}) collective-permute-start(bf16[512,1024]{1,0:T(8,128)(2,1)S(1)} %get-tuple-element.53.refs_0_), channel_id=1, source_target_pairs={{0,2},{1,3},{2,0},{3,1},{4,6},{5,7},{6,4},{7,5},{8,10},{9,11},{10,... | collective-permute-start | bytes 3145736 | tf_op jit(solution)/shard_map/forward/ppermute | solution.py:40
  63.0 26.8 %collective-permute-start.16 = (bf16[512,1024]{1,0:T(8,128)(2,1)S(1)}, bf16[512,1024]{1,0:T(8,128)(2,1)S(1)}, u32[]{:S(2)}, u32[]{:S(2)}) collective-permute-start(bf16[512,1024]{1,0:T(8,128)(2,1)S(1)} %get-tuple-element.56.refs_3_), channel_id=1, source_target_pairs={{0,4},{64,68},{4,0},{68,64},{1,5},{65,69},{5,1},{69,65},{2,6},{66,... | collective-permute-start | bytes 3145736 | tf_op jit(solution)/shard_map/forward/ppermute | solution.py:40
  65.4 24.3 %copy-start = (s32[6144,128]{1,0:T(8,128)S(1)}, s32[6144,128]{1,0:T(8,128)}, u32[]{:S(2)}) copy-start(s32[6144,128]{1,0:T(8,128)} %get-tuple-element.51.docs_all) | copy-start | bytes 9437188
  65.4 24.3 %copy-start.1 = (f32[768,1024]{1,0:T(8,128)S(1)}, f32[768,1024]{1,0:T(8,128)}, u32[]{:S(2)}) copy-start(f32[768,1024]{1,0:T(8,128)} %get-tuple-element.52.normed) | copy-start | bytes 9437188
  103.3 5.7 %collective-permute-start.17 = (f32[768,1024]{1,0:T(8,128)S(1)}, f32[768,1024]{1,0:T(8,128)S(1)}, u32[]{:S(2)}, u32[]{:S(2)}) collective-permute-start(f32[768,1024]{1,0:T(8,128)S(1)} %get-tuple-element.60), channel_id=1, source_target_pairs={{0,8},{8,0},{1,9},{9,1},{2,10},{10,2},{3,11},{11,3},{4,12},{12,4},... | collective-permute-start | bytes 9437192 | tf_op jit(solution)/shard_map/pooled/ppermute | solution.py:40
  110.7 5.2 %copy-start.4 = (s32[96,1]{0,1:T(1,128)S(1)}, s32[96,1]{0,1:T(1,128)}, u32[]{:S(2)}) copy-start(s32[96,1]{0,1:T(1,128)} %param.9) | copy-start | bytes 1156
  110.7 26.3 %all-to-all-start = ((bf16[8,96,1024]{2,1,0:T(8,128)(2,1)}), bf16[8,96,1024]{2,1,0:T(8,128)(2,1)S(1)}, u32[]{:S(2)}, u32[]{:S(2)}) async-start(bf16[8,96,1024]{2,1,0:T(8,128)(2,1)} %bitcast.4), calls=%async_computation | async-start | bytes 3145728 | tf_op jit(solution)/shard_map/pooled/all_to_all | solution.py:546
  159.5 1.9 %collective-permute-start.18 = (bf16[64,4,1024]{2,1,0:T(4,128)(2,1)S(1)}, bf16[64,4,1024]{2,1,0:T(4,128)(2,1)S(1)}, u32[]{:S(2)}, u32[]{:S(2)}) collective-permute-start(bf16[64,4,1024]{2,1,0:T(4,128)(2,1)S(1)} %all_to_all.19), channel_id=1, source_target_pairs={{0,8},{8,0},{1,9},{9,1},{2,10},{10,2},{3,11},{11,3},{4,12},{12,4},... | collective-permute-start | bytes 1572872 | tf_op jit(solution)/shard_map/match/ppermute | solution.py:40

commit v8 on v7

--- a/solution.py
+++ b/solution.py
@@ -22,7 +22,7 @@
 NONE = 1 << 30
 BOUNDS = 64
 CHUNK = 512
-WINDOW = 384
+WINDOW = 256
 ERF_Q = (
     0.7978853416207131,
     0.03633264203955081,

time: 179 us -> 178 us (level)
  Pallas kernels: 51 us -> 45.5 us
  waiting for transfers between devices: 49.1 us -> 52.7 us
  starting transfers between devices: 32.4 us -> 34.7 us
    ppermute x18, waiting for transfers between devices: 28.3 us -> 31.9 us  [step(): lax.ppermute(value, axis, [(place(i), place((i + by) % count)) for i in r...]
    pallas_call x1, Pallas kernels: 19.1 us -> 16.6 us  [run_first(): pl.pallas_call(functools.partial(first_units, len(near)), in_specs=[smem,...]
    all_to_all x1, starting transfers between devices: 5.16 us -> 7.55 us  [local(): sums = lax.all_to_all(sums, COL, 0, 0, tiled=True)]
  transfers between devices with their start and end apart: 20 -> 20, of which waited for: 10 -> 10; matrix products, arithmetic and copies ran while one was open for 2% -> 2% of each run, Pallas kernels for 21% -> 19%
where the time goes in v8:
time: 178 us; the launch traced here: 177 us
  waiting for transfers between devices  52.7 us (30%)
  Pallas kernels  45.5 us (26%)
  starting transfers between devices  34.7 us (19%)
  blocking collectives  34.2 us (19%)
  local copies, waits for them, and re-layouts  4.56 us (3%)
  other arithmetic  3.74 us (2%)
    ppermute x18, waiting for transfers between devices, step(): lax.ppermute(value, axis, [(place(i), place((i + by) % count)) for i in r...  31.9 us
    ppermute x18, starting transfers between devices, step(): lax.ppermute(value, axis, [(place(i), place((i + by) % count)) for i in r...  24 us
    all_to_all x1, waiting for transfers between devices, local(): sums = lax.all_to_all(sums, COL, 0, 0, tiled=True)  20.8 us
    all_to_all x1, blocking collectives, local(): members = lax.all_to_all(outgoing, CHIPS, 0, 0, tiled=True)  19.7 us
    pallas_call x1, Pallas kernels, run_prepare(): pl.pallas_call(prepare, in_specs=[smem, vmem, vmem, hbm, vmem], out_specs...  16.6 us
    pallas_call x1, Pallas kernels, run_first(): pl.pallas_call(functools.partial(first_units, len(near)), in_specs=[smem,...  16.6 us
    all_to_all x1, blocking collectives, local(): lax.all_to_all(best.reshape(n_clusters, 4), CHIPS, 0, 0, tiled=True)  14.6 us
    pallas_call x1, Pallas kernels, run_second(): pl.pallas_call(functools.partial(second_units, len(far)), in_specs=[smem,...  12 us
  transfers between devices with their start and end apart: 20, of which 10 were waited for; matrix products, arithmetic and copies ran while one was open for 2% of the time, Pallas kernels for 19%

profile of v8, /device:TPU:0, one launch (start us, length us, event | category | flops | bytes accessed | tf_op | source)
XLA Modules:
  0.0 177.4 jit_solution(3758036356000423792)
XLA Ops:
  1.7 3.2 %collective-permute-start.3 = (bf16[16,128]{1,0:T(8,128)(2,1)S(1)}, bf16[16,128]{1,0:T(8,128)(2,1)S(1)}, u32[]{:S(2)}, u32[]{:S(2)}) collective-permute-start(bf16[16,128]{1,0:T(8,128)(2,1)S(1)} %pad.17), channel_id=1, source_target_pairs={{0,4},{4,0},{1,5},{5,1},{2,6},{6,2},{3,7},{7,3},{8,12},{12,8},{9,1... | collective-permute-start | bytes 12296 | tf_op jit(solution)/shard_map/weights/ppermute | solution.py:514
  4.9 1.9 %collective-permute-start = (bf16[64,1024]{1,0:T(8,128)(2,1)S(1)}, bf16[64,1024]{1,0:T(8,128)(2,1)S(1)}, u32[]{:S(2)}, u32[]{:S(2)}) collective-permute-start(bf16[64,1024]{1,0:T(8,128)(2,1)S(1)} %pad_maximum_fusion.refs_0_.refs_4_), channel_id=1, source_target_pairs={{0,16},{16,32},{32,48},{48,0},{1,17},{17,33},{33,49},{49,1},{2,18}... | collective-permute-start | bytes 393224 | tf_op jit(solution)/shard_map/weights/ppermute | solution.py:40
  6.8 2.1 %collective-permute-start.1 = (bf16[64,1024]{1,0:T(8,128)(2,1)S(1)}, bf16[64,1024]{1,0:T(8,128)(2,1)S(1)}, u32[]{:S(2)}, u32[]{:S(2)}) collective-permute-start(bf16[64,1024]{1,0:T(8,128)(2,1)S(1)} %pad_maximum_fusion.refs_0_.refs_4_), channel_id=1, source_target_pairs={{0,48},{16,0},{32,16},{48,32},{1,49},{17,1},{33,17},{49,33},{2,50}... | collective-permute-start | bytes 393224 | tf_op jit(solution)/shard_map/weights/ppermute | solution.py:40
  8.9 1.9 %collective-permute-start.2 = (bf16[64,1024]{1,0:T(8,128)(2,1)S(1)}, bf16[64,1024]{1,0:T(8,128)(2,1)S(1)}, u32[]{:S(2)}, u32[]{:S(2)}) collective-permute-start(bf16[64,1024]{1,0:T(8,128)(2,1)S(1)} %pad_maximum_fusion.refs_0_.refs_4_), channel_id=1, source_target_pairs={{0,32},{16,48},{32,0},{48,16},{1,33},{17,49},{33,1},{49,17},{2,34}... | collective-permute-start | bytes 393224 | tf_op jit(solution)/shard_map/weights/ppermute | solution.py:40
  10.8 1.3 collective-permute-done.refs_1_.refs_5_
  12.1 2.1 %collective-permute-done.1.refs_2_.refs_6_ = bf16[64,1024]{1,0:T(8,128)(2,1)S(1)} collective-permute-done((bf16[64,1024]{1,0:T(8,128)(2,1)S(1)}, bf16[64,1024]{1,0:T(8,128)(2,1)S(1)}, u32[]{:S(2)}, u32[]{:S(2)}) %collective-permute-start.1) | collective-permute-done | bytes 131104 | tf_op jit(solution)/shard_map/weights/ppermute | solution.py:40
  14.2 1.9 %collective-permute-done.2.refs_3_.refs_7_ = bf16[64,1024]{1,0:T(8,128)(2,1)S(1)} collective-permute-done((bf16[64,1024]{1,0:T(8,128)(2,1)S(1)}, bf16[64,1024]{1,0:T(8,128)(2,1)S(1)}, u32[]{:S(2)}, u32[]{:S(2)}) %collective-permute-start.2) | collective-permute-done | bytes 131104 | tf_op jit(solution)/shard_map/weights/ppermute | solution.py:40
  16.8 1.6 collective-permute-start.7
  18.4 1.7 collective-permute-start.8
  20.1 2.0 %collective-permute-start.9 = (bf16[144,1024]{1,0:T(8,128)(2,1)S(1)}, bf16[144,1024]{1,0:T(8,128)(2,1)S(1)}, u32[]{:S(2)}, u32[]{:S(2)}) collective-permute-start(bf16[144,1024]{1,0:T(8,128)(2,1)S(1)} %get-tuple-element.38.refs_0_.refs_4_), channel_id=1, source_target_pairs={{0,2},{1,3},{2,0},{3,1},{4,6},{5,7},{6,4},{7,5},{8,10},{9,11},{10,... | collective-permute-start | bytes 884744 | tf_op jit(solution)/shard_map/weights/ppermute | solution.py:40
  22.1 2.6 %collective-permute-start.5 = (bf16[128,1024]{1,0:T(8,128)(2,1)S(1)}, bf16[128,1024]{1,0:T(8,128)(2,1)S(1)}, u32[]{:S(2)}, u32[]{:S(2)}) collective-permute-start(bf16[128,1024]{1,0:T(8,128)(2,1)S(1)} %get-tuple-element.43.refs_0_), channel_id=1, source_target_pairs={{0,68},{64,0},{4,64},{68,4},{1,69},{65,1},{5,65},{69,5},{2,70},{66... | collective-permute-start | bytes 786440 | tf_op jit(solution)/shard_map/weights/ppermute | solution.py:40
  24.7 9.2 %collective-permute-done.5.refs_2_ = bf16[128,1024]{1,0:T(8,128)(2,1)S(1)} collective-permute-done((bf16[128,1024]{1,0:T(8,128)(2,1)S(1)}, bf16[128,1024]{1,0:T(8,128)(2,1)S(1)}, u32[]{:S(2)}, u32[]{:S(2)}) %collective-permute-start.5) | collective-permute-done | bytes 262176 | tf_op jit(solution)/shard_map/weights/ppermute | solution.py:40
  34.9 2.6 %collective-permute-start.12 = (bf16[512,1024]{1,0:T(8,128)(2,1)S(1)}, bf16[512,1024]{1,0:T(8,128)(2,1)}, u32[]{:S(2)}, u32[]{:S(2)}) collective-permute-start(bf16[512,1024]{1,0:T(8,128)(2,1)S(1)} %get-tuple-element.53.refs_0_), channel_id=1, source_target_pairs={{0,3},{1,0},{2,1},{3,2},{4,7},{5,4},{6,5},{7,6},{8,11},{9,8},{10,9... | collective-permute-start | bytes 3145736 | tf_op jit(solution)/shard_map/weights/ppermute | solution.py:40
  37.4 1.6 collective-permute-start.13
  39.0 2.1 %collective-permute-start.14 = (bf16[512,1024]{1,0:T(8,128)(2,1)S(1)}, bf16[512,1024]{1,0:T(8,128)(2,1)}, u32[]{:S(2)}, u32[]{:S(2)}) collective-permute-start(bf16[512,1024]{1,0:T(8,128)(2,1)S(1)} %get-tuple-element.56.refs_3_), channel_id=1, source_target_pairs={{0,68},{64,0},{4,64},{68,4},{1,69},{65,1},{5,65},{69,5},{2,70},{66... | collective-permute-start | bytes 3145736 | tf_op jit(solution)/shard_map/weights/ppermute | solution.py:40
  41.1 0.9 copy.18
  42.0 1.1 reshape.70
  43.4 1.2 collective-permute-done.10.other_ids
  44.6 16.6 %prepare.1 = (bf16[6144,1024]{1,0:T(8,128)(2,1)}, s32[6144,128]{1,0:T(8,128)}, s32[64]{0:T(128)S(1)}, f32[768,1024]{1,0:T(8,128)}) custom-call(s32[2]{0:T(128)S(1)} %pad_add_fusion.place, s32[256,128]{1,0:T(8,128)S(1)} %weights.4.own_ids, s32[256,128]{1,0:T(8,128)S(1)} %collective-permute-done.10.other_ids, bf16[3840,1024]{1,0:T(8,128)(2,1)} %table_all.1, ...), custom_call_target="tpu_custom_call" | custom-call | flops 1073741824 | bytes 1048576 | tf_op jit(solution)/shard_map/prepare/pallas_call | solution.py:287
  61.3 1.4 collective-permute-start.15
  62.8 1.0 collective-permute-start.16
  63.7 16.6 %forward.2.sums_all = f32[6144,1024]{1,0:T(8,128)} custom-call(s32[64]{0:T(128)S(1)} %get-tuple-element.42.bounds, bf16[6144,1024]{1,0:T(8,128)(2,1)} %get-tuple-element.50.x_all, bf16[512,1024]{1,0:T(8,128)(2,1)S(1)} %get-tuple-element.53.refs_0_, bf16[512,1024]{1,0:T(8,128)(2,1)} %collective-permute-done.11.refs_1_, ...), custom_call_target="tpu_custom_call" | custom-call | flops 21474836480 | bytes 16777216 | tf_op jit(solution)/shard_map/forward/pallas_call | solution.py:451
  80.3 7.8 %collective-permute-done.15.refs_0_ = bf16[512,1024]{1,0:T(8,128)(2,1)S(1)} collective-permute-done((bf16[512,1024]{1,0:T(8,128)(2,1)S(1)}, bf16[512,1024]{1,0:T(8,128)(2,1)S(1)}, u32[]{:S(2)}, u32[]{:S(2)}) %collective-permute-start.15) | collective-permute-done | bytes 1048608 | tf_op jit(solution)/shard_map/forward/ppermute | solution.py:40
  88.1 1.1 collective-permute-done.16.refs_1_
  89.2 12.0 %forward.3 = (f32[768,1024]{1,0:T(8,128)S(1)}, f32[768,1024]{1,0:T(8,128)S(1)}) custom-call(s32[64]{0:T(128)S(1)} %get-tuple-element.42.bounds, bf16[6144,1024]{1,0:T(8,128)(2,1)} %get-tuple-element.50.x_all, s32[6144,128]{1,0:T(8,128)S(1)} %copy-done, f32[768,1024]{1,0:T(8,128)S(1)} %copy-done.1, f32[6144,1024]{1,0:T(8,128)} %forward.2.sums_all, ...), custom_call_target="tpu_custom_call" | custom-call | flops 12884901888 | bytes 25165824 | tf_op jit(solution)/shard_map/forward/pallas_call | solution.py:477
  101.3 5.6 %collective-permute-done.17 = f32[768,1024]{1,0:T(8,128)S(1)} collective-permute-done((f32[768,1024]{1,0:T(8,128)S(1)}, f32[768,1024]{1,0:T(8,128)S(1)}, u32[]{:S(2)}, u32[]{:S(2)}) %collective-permute-start.17) | collective-permute-done | bytes 3145760 | tf_op jit(solution)/shard_map/pooled/ppermute | solution.py:40
  107.0 1.7 add_convert_fusion
  108.7 7.6 %all-to-all-start = ((bf16[8,96,1024]{2,1,0:T(8,128)(2,1)}), bf16[8,96,1024]{2,1,0:T(8,128)(2,1)S(1)}, u32[]{:S(2)}, u32[]{:S(2)}) async-start(bf16[8,96,1024]{2,1,0:T(8,128)(2,1)} %bitcast.4), calls=%async_computation | async-start | bytes 3145728 | tf_op jit(solution)/shard_map/pooled/all_to_all | solution.py:546
  116.5 20.8 %all-to-all-done = bf16[8,96,1024]{2,1,0:T(8,128)(2,1)S(1)} async-done(((bf16[8,96,1024]{2,1,0:T(8,128)(2,1)}), bf16[8,96,1024]{2,1,0:T(8,128)(2,1)S(1)}, u32[]{:S(2)}, u32[]{:S(2)}) %all-to-all-start) | async-done | bytes 1572896 | tf_op jit(solution)/shard_map/pooled/all_to_all | solution.py:546
  138.8 19.7 %all_to_all.19 = bf16[64,4,1024]{2,1,0:T(4,128)(2,1)S(1)} all-to-all(bf16[64,4,1024]{2,1,0:T(4,128)(2,1)S(1)} %select_convert_fusion), channel_id=1, replica_groups=mesh['x_lo'=2,'z'=4,'core'=2,'x_hi'=2,'y'=4] {'x_lo','z','x_hi','y'}, dimensions={0} | all-to-all | bytes 1048576 | tf_op jit(solution)/shard_map/match/all_to_all | solution.py:566
  158.8 1.6 collective-permute-done.18
  162.1 14.6 %all_to_all.20 = f32[64,1,4]{2,1,0:T(1,128)S(1)} all-to-all(f32[64,1,4]{2,1,0:T(1,128)S(1)} %bitcast.13), channel_id=1, replica_groups=mesh['x_lo'=2,'z'=4,'core'=2,'x_hi'=2,'y'=4] {'x_lo','z','x_hi','y'}, dimensions={0} | all-to-all | bytes 2048 | tf_op jit(solution)/shard_map/match/all_to_all | solution.py:577
  (62 shorter events, 8.0 us)
Async XLA Ops:
  0.0 41.1 %copy-start.2 = (s32[768,16]{0,1:T(8,128)S(1)}, s32[768,16]{0,1:T(8,128)}, u32[]{:S(2)}) copy-start(s32[768,16]{0,1:T(8,128)} %param.7) | copy-start | bytes 147460
  0.0 43.3 %copy-start.3 = (bf16[16,1024]{1,0:T(8,128)(2,1)S(1)}, bf16[16,1024]{1,0:T(8,128)(2,1)}, u32[]{:S(2)}) copy-start(bf16[16,1024]{1,0:T(8,128)(2,1)} %param.11) | copy-start | bytes 98308
  1.7 9.1 %collective-permute-start.3 = (bf16[16,128]{1,0:T(8,128)(2,1)S(1)}, bf16[16,128]{1,0:T(8,128)(2,1)S(1)}, u32[]{:S(2)}, u32[]{:S(2)}) collective-permute-start(bf16[16,128]{1,0:T(8,128)(2,1)S(1)} %pad.17), channel_id=1, source_target_pairs={{0,4},{4,0},{1,5},{5,1},{2,6},{6,2},{3,7},{7,3},{8,12},{12,8},{9,1... | collective-permute-start | bytes 12296 | tf_op jit(solution)/shard_map/weights/ppermute | solution.py:514
  4.9 7.3 %collective-permute-start = (bf16[64,1024]{1,0:T(8,128)(2,1)S(1)}, bf16[64,1024]{1,0:T(8,128)(2,1)S(1)}, u32[]{:S(2)}, u32[]{:S(2)}) collective-permute-start(bf16[64,1024]{1,0:T(8,128)(2,1)S(1)} %pad_maximum_fusion.refs_0_.refs_4_), channel_id=1, source_target_pairs={{0,16},{16,32},{32,48},{48,0},{1,17},{17,33},{33,49},{49,1},{2,18}... | collective-permute-start | bytes 393224 | tf_op jit(solution)/shard_map/weights/ppermute | solution.py:40
  6.8 7.5 %collective-permute-start.1 = (bf16[64,1024]{1,0:T(8,128)(2,1)S(1)}, bf16[64,1024]{1,0:T(8,128)(2,1)S(1)}, u32[]{:S(2)}, u32[]{:S(2)}) collective-permute-start(bf16[64,1024]{1,0:T(8,128)(2,1)S(1)} %pad_maximum_fusion.refs_0_.refs_4_), channel_id=1, source_target_pairs={{0,48},{16,0},{32,16},{48,32},{1,49},{17,1},{33,17},{49,33},{2,50}... | collective-permute-start | bytes 393224 | tf_op jit(solution)/shard_map/weights/ppermute | solution.py:40
  8.9 7.2 %collective-permute-start.2 = (bf16[64,1024]{1,0:T(8,128)(2,1)S(1)}, bf16[64,1024]{1,0:T(8,128)(2,1)S(1)}, u32[]{:S(2)}, u32[]{:S(2)}) collective-permute-start(bf16[64,1024]{1,0:T(8,128)(2,1)S(1)} %pad_maximum_fusion.refs_0_.refs_4_), channel_id=1, source_target_pairs={{0,32},{16,48},{32,0},{48,16},{1,33},{17,49},{33,1},{49,17},{2,34}... | collective-permute-start | bytes 393224 | tf_op jit(solution)/shard_map/weights/ppermute | solution.py:40
  16.2 8.5 %collective-permute-start.4 = (bf16[128,1024]{1,0:T(8,128)(2,1)S(1)}, bf16[128,1024]{1,0:T(8,128)(2,1)S(1)}, u32[]{:S(2)}, u32[]{:S(2)}) collective-permute-start(bf16[128,1024]{1,0:T(8,128)(2,1)S(1)} %get-tuple-element.43.refs_0_), channel_id=1, source_target_pairs={{0,64},{64,4},{4,68},{68,0},{1,65},{65,5},{5,69},{69,1},{2,66},{66... | collective-permute-start | bytes 786440 | tf_op jit(solution)/shard_map/weights/ppermute | solution.py:40
  16.8 17.1 %collective-permute-start.7 = (bf16[144,1024]{1,0:T(8,128)(2,1)S(1)}, bf16[144,1024]{1,0:T(8,128)(2,1)S(1)}, u32[]{:S(2)}, u32[]{:S(2)}) collective-permute-start(bf16[144,1024]{1,0:T(8,128)(2,1)S(1)} %get-tuple-element.38.refs_0_.refs_4_), channel_id=1, source_target_pairs={{0,1},{1,2},{2,3},{3,0},{4,5},{5,6},{6,7},{7,4},{8,9},{9,10},{10,1... | collective-permute-start | bytes 884744 | tf_op jit(solution)/shard_map/weights/ppermute | solution.py:40
  18.4 15.6 %collective-permute-start.8 = (bf16[144,1024]{1,0:T(8,128)(2,1)S(1)}, bf16[144,1024]{1,0:T(8,128)(2,1)S(1)}, u32[]{:S(2)}, u32[]{:S(2)}) collective-permute-start(bf16[144,1024]{1,0:T(8,128)(2,1)S(1)} %get-tuple-element.38.refs_0_.refs_4_), channel_id=1, source_target_pairs={{0,3},{1,0},{2,1},{3,2},{4,7},{5,4},{6,5},{7,6},{8,11},{9,8},{10,9... | collective-permute-start | bytes 884744 | tf_op jit(solution)/shard_map/weights/ppermute | solution.py:40
  20.1 13.9 %collective-permute-start.9 = (bf16[144,1024]{1,0:T(8,128)(2,1)S(1)}, bf16[144,1024]{1,0:T(8,128)(2,1)S(1)}, u32[]{:S(2)}, u32[]{:S(2)}) collective-permute-start(bf16[144,1024]{1,0:T(8,128)(2,1)S(1)} %get-tuple-element.38.refs_0_.refs_4_), channel_id=1, source_target_pairs={{0,2},{1,3},{2,0},{3,1},{4,6},{5,7},{6,4},{7,5},{8,10},{9,11},{10,... | collective-permute-start | bytes 884744 | tf_op jit(solution)/shard_map/weights/ppermute | solution.py:40
  22.1 11.9 %collective-permute-start.5 = (bf16[128,1024]{1,0:T(8,128)(2,1)S(1)}, bf16[128,1024]{1,0:T(8,128)(2,1)S(1)}, u32[]{:S(2)}, u32[]{:S(2)}) collective-permute-start(bf16[128,1024]{1,0:T(8,128)(2,1)S(1)} %get-tuple-element.43.refs_0_), channel_id=1, source_target_pairs={{0,68},{64,0},{4,64},{68,4},{1,69},{65,1},{5,65},{69,5},{2,70},{66... | collective-permute-start | bytes 786440 | tf_op jit(solution)/shard_map/weights/ppermute | solution.py:40
  24.7 9.3 %collective-permute-start.6 = (bf16[128,1024]{1,0:T(8,128)(2,1)S(1)}, bf16[128,1024]{1,0:T(8,128)(2,1)S(1)}, u32[]{:S(2)}, u32[]{:S(2)}) collective-permute-start(bf16[128,1024]{1,0:T(8,128)(2,1)S(1)} %get-tuple-element.43.refs_0_), channel_id=1, source_target_pairs={{0,4},{64,68},{4,0},{68,64},{1,5},{65,69},{5,1},{69,65},{2,6},{66,... | collective-permute-start | bytes 786440 | tf_op jit(solution)/shard_map/weights/ppermute | solution.py:40
  34.1 27.2 %collective-permute-start.11 = (bf16[512,1024]{1,0:T(8,128)(2,1)S(1)}, bf16[512,1024]{1,0:T(8,128)(2,1)}, u32[]{:S(2)}, u32[]{:S(2)}) collective-permute-start(bf16[512,1024]{1,0:T(8,128)(2,1)S(1)} %get-tuple-element.53.refs_0_), channel_id=1, source_target_pairs={{0,1},{1,2},{2,3},{3,0},{4,5},{5,6},{6,7},{7,4},{8,9},{9,10},{10,1... | collective-permute-start | bytes 3145736 | tf_op jit(solution)/shard_map/weights/ppermute | solution.py:40
  34.9 26.4 %collective-permute-start.12 = (bf16[512,1024]{1,0:T(8,128)(2,1)S(1)}, bf16[512,1024]{1,0:T(8,128)(2,1)}, u32[]{:S(2)}, u32[]{:S(2)}) collective-permute-start(bf16[512,1024]{1,0:T(8,128)(2,1)S(1)} %get-tuple-element.53.refs_0_), channel_id=1, source_target_pairs={{0,3},{1,0},{2,1},{3,2},{4,7},{5,4},{6,5},{7,6},{8,11},{9,8},{10,9... | collective-permute-start | bytes 3145736 | tf_op jit(solution)/shard_map/weights/ppermute | solution.py:40
  37.4 23.9 %collective-permute-start.13 = (bf16[512,1024]{1,0:T(8,128)(2,1)S(1)}, bf16[512,1024]{1,0:T(8,128)(2,1)}, u32[]{:S(2)}, u32[]{:S(2)}) collective-permute-start(bf16[512,1024]{1,0:T(8,128)(2,1)S(1)} %get-tuple-element.56.refs_3_), channel_id=1, source_target_pairs={{0,64},{64,4},{4,68},{68,0},{1,65},{65,5},{5,69},{69,1},{2,66},{66... | collective-permute-start | bytes 3145736 | tf_op jit(solution)/shard_map/weights/ppermute | solution.py:40
  39.0 22.3 %collective-permute-start.14 = (bf16[512,1024]{1,0:T(8,128)(2,1)S(1)}, bf16[512,1024]{1,0:T(8,128)(2,1)}, u32[]{:S(2)}, u32[]{:S(2)}) collective-permute-start(bf16[512,1024]{1,0:T(8,128)(2,1)S(1)} %get-tuple-element.56.refs_3_), channel_id=1, source_target_pairs={{0,68},{64,0},{4,64},{68,4},{1,69},{65,1},{5,65},{69,5},{2,70},{66... | collective-permute-start | bytes 3145736 | tf_op jit(solution)/shard_map/weights/ppermute | solution.py:40
  43.2 1.4 collective-permute-start.10
  61.3 26.8 %collective-permute-start.15 = (bf16[512,1024]{1,0:T(8,128)(2,1)S(1)}, bf16[512,1024]{1,0:T(8,128)(2,1)S(1)}, u32[]{:S(2)}, u32[]{:S(2)}) collective-permute-start(bf16[512,1024]{1,0:T(8,128)(2,1)S(1)} %get-tuple-element.53.refs_0_), channel_id=1, source_target_pairs={{0,2},{1,3},{2,0},{3,1},{4,6},{5,7},{6,4},{7,5},{8,10},{9,11},{10,... | collective-permute-start | bytes 3145736 | tf_op jit(solution)/shard_map/forward/ppermute | solution.py:40
  62.8 26.4 %collective-permute-start.16 = (bf16[512,1024]{1,0:T(8,128)(2,1)S(1)}, bf16[512,1024]{1,0:T(8,128)(2,1)S(1)}, u32[]{:S(2)}, u32[]{:S(2)}) collective-permute-start(bf16[512,1024]{1,0:T(8,128)(2,1)S(1)} %get-tuple-element.56.refs_3_), channel_id=1, source_target_pairs={{0,4},{64,68},{4,0},{68,64},{1,5},{65,69},{5,1},{69,65},{2,6},{66,... | collective-permute-start | bytes 3145736 | tf_op jit(solution)/shard_map/forward/ppermute | solution.py:40
  63.7 25.4 %copy-start = (s32[6144,128]{1,0:T(8,128)S(1)}, s32[6144,128]{1,0:T(8,128)}, u32[]{:S(2)}) copy-start(s32[6144,128]{1,0:T(8,128)} %get-tuple-element.51.docs_all) | copy-start | bytes 9437188
  63.7 25.4 %copy-start.1 = (f32[768,1024]{1,0:T(8,128)S(1)}, f32[768,1024]{1,0:T(8,128)}, u32[]{:S(2)}) copy-start(f32[768,1024]{1,0:T(8,128)} %get-tuple-element.52.normed) | copy-start | bytes 9437188
  101.2 5.7 %collective-permute-start.17 = (f32[768,1024]{1,0:T(8,128)S(1)}, f32[768,1024]{1,0:T(8,128)S(1)}, u32[]{:S(2)}, u32[]{:S(2)}) collective-permute-start(f32[768,1024]{1,0:T(8,128)S(1)} %get-tuple-element.60), channel_id=1, source_target_pairs={{0,8},{8,0},{1,9},{9,1},{2,10},{10,2},{3,11},{11,3},{4,12},{12,4},... | collective-permute-start | bytes 9437192 | tf_op jit(solution)/shard_map/pooled/ppermute | solution.py:40
  108.7 7.6 %copy-start.4 = (s32[96,1]{0,1:T(1,128)S(1)}, s32[96,1]{0,1:T(1,128)}, u32[]{:S(2)}) copy-start(s32[96,1]{0,1:T(1,128)} %param.9) | copy-start | bytes 1156
  108.7 28.7 %all-to-all-start = ((bf16[8,96,1024]{2,1,0:T(8,128)(2,1)}), bf16[8,96,1024]{2,1,0:T(8,128)(2,1)S(1)}, u32[]{:S(2)}, u32[]{:S(2)}) async-start(bf16[8,96,1024]{2,1,0:T(8,128)(2,1)} %bitcast.4), calls=%async_computation | async-start | bytes 3145728 | tf_op jit(solution)/shard_map/pooled/all_to_all | solution.py:546
  158.5 1.9 %collective-permute-start.18 = (bf16[64,4,1024]{2,1,0:T(4,128)(2,1)S(1)}, bf16[64,4,1024]{2,1,0:T(4,128)(2,1)S(1)}, u32[]{:S(2)}, u32[]{:S(2)}) collective-permute-start(bf16[64,4,1024]{2,1,0:T(4,128)(2,1)S(1)} %all_to_all.19), channel_id=1, source_target_pairs={{0,8},{8,0},{1,9},{9,1},{2,10},{10,2},{3,11},{11,3},{4,12},{12,4},... | collective-permute-start | bytes 1572872 | tf_op jit(solution)/shard_map/match/ppermute | solution.py:40
